TPU v7x, 32 devices: a whole 2x2x4 slice. The times are simulated.
32 devices in a mesh: groups: 2 (over y), seq: 4 (over z), dp: 2 (over x), tensor: 2 (over core).
Axes of the slice: x: 2, y: 2, z: 4, core: 2. Of those that a mesh axis runs over, the one named last changes fastest.
Arguments:
- tokens: bfloat16 [4, 512, 2048], P(('groups', 'dp'), 'seq', 'tensor'), parts along dimension 0, may hold values from -6 to 6
- grad_out: bfloat16 [4, 512, 2048], P(('groups', 'dp'), 'seq', 'tensor'), parts along dimension 0, may hold values from -6 to 6
- picks: int32 [4, 64], P(('groups', 'dp')), parts along dimension 0, may hold values from 0 to 511, as said below
- scores: float32 [4, 64], P(('groups', 'dp')), parts along dimension 0, may hold values from 0.1 to 1
- w_gate: bfloat16 [2048, 1792], P('dp', ('seq', 'tensor')), may hold values from -0.125 to 0.125
- w_up: bfloat16 [2048, 1792], P('dp', ('seq', 'tensor')), may hold values from -0.125 to 0.125
- w_down: bfloat16 [1792, 2048], P(('seq', 'tensor'), 'dp'), may hold values from -0.125 to 0.125
Outputs:
- grad_tokens: bfloat16 [4, 512, 2048], P(('groups', 'dp'), 'seq', 'tensor'), parts along dimension 0
- grad_gate: bfloat16 [4096, 1792], P(('groups', 'dp'), ('seq', 'tensor')), parts along dimension 0
- grad_up: bfloat16 [4096, 1792], P(('groups', 'dp'), ('seq', 'tensor')), parts along dimension 0
- grad_down: bfloat16 [3584, 2048], P(('groups', 'seq', 'tensor'), 'dp'), parts along dimension 0
There are 2 independent parts, one for each index of `groups`. A program takes and returns all parts, laid end to end along the dimension named above; an argument that names none is the same for every part. Nothing has to cross between parts.
Inputs may be any that keep to these rules, and one draw needn't show every extreme that they name: Each row lists 64 different positions, in an order drawn from the seed. Among the positions k * 128 to (k + 1) * 128 - 1 of one shard lie at most 32 picks of a row, and in every row one shard holds exactly 32.
All inputs are finite; a program needn't handle non-finite values.
Results may differ from a plain program's by a relative error of at most 0.0066.
Values may be sent and summed in bfloat16 or wider, within the bound.
No kernel may reach another device: no remote copies, remote signals or barrier semaphores. Data moves between devices by JAX's collectives and lax.ppermute only.
A program may use at most 64 MiB of HBM per device.

v0:
```python
import jax
import jax.numpy as jnp
from jax import lax
from jax.sharding import PartitionSpec as P

MOST = 32


def local(tokens, grad_out, picks, scores, w_gate, w_up, w_down):
    tok_dev = tokens.shape[1]
    half = tokens.shape[2]
    seq_count = lax.axis_size("seq")
    ten_count = lax.axis_size("tensor")
    picks_row = picks[0]
    score_row = scores[0]
    cap = picks_row.shape[0]
    each = cap // (seq_count * ten_count)
    my_seq = lax.axis_index("seq")
    my_ten = lax.axis_index("tensor")
    my_replica = lax.axis_index("dp")
    share = w_gate.shape[0]
    full_gate, full_up, full_down = (
        lax.all_gather(w_gate, "dp", axis=0, tiled=True),
        lax.all_gather(w_up, "dp", axis=0, tiled=True),
        lax.all_gather(w_down, "dp", axis=1, tiled=True),
    )
    owner = picks_row // tok_dev
    mine = owner == my_seq
    place = jnp.clip(picks_row - my_seq * tok_dev, 0, tok_dev - 1)
    local_rows = tokens[0]
    local_grads = grad_out[0]
    zero_value = jnp.zeros((), jnp.bfloat16)
    shard_ids = jnp.arange(seq_count, dtype=jnp.int32)
    owner_table = (owner[:, None] == shard_ids[None, :]).astype(jnp.int32)
    earlier = jnp.cumsum(owner_table, axis=0) - owner_table
    slot_of = jnp.sum(earlier * owner_table, axis=1)
    slot_ids = jnp.arange(MOST, dtype=jnp.int32)
    match = (mine[None, :] & (slot_of[None, :] == slot_ids[:, None])).astype(jnp.int32)
    pick_ids = jnp.sum(match * jnp.arange(cap, dtype=jnp.int32)[None, :], axis=1)
    valid = jnp.sum(match, axis=1) > 0
    rows_at = jnp.clip(jnp.take(picks_row, pick_ids) - my_seq * tok_dev, 0, tok_dev - 1)
    pack_rows = jnp.where(valid[:, None], jnp.take(local_rows, rows_at, axis=0), zero_value)
    pack_grads = jnp.where(valid[:, None], jnp.take(local_grads, rows_at, axis=0), zero_value)
    all_rows, all_grads = (
        lax.all_gather(pack_rows, ("seq", "tensor"), axis=0, tiled=True),
        lax.all_gather(pack_grads, ("seq", "tensor"), axis=0, tiled=True),
    )

    def unpack(block):
        parts = [
            jnp.take(block, (owner * ten_count + part) * MOST + slot_of, axis=0)
            for part in range(ten_count)
        ]
        return jnp.concatenate(parts, axis=1)

    x_rows = unpack(all_rows)
    dy_rows = unpack(all_grads)
    dz = (score_row[:, None] * dy_rows.astype(jnp.float32)).astype(jnp.bfloat16)
    gate = jnp.dot(x_rows, full_gate, preferred_element_type=jnp.float32)
    upper = jnp.dot(x_rows, full_up, preferred_element_type=jnp.float32)
    sigma = jax.nn.sigmoid(gate)
    act = (gate * sigma * upper).astype(jnp.bfloat16)
    last_dims = (((1,), (1,)), ((), ()))
    first_dims = (((0,), (0,)), ((), ()))
    d_act = lax.dot_general(dz, full_down, last_dims, preferred_element_type=jnp.float32)
    d_gate = (d_act * upper * sigma * (1.0 + gate * (1.0 - sigma))).astype(jnp.bfloat16)
    d_up = (d_act * gate * sigma).astype(jnp.bfloat16)
    result = lax.dot_general(d_gate, full_gate, last_dims, preferred_element_type=jnp.float32)
    summed = lax.psum_scatter(
        result + lax.dot_general(d_up, full_up, last_dims, preferred_element_type=jnp.float32),
        ("seq", "tensor"),
        scatter_dimension=0,
        tiled=True,
    )
    coeff = float(lax.axis_size("dp") * cap) ** (-0.5)
    term_gate = (
        coeff * lax.dot_general(x_rows, d_gate, first_dims, preferred_element_type=jnp.float32)
    ).astype(jnp.bfloat16)
    term_up = (
        coeff * lax.dot_general(x_rows, d_up, first_dims, preferred_element_type=jnp.float32)
    ).astype(jnp.bfloat16)
    term_down = (
        coeff * lax.dot_general(act, dz, first_dims, preferred_element_type=jnp.float32)
    ).astype(jnp.bfloat16)
    sum_gate, sum_up, sum_down = (
        lax.psum(term_gate, "dp").astype(jnp.float32),
        lax.psum(term_up, "dp").astype(jnp.float32),
        lax.psum(term_down, "dp").astype(jnp.float32),
    )
    own_gate = lax.dynamic_slice_in_dim(sum_gate, my_replica * share, share, 0)
    own_up = lax.dynamic_slice_in_dim(sum_up, my_replica * share, share, 0)
    own_down = lax.dynamic_slice_in_dim(sum_down, my_replica * share, share, 1)
    my_block = my_seq * ten_count + my_ten
    block_owner = lax.dynamic_slice_in_dim(owner, my_block * each, each, 0)
    block_rows = summed.astype(jnp.bfloat16).reshape(each, ten_count, half).transpose(1, 0, 2)
    targets = block_owner[None, :] == jnp.arange(seq_count, dtype=jnp.int32)[:, None]
    outgoing = jnp.where(targets[:, None, :, None], block_rows[None], zero_value)
    incoming = lax.all_to_all(
        outgoing.reshape(seq_count * ten_count * each, half),
        ("seq", "tensor"),
        split_axis=0,
        concat_axis=0,
        tiled=True,
    )
    positions = jnp.arange(tok_dev, dtype=jnp.int32)
    selector = ((place[None, :] == positions[:, None]) & mine[None, :]).astype(jnp.bfloat16)
    grad_local = jnp.dot(selector, incoming, preferred_element_type=jnp.float32).astype(
        jnp.bfloat16
    )
    return (
        grad_local.reshape(1, tok_dev, half),
        own_gate.astype(jnp.bfloat16),
        own_up.astype(jnp.bfloat16),
        own_down.astype(jnp.bfloat16),
    )


def solution(mesh):
    in_specs = (
        P(("groups", "dp"), "seq", "tensor"),
        P(("groups", "dp"), "seq", "tensor"),
        P(("groups", "dp"), None),
        P(("groups", "dp"), None),
        P("dp", ("seq", "tensor")),
        P("dp", ("seq", "tensor")),
        P(("seq", "tensor"), "dp"),
    )
    out_specs = (
        P(("groups", "dp"), "seq", "tensor"),
        P(("groups", "dp"), ("seq", "tensor")),
        P(("groups", "dp"), ("seq", "tensor")),
        P(("groups", "seq", "tensor"), "dp"),
    )
    return jax.shard_map(local, mesh=mesh, in_specs=in_specs, out_specs=out_specs, check_vma=False)
```

profile of v0, /device:TPU:0, one launch (start us, length us, event | category | flops | bytes accessed | tf_op | source)
XLA Modules:
  0.0 183.3 jit_solution(16044150363135591139)
XLA Ops:
  8.1 0.7 and_select_fusion.1
  8.8 0.7 compare_bitcast_fusion
  9.8 0.7 compare_and_fusion.1
  10.6 1.4 gather_fusion
  12.0 0.6 gather_fusion.4
  12.7 0.6 gather_fusion.1
  13.4 16.6 %all_gather.15 = bf16[256,1024]{1,0:T(8,128)(2,1)S(1)} all-gather(bf16[32,1024]{1,0:T(8,128)(2,1)S(1)} %get-tuple-element.19), channel_id=1, replica_groups=mesh['groups'=2,'seq'=4,'dp'=2,'tensor'=2] {'seq','tensor'}, dimensions={0}, use_global_device_ids=true | all-gather | bytes 589824 | tf_op jit(solution)/shard_map/all_gather | solution.py:46
  30.0 0.7 gather_fusion.3
  30.7 0.7 gather_fusion.2
  31.4 14.7 %all_gather.17 = bf16[256,1024]{1,0:T(8,128)(2,1)S(1)} all-gather(bf16[32,1024]{1,0:T(8,128)(2,1)S(1)} %get-tuple-element.20), channel_id=1, replica_groups=mesh['groups'=2,'seq'=4,'dp'=2,'tensor'=2] {'seq','tensor'}, dimensions={0}, use_global_device_ids=true | all-gather | bytes 589824 | tf_op jit(solution)/shard_map/all_gather | solution.py:45
  46.1 0.7 gather_fusion.6
  46.8 0.7 gather_fusion.5
  47.6 13.6 %all_gather.19 = bf16[2048,224]{0,1:T(8,128)(2,1)S(1)} all-gather(bf16[1024,224]{0,1:T(8,128)(2,1)S(1)} %copy-done.3), channel_id=1, replica_groups=mesh['groups'=2,'seq'=4,'dp'=2,'tensor'=2] {'dp'}, dimensions={0}, use_global_device_ids=true | all-gather | bytes 1376256 | tf_op jit(solution)/shard_map/all_gather | solution.py:23
  61.2 12.6 %all_gather.18 = bf16[2048,224]{0,1:T(8,128)(2,1)S(1)} all-gather(bf16[1024,224]{0,1:T(8,128)(2,1)S(1)} %copy-done.4), channel_id=1, replica_groups=mesh['groups'=2,'seq'=4,'dp'=2,'tensor'=2] {'dp'}, dimensions={0}, use_global_device_ids=true | all-gather | bytes 1376256 | tf_op jit(solution)/shard_map/all_gather | solution.py:24
  74.0 0.4 fusion.17
  74.8 0.6 copy-done.5
  75.4 11.9 %all_gather.16 = bf16[224,2048]{1,0:T(8,128)(2,1)S(1)} all-gather(bf16[224,1024]{1,0:T(8,128)(2,1)S(1)} %copy-done.5), channel_id=1, replica_groups=mesh['groups'=2,'seq'=4,'dp'=2,'tensor'=2] {'dp'}, dimensions={1}, use_global_device_ids=true | all-gather | bytes 1376256 | tf_op jit(solution)/shard_map/all_gather | solution.py:25
  87.3 0.4 multiply_convert_fusion.2
  88.0 1.1 convolution_add_fusion
  89.2 1.4 fusion.1
  90.5 1.4 fusion
  91.9 1.4 fusion.2
  93.5 28.1 %reduce-scatter.2.cloned.1.call-done = f32[8,2048]{1,0:T(8,128)} async-done(((f32[64,2048]{1,0:T(8,128)}), f32[8,2048]{1,0:T(8,128)}) %reduce-scatter.2.cloned.1.call-update) | async-done | bytes 65552 | tf_op jit(solution)/shard_map/reduce_scatter | solution.py:69
  121.6 0.8 convert_element_type.61
  122.4 0.7 bitcast_select_fusion
  123.2 3.4 %all-to-all-start = ((bf16[8,8,1024]{2,1,0:T(8,128)(2,1)}), bf16[8,8,1024]{2,1,0:T(8,128)(2,1)S(1)}, u32[]{:S(2)}, u32[]{:S(2)}) async-start(bf16[8,8,1024]{2,1,0:T(8,128)(2,1)} %bitcast_select_fusion), calls=%async_computation.1 | async-start | bytes 262144 | tf_op jit(solution)/shard_map/all_to_all | solution.py:98
  126.6 6.7 %all-to-all-done = bf16[8,8,1024]{2,1,0:T(8,128)(2,1)S(1)} async-done(((bf16[8,8,1024]{2,1,0:T(8,128)(2,1)}), bf16[8,8,1024]{2,1,0:T(8,128)(2,1)S(1)}, u32[]{:S(2)}, u32[]{:S(2)}) %all-to-all-start) | async-done | bytes 131104 | tf_op jit(solution)/shard_map/all_to_all | solution.py:98
  133.2 0.9 fusion.3
  134.2 38.1 %all-reduce.3.cloned.1.call-done = (bf16[2048,224]{0,1:T(8,128)(2,1)}, bf16[2048,224]{0,1:T(8,128)(2,1)}, bf16[224,2048]{1,0:T(8,128)(2,1)}) async-done(((bf16[2048,224]{0,1:T(8,128)(2,1)}, bf16[2048,224]{0,1:T(8,128)(2,1)}, bf16[224,2048]{1,0:T(8,128)(2,1)}), (bf16[2048,224]{0,1:T(8,128)(2,1)}, bf16[2048,224]{0,1:T(8,128)(2,1)}, bf16[224,2048]{1,0:T(8,128)(2,1)})) %all-reduce.3.cloned.1.call-update) | async-done | bytes 2752528 | tf_op jit(solution)/shard_map/psum | solution.py:86
  172.3 1.9 %convert_convert_fusion.2 = bf16[1024,224]{0,1:T(8,128)(2,1)} fusion(bf16[2048,224]{0,1:T(8,128)(2,1)} %get-tuple-element.8, s32[]{:T(128)S(6)} %select_n.74), kind=kLoop, calls=%fused_computation.18 | loop fusion | flops 458752 | bytes 917508 | tf_op jit(solution)/shard_map/convert_element_type | solution.py:112
  174.2 0.8 convert_convert_fusion.1
  175.0 0.8 convert_convert_fusion
  (40 shorter events, 1.8 us)
Async XLA Ops:
  8.0 4.0 %copy-start = (bf16[1,128,1024]{2,1,0:T(8,128)(2,1)S(1)}, bf16[1,128,1024]{2,1,0:T(8,128)(2,1)}, u32[]{:S(2)}) copy-start(bf16[1,128,1024]{2,1,0:T(8,128)(2,1)} %param.11) | copy-start | bytes 786436
  8.0 4.7 %copy-start.2 = (bf16[1,128,1024]{2,1,0:T(8,128)(2,1)S(1)}, bf16[1,128,1024]{2,1,0:T(8,128)(2,1)}, u32[]{:S(2)}) copy-start(bf16[1,128,1024]{2,1,0:T(8,128)(2,1)} %param.12) | copy-start | bytes 786436
  8.0 113.5 %reduce-scatter.2.cloned.1.call-start = ((), (), s32[]{:S(2)}) async-start(), calls=%async_computation.2 | async-start | bytes 589824 | tf_op jit(solution)/shard_map/reduce_scatter | solution.py:69
  46.1 1.4 copy-start.3
  47.6 13.6 %copy-start.4 = (bf16[1024,224]{0,1:T(8,128)(2,1)S(1)}, bf16[1024,224]{0,1:T(8,128)(2,1)}, u32[]{:S(2)}) copy-start(bf16[1024,224]{0,1:T(8,128)(2,1)} %param.16) | copy-start | bytes 1376260
  74.4 1.0 copy-start.5
  75.4 11.9 %copy-start.8 = (f32[1,64]{1,0:T(1,128)S(1)}, f32[1,64]{1,0:T(1,128)}, u32[]{:S(2)}) copy-start(f32[1,64]{1,0:T(1,128)} %param.14) | copy-start | bytes 772
  89.1 83.1 %all-reduce.3.cloned.1.call-start = ((), (), s32[]{:S(2)}) async-start(), calls=%async_computation.3 | async-start | bytes 5505024 | tf_op jit(solution)/shard_map/psum | solution.py:86
  93.3 33.2 %copy-start.1 = (s32[1,64]{1,0:T(1,128)S(1)}, s32[1,64]{1,0:T(1,128)}, u32[]{:S(2)}) copy-start(s32[1,64]{1,0:T(1,128)} %param.13) | copy-start | bytes 772
  123.2 10.1 %all-to-all-start = ((bf16[8,8,1024]{2,1,0:T(8,128)(2,1)}), bf16[8,8,1024]{2,1,0:T(8,128)(2,1)S(1)}, u32[]{:S(2)}, u32[]{:S(2)}) async-start(bf16[8,8,1024]{2,1,0:T(8,128)(2,1)} %bitcast_select_fusion), calls=%async_computation.1 | async-start | bytes 262144 | tf_op jit(solution)/shard_map/all_to_all | solution.py:98
  172.2 2.0 %copy-start.7 = (bf16[2048,224]{0,1:T(8,128)(2,1)S(1)}, bf16[2048,224]{0,1:T(8,128)(2,1)}, u32[]{:S(2)}) copy-start(bf16[2048,224]{0,1:T(8,128)(2,1)} %get-tuple-element.9) | copy-start | bytes 2752516
  172.2 2.8 %copy-start.6 = (bf16[224,2048]{1,0:T(8,128)(2,1)S(1)}, bf16[224,2048]{1,0:T(8,128)(2,1)}, u32[]{:S(2)}) copy-start(bf16[224,2048]{1,0:T(8,128)(2,1)} %get-tuple-element.10) | copy-start | bytes 2752516
Sparse Core Ops, SparseCore 0:
  89.2 32.2 reduce-scatter.1
Sparse Core Ops, SparseCore 1:
  93.4 78.8 all-reduce.2
where the time goes:
time: 184 us; the launch traced here: 183 us
  waiting for transfers between devices  72.9 us (40%)
  blocking collectives  69.4 us (38%)
  between operations  15.7 us (9%)
  other arithmetic  7.99 us (4%)
  matrix products  7.69 us (4%)
  local copies, waits for them, and re-layouts  6.2 us (3%)
  starting transfers between devices  3.45 us (2%)
    psum x1, waiting for transfers between devices, local(): lax.psum(term_gate, 'dp').astype(jnp.float32)  38.1 us
    reduce_scatter x1, waiting for transfers between devices, local(): lax.psum_scatter(result + lax.dot_general(d_up, full_up, last_dims, prefe...  28.1 us
    all_gather x1, blocking collectives, local(): lax.all_gather(pack_grads, ('seq', 'tensor'), axis=0, tiled=True)  16.6 us
    all_gather x1, blocking collectives, local(): lax.all_gather(pack_rows, ('seq', 'tensor'), axis=0, tiled=True)  14.7 us
    all_gather x1, blocking collectives, local(): lax.all_gather(w_gate, 'dp', axis=0, tiled=True)  13.6 us
    all_gather x1, blocking collectives, local(): lax.all_gather(w_up, 'dp', axis=0, tiled=True)  12.6 us
    all_gather x1, blocking collectives, local(): lax.all_gather(w_down, 'dp', axis=1, tiled=True)  11.9 us
    all_to_all x1, waiting for transfers between devices, local(): lax.all_to_all(outgoing.reshape(seq_count * ten_count * each, half), ('se...  6.68 us
  transfers between devices with their start and end apart: 3, of which 3 were waited for; matrix products, arithmetic and copies ran while one was open for 4% of the time, Pallas kernels for 0%

commit v1 on v0

--- a/solution.py
+++ b/solution.py
@@ -1,12 +1,180 @@
+import functools
+
 import jax
 import jax.numpy as jnp
 from jax import lax
+from jax.experimental import pallas as pl
+from jax.experimental.pallas import tpu as pltpu
 from jax.sharding import PartitionSpec as P
 
 MOST = 32
-
-
-def local(tokens, grad_out, picks, scores, w_gate, w_up, w_down):
+BF = jnp.bfloat16
+F32 = jnp.float32
+NN = (((1,), (0,)), ((), ()))
+NT = (((1,), (1,)), ((), ()))
+TN = (((0,), (0,)), ((), ()))
+
+
+def dot(a, b, dims):
+    return lax.dot_general(a, b, dims, preferred_element_type=F32)
+
+
+def call(body, outs, *args, flops=0):
+    size = sum(a.size * a.dtype.itemsize for a in args) + sum(o.size * o.dtype.itemsize for o in outs)
+    return pl.pallas_call(
+        body,
+        out_shape=outs,
+        in_specs=[pl.BlockSpec(memory_space=pltpu.VMEM)] * len(args),
+        out_specs=[pl.BlockSpec(memory_space=pltpu.VMEM)] * len(outs),
+        cost_estimate=pl.CostEstimate(flops=flops, bytes_accessed=size, transcendentals=0),
+        compiler_params=pltpu.CompilerParams(vmem_limit_bytes=24 * 1024 * 1024),
+    )(*args)
+
+
+def arr(shape, dtype=BF):
+    return jax.ShapeDtypeStruct(shape, dtype)
+
+
+def pack_body(picks_ref, scores_ref, tok_ref, grad_ref, x_ref, dz_ref, sel_ref):
+    tok_dev = tok_ref.shape[0]
+    cap = picks_ref.shape[1]
+    base = lax.axis_index("seq") * tok_dev
+    where = picks_ref[...] - base
+    hit = (lax.broadcasted_iota(jnp.int32, (tok_dev, cap), 0) == where).astype(F32).astype(BF)
+    picked = dot(jnp.ones((8, cap), BF), hit, NT)
+    before = (
+        lax.broadcasted_iota(jnp.int32, (tok_dev, tok_dev), 0) < lax.broadcasted_iota(jnp.int32, (tok_dev, tok_dev), 1)
+    ).astype(F32).astype(BF)
+    rank = dot(picked.astype(BF), before, NN)[0:1]
+    slots = lax.broadcasted_iota(jnp.int32, (MOST, tok_dev), 0).astype(F32)
+    sel = jnp.where((rank == slots) & (picked[0:1] > 0.5), 1.0, 0.0).astype(BF)
+    sel_ref[...] = sel
+    chosen = dot(sel, hit, NN)
+    score = jnp.sum(chosen * scores_ref[...], axis=1, keepdims=True)
+    x_ref[...] = dot(sel, tok_ref[...], NN).astype(BF)
+    dz_ref[...] = (score * dot(sel, grad_ref[...], NN)).astype(BF)
+
+
+def rows_of(refs):
+    return jnp.concatenate([r[...] for r in refs], axis=0)
+
+
+def gate_up_body(n, *refs):
+    x = rows_of(refs[:n])
+    gate_own, gate_oth, up_own, up_oth, send_ref, keep_ref = refs[n:]
+    h = gate_own.shape[0]
+    for i, w in enumerate((gate_own, gate_oth, up_own, up_oth)):
+        part = dot(w[...], x, NT)
+        keep_ref[i * h : (i + 1) * h] = part
+        send_ref[i * h : (i + 1) * h] = part.astype(BF)
+
+
+def d_act_body(n, *refs):
+    dz = rows_of(refs[:n])
+    down_own, down_oth, send_ref, keep_ref = refs[n:]
+    h = down_own.shape[0]
+    for i, w in enumerate((down_own, down_oth)):
+        part = dot(w[...], dz, NT)
+        keep_ref[i * h : (i + 1) * h] = part
+        send_ref[i * h : (i + 1) * h] = part.astype(BF)
+
+
+def middle_body(n, gu_keep, gu_recv, da_keep, da_recv, gate_own, gate_oth, up_own, up_oth, own_ref, oth_ref, *dx_refs):
+    h = gate_own.shape[0]
+    total = jnp.zeros((gu_keep.shape[1], gate_own.shape[1]), F32)
+    for i, (wg, wu, out) in enumerate(((gate_own, up_own, own_ref), (gate_oth, up_oth, oth_ref))):
+        at = slice(i * h, (i + 1) * h)
+        au = slice((2 + i) * h, (3 + i) * h)
+        gate = gu_keep[at] + gu_recv[at].astype(F32)
+        upper = gu_keep[au] + gu_recv[au].astype(F32)
+        d_act = da_keep[at] + da_recv[at].astype(F32)
+        sigma = jax.nn.sigmoid(gate)
+        gs = gate * sigma
+        d_gate = (d_act * upper * sigma * (1.0 + gate * (1.0 - sigma))).astype(BF)
+        d_up = (d_act * gs).astype(BF)
+        out[0:h] = d_gate
+        out[h : 2 * h] = d_up
+        out[2 * h : 3 * h] = (gs * upper).astype(BF)
+        total += dot(d_gate, wg[...], TN) + dot(d_up, wu[...], TN)
+    for s, ref in enumerate(dx_refs):
+        ref[...] = total[s * MOST : (s + 1) * MOST].astype(BF)
+
+
+def weights_body(n, coeff, h, *refs):
+    x_own, x_oth, dz_own, dz_oth = (rows_of(refs[i * n : (i + 1) * n]) for i in range(4))
+    own, oth, gate_ref, up_ref, down_ref = refs[4 * n :]
+    for i, (a, b, out) in enumerate(((x_own, x_oth, gate_ref), (x_own, x_oth, up_ref), (dz_own, dz_oth, down_ref))):
+        at = slice(i * h, (i + 1) * h)
+        one = (coeff * dot(own[at], a, NN)).astype(BF).astype(F32)
+        two = (coeff * dot(oth[at], b, NN)).astype(BF).astype(F32)
+        out[...] = (one + two).astype(BF)
+
+
+def spread_body(sel_ref, *refs):
+    total = refs[0][...].astype(F32)
+    for r in refs[1:-1]:
+        total += r[...].astype(F32)
+    refs[-1][...] = dot(sel_ref[...], total.astype(BF), TN).astype(BF)
+
+
+def swapped(tokens, grad_out, picks, scores, w_gate, w_up, w_down):
+    n = lax.axis_size("seq")
+    replicas = lax.axis_size("dp")
+    tok_dev, half = tokens.shape[1:]
+    cap = picks.shape[1]
+    h = w_gate.shape[1]
+    rows = n * MOST
+    coeff = float(replicas * cap) ** -0.5
+
+    def index(d, k, t):
+        return (k * 2 + d) * 2 + t
+
+    def across(x, s):
+        pairs = [(index(d, k, t), index(t, k ^ s, d)) for d in range(2) for k in range(n) for t in range(2)]
+        return lax.ppermute(x, ("seq", "dp", "tensor"), pairs)
+
+    def swap(x, axis):
+        return lax.ppermute(x, axis, [(0, 1), (1, 0)])
+
+    gate, up, down = w_gate.T, w_up.T, w_down
+    x_mine, dz_mine, sel = call(
+        pack_body,
+        [arr((MOST, half)), arr((MOST, half)), arr((MOST, tok_dev))],
+        picks, scores, tokens[0], grad_out[0],
+    )
+    order = range(n)
+    x_own = [across(x_mine, s) for s in order]
+    dz_own = [across(dz_mine, s) for s in order]
+    gate_oth, up_oth, down_oth = (swap(w, "tensor") for w in (gate, up, down))
+    flops = 2 * rows * half * h
+    gu_send, gu_keep = call(
+        functools.partial(gate_up_body, n), [arr((4 * h, rows)), arr((4 * h, rows), F32)],
+        *x_own, gate, gate_oth, up, up_oth, flops=4 * flops,
+    )
+    gu_recv = swap(gu_send, "dp")
+    da_send, da_keep = call(
+        functools.partial(d_act_body, n), [arr((2 * h, rows)), arr((2 * h, rows), F32)],
+        *dz_own, down, down_oth, flops=2 * flops,
+    )
+    da_recv = swap(da_send, "dp")
+    x_oth = [swap(b, "tensor") for b in x_own]
+    dz_oth = [swap(b, "tensor") for b in dz_own]
+    own, lent, *dx = call(
+        functools.partial(middle_body, n),
+        [arr((3 * h, rows))] * 2 + [arr((MOST, half))] * n,
+        gu_keep, gu_recv, da_keep, da_recv, gate, gate_oth, up, up_oth, flops=4 * flops,
+    )
+    back = [across(b, s) for s, b in enumerate(dx)]
+    oth = swap(lent, "tensor")
+    grads = call(
+        functools.partial(weights_body, n, coeff, h), [arr((h, half))] * 3,
+        *x_own, *x_oth, *dz_own, *dz_oth, own, oth, flops=6 * flops,
+    )
+    (grad_local,) = call(spread_body, [arr((tok_dev, half))], sel, *back)
+    return grad_local[None], grads[0].T, grads[1].T, grads[2]
+
+
+def gathered(tokens, grad_out, picks, scores, w_gate, w_up, w_down):
     tok_dev = tokens.shape[1]
     half = tokens.shape[2]
     seq_count = lax.axis_size("seq")
@@ -131,4 +299,7 @@
         P(("groups", "dp"), ("seq", "tensor")),
         P(("groups", "seq", "tensor"), "dp"),
     )
+    size = mesh.shape
+    pairs = size["dp"] == size["tensor"] == 2 and size["seq"] in (2, 4, 8)
+    local = swapped if pairs else gathered
     return jax.shard_map(local, mesh=mesh, in_specs=in_specs, out_specs=out_specs, check_vma=False)

time: 184 us -> 57 us (0.31)
  blocking collectives: 69.4 us -> 0 us
  waiting for transfers between devices: 72.9 us -> 12.5 us
  starting transfers between devices: 3.45 us -> 34.5 us
  between operations: 15.7 us -> 0.78 us
  other arithmetic: 7.99 us -> 0 us
  matrix products: 7.69 us -> 0 us
  Pallas kernels: 0 us -> 4.7 us
  local copies, waits for them, and re-layouts: 6.2 us -> 4.24 us
    all_gather x5 -> x0, blocking collectives: 69.4 us -> none  [the longest x1 16.6 us: local(): lax.all_gather(pack_grads, ('seq', 'tensor'), axis=0, tiled=True)]
    psum x1 -> x0, waiting for transfers between devices: 38.1 us -> none  [local(): lax.psum(term_gate, 'dp').astype(jnp.float32)]
    ppermute x0 -> x26, starting transfers between devices: none -> 34.5 us  [the longest x12 19.8 us: across(): return lax.ppermute(x, ('seq', 'dp', 'tensor'), pairs)]
    reduce_scatter x1 -> x0, waiting for transfers between devices: 28.1 us -> none  [local(): lax.psum_scatter(result + lax.dot_general(d_up, full_up, last_dims, prefe...]
    ppermute x0 -> x26, waiting for transfers between devices: none -> 12.5 us  [the longest x12 8.18 us: across(): return lax.ppermute(x, ('seq', 'dp', 'tensor'), pairs)]
    dot_general x9 -> x0, matrix products: 7.69 us -> none  [the longest x1 1.42 us: local(): lax.dot_general(act, dz, first_dims, preferred_element_type=jnp.float32)]
    all_to_all x1 -> x0, waiting for transfers between devices: 6.68 us -> none  [local(): lax.all_to_all(outgoing.reshape(seq_count * ten_count * each, half), ('se...]
    gather x7 -> x0, local copies, waits for them, and re-layouts: 5.44 us -> none  [the longest x4 2.83 us: unpack(): jnp.take(block, (owner * ten_count + part) * MOST + slot_of, axis=0)]
  transfers between devices with their start and end apart: 3 -> 26, of which waited for: 3 -> 5; matrix products, arithmetic and copies ran while one was open for 4% -> 0% of each run, Pallas kernels for 0% -> 5%
where the time goes in v1:
time: 57 us; the launch traced here: 56.8 us
  starting transfers between devices  34.5 us (61%)
  waiting for transfers between devices  12.5 us (22%)
  Pallas kernels  4.7 us (8%)
  local copies, waits for them, and re-layouts  4.24 us (7%)
  between operations  0.78 us (1%)
    ppermute x12, starting transfers between devices, across(): return lax.ppermute(x, ('seq', 'dp', 'tensor'), pairs)  19.8 us
    ppermute x14, starting transfers between devices, swap(): return lax.ppermute(x, axis, [(0, 1), (1, 0)])  14.7 us
    ppermute x12, waiting for transfers between devices, across(): return lax.ppermute(x, ('seq', 'dp', 'tensor'), pairs)  8.18 us
    pallas_call x6, Pallas kernels, call(): pl.pallas_call(body, out_shape=outs, in_specs=[pl.BlockSpec(memory_space=...  4.7 us
    ppermute x14, waiting for transfers between devices, swap(): return lax.ppermute(x, axis, [(0, 1), (1, 0)])  4.34 us
    unnamed x16, local copies, waits for them, and re-layouts  4.24 us
  transfers between devices with their start and end apart: 26, of which 5 were waited for; matrix products, arithmetic and copies ran while one was open for 0% of the time, Pallas kernels for 5%

profile of v1, /device:TPU:0, one launch (start us, length us, event | category | flops | bytes accessed | tf_op | source)
XLA Modules:
  0.0 56.8 jit_solution(5014293515850447496)
XLA Ops:
  0.6 0.5 collective-permute-start.4
  1.7 0.9 %copy-done.4 = bf16[1,128,1024]{2,1,0:T(8,128)(2,1)S(1)} copy-done((bf16[1,128,1024]{2,1,0:T(8,128)(2,1)S(1)}, bf16[1,128,1024]{2,1,0:T(8,128)(2,1)}, u32[]{:S(2)}) %copy-start.4) | copy-done | bytes 262168
  2.6 0.9 %copy-done.5 = bf16[1,128,1024]{2,1,0:T(8,128)(2,1)S(1)} copy-done((bf16[1,128,1024]{2,1,0:T(8,128)(2,1)S(1)}, bf16[1,128,1024]{2,1,0:T(8,128)(2,1)}, u32[]{:S(2)}) %copy-start.5) | copy-done | bytes 262168
  3.6 0.7 %copy-done.6 = s32[1,64]{1,0:T(1,128)S(1)} copy-done((s32[1,64]{1,0:T(1,128)S(1)}, s32[1,64]{1,0:T(1,128)}, u32[]{:S(2)}) %copy-start.6) | copy-done | bytes 280
  4.2 0.7 %copy-done.7 = f32[1,64]{1,0:T(1,128)S(1)} copy-done((f32[1,64]{1,0:T(1,128)S(1)}, f32[1,64]{1,0:T(1,128)}, u32[]{:S(2)}) %copy-start.7) | copy-done | bytes 280
  5.4 0.7 %collective-permute-start = (bf16[32,1024]{1,0:T(8,128)(2,1)S(1)}, bf16[32,1024]{1,0:T(8,128)(2,1)S(1)}, u32[]{:S(2)}, u32[]{:S(2)}) collective-permute-start(bf16[32,1024]{1,0:T(8,128)(2,1)S(1)} %get-tuple-element.21), channel_id=1, source_target_pairs={{0,0},{1,2},{4,4},{5,6},{8,8},{9,10},{12,12},{13,14},{2,1},{3,3},{... | collective-permute-start | bytes 196616 | tf_op jit(solution)/shard_map/ppermute | solution.py:134
  6.0 2.7 %collective-permute-start.1 = (bf16[32,1024]{1,0:T(8,128)(2,1)S(1)}, bf16[32,1024]{1,0:T(8,128)(2,1)S(1)}, u32[]{:S(2)}, u32[]{:S(2)}) collective-permute-start(bf16[32,1024]{1,0:T(8,128)(2,1)S(1)} %get-tuple-element.21), channel_id=1, source_target_pairs={{0,4},{1,6},{4,0},{5,2},{8,12},{9,14},{12,8},{13,10},{2,5},{3,7},{... | collective-permute-start | bytes 196616 | tf_op jit(solution)/shard_map/ppermute | solution.py:134
  8.8 2.6 %collective-permute-start.2 = (bf16[32,1024]{1,0:T(8,128)(2,1)S(1)}, bf16[32,1024]{1,0:T(8,128)(2,1)S(1)}, u32[]{:S(2)}, u32[]{:S(2)}) collective-permute-start(bf16[32,1024]{1,0:T(8,128)(2,1)S(1)} %get-tuple-element.21), channel_id=1, source_target_pairs={{0,8},{1,10},{4,12},{5,14},{8,0},{9,2},{12,4},{13,6},{2,9},{3,11},... | collective-permute-start | bytes 196616 | tf_op jit(solution)/shard_map/ppermute | solution.py:134
  11.3 3.7 %collective-permute-start.3 = (bf16[32,1024]{1,0:T(8,128)(2,1)S(1)}, bf16[32,1024]{1,0:T(8,128)(2,1)S(1)}, u32[]{:S(2)}, u32[]{:S(2)}) collective-permute-start(bf16[32,1024]{1,0:T(8,128)(2,1)S(1)} %get-tuple-element.21), channel_id=1, source_target_pairs={{0,12},{1,14},{4,8},{5,10},{8,4},{9,6},{12,0},{13,2},{2,13},{3,15}... | collective-permute-start | bytes 196616 | tf_op jit(solution)/shard_map/ppermute | solution.py:134
  15.0 0.7 %collective-permute-start.7 = (bf16[32,1024]{1,0:T(8,128)(2,1)S(1)}, bf16[32,1024]{1,0:T(8,128)(2,1)S(1)}, u32[]{:S(2)}, u32[]{:S(2)}) collective-permute-start(bf16[32,1024]{1,0:T(8,128)(2,1)S(1)} %get-tuple-element.24), channel_id=1, source_target_pairs={{0,0},{1,2},{4,4},{5,6},{8,8},{9,10},{12,12},{13,14},{2,1},{3,3},{... | collective-permute-start | bytes 196616 | tf_op jit(solution)/shard_map/ppermute | solution.py:134
  15.7 1.8 %collective-permute-done.3.refs_3_ = bf16[32,1024]{1,0:T(8,128)(2,1)S(1)} collective-permute-done((bf16[32,1024]{1,0:T(8,128)(2,1)S(1)}, bf16[32,1024]{1,0:T(8,128)(2,1)S(1)}, u32[]{:S(2)}, u32[]{:S(2)}) %collective-permute-start.3) | collective-permute-done | bytes 65568 | tf_op jit(solution)/shard_map/ppermute | solution.py:134
  17.5 1.0 %copy-done.1 = bf16[1024,224]{0,1:T(8,128)(2,1)S(1)} copy-done((bf16[1024,224]{0,1:T(8,128)(2,1)S(1)}, bf16[1024,224]{0,1:T(8,128)(2,1)}, u32[]{:S(2)}) %copy-start.1) | copy-done | bytes 458776
  18.5 0.6 %shard_map.103 = (bf16[896,128]{1,0:T(8,128)(2,1)S(1)}, f32[896,128]{1,0:T(8,128)S(1)}) custom-call(bf16[32,1024]{1,0:T(8,128)(2,1)S(1)} %collective-permute-done.refs_0_, bf16[32,1024]{1,0:T(8,128)(2,1)S(1)} %collective-permute-done.1.refs_1_, bf16[32,1024]{1,0:T(8,128)(2,1)S(1)} %collective-permute-done.2.refs_2_, ...), custom_call_target="tpu_custom_call" | custom-call | flops 234881024 | bytes 2785280 | tf_op jit(solution)/shard_map/pallas_call | solution.py:24
  19.2 5.2 %collective-permute-start.6 = (bf16[896,128]{1,0:T(8,128)(2,1)S(1)}, bf16[896,128]{1,0:T(8,128)(2,1)S(1)}, u32[]{:S(2)}, u32[]{:S(2)}) collective-permute-start(bf16[896,128]{1,0:T(8,128)(2,1)S(1)} %get-tuple-element.23), channel_id=1, source_target_pairs={{0,2},{2,0},{1,3},{3,1},{4,6},{6,4},{5,7},{7,5},{8,10},{10,8},{9,1... | collective-permute-start | bytes 688136 | tf_op jit(solution)/shard_map/ppermute | solution.py:137
  24.4 0.8 %collective-permute-start.8 = (bf16[32,1024]{1,0:T(8,128)(2,1)S(1)}, bf16[32,1024]{1,0:T(8,128)(2,1)S(1)}, u32[]{:S(2)}, u32[]{:S(2)}) collective-permute-start(bf16[32,1024]{1,0:T(8,128)(2,1)S(1)} %get-tuple-element.24), channel_id=1, source_target_pairs={{0,4},{1,6},{4,0},{5,2},{8,12},{9,14},{12,8},{13,10},{2,5},{3,7},{... | collective-permute-start | bytes 196616 | tf_op jit(solution)/shard_map/ppermute | solution.py:134
  25.1 3.0 %collective-permute-start.9 = (bf16[32,1024]{1,0:T(8,128)(2,1)S(1)}, bf16[32,1024]{1,0:T(8,128)(2,1)S(1)}, u32[]{:S(2)}, u32[]{:S(2)}) collective-permute-start(bf16[32,1024]{1,0:T(8,128)(2,1)S(1)} %get-tuple-element.24), channel_id=1, source_target_pairs={{0,8},{1,10},{4,12},{5,14},{8,0},{9,2},{12,4},{13,6},{2,9},{3,11},... | collective-permute-start | bytes 196616 | tf_op jit(solution)/shard_map/ppermute | solution.py:134
  28.2 0.6 %collective-permute-start.10 = (bf16[32,1024]{1,0:T(8,128)(2,1)S(1)}, bf16[32,1024]{1,0:T(8,128)(2,1)S(1)}, u32[]{:S(2)}, u32[]{:S(2)}) collective-permute-start(bf16[32,1024]{1,0:T(8,128)(2,1)S(1)} %get-tuple-element.24), channel_id=1, source_target_pairs={{0,12},{1,14},{4,8},{5,10},{8,4},{9,6},{12,0},{13,2},{2,13},{3,15}... | collective-permute-start | bytes 196616 | tf_op jit(solution)/shard_map/ppermute | solution.py:134
  28.8 3.3 %collective-permute-done.9.refs_2_.refs_10_ = bf16[32,1024]{1,0:T(8,128)(2,1)S(1)} collective-permute-done((bf16[32,1024]{1,0:T(8,128)(2,1)S(1)}, bf16[32,1024]{1,0:T(8,128)(2,1)S(1)}, u32[]{:S(2)}, u32[]{:S(2)}) %collective-permute-start.9) | collective-permute-done | bytes 65568 | tf_op jit(solution)/shard_map/ppermute | solution.py:134
  32.0 2.6 %collective-permute-done.10.refs_3_.refs_11_ = bf16[32,1024]{1,0:T(8,128)(2,1)S(1)} collective-permute-done((bf16[32,1024]{1,0:T(8,128)(2,1)S(1)}, bf16[32,1024]{1,0:T(8,128)(2,1)S(1)}, u32[]{:S(2)}, u32[]{:S(2)}) %collective-permute-start.10) | collective-permute-done | bytes 65568 | tf_op jit(solution)/shard_map/ppermute | solution.py:134
  35.0 1.2 %collective-permute-start.12 = (bf16[448,128]{1,0:T(8,128)(2,1)S(1)}, bf16[448,128]{1,0:T(8,128)(2,1)S(1)}, u32[]{:S(2)}, u32[]{:S(2)}) collective-permute-start(bf16[448,128]{1,0:T(8,128)(2,1)S(1)} %get-tuple-element.26), channel_id=1, source_target_pairs={{0,2},{2,0},{1,3},{3,1},{4,6},{6,4},{5,7},{7,5},{8,10},{10,8},{9,1... | collective-permute-start | bytes 344072 | tf_op jit(solution)/shard_map/ppermute | solution.py:137
  36.7 4.3 %collective-permute-done.12.da_recv = bf16[448,128]{1,0:T(8,128)(2,1)S(1)} collective-permute-done((bf16[448,128]{1,0:T(8,128)(2,1)S(1)}, bf16[448,128]{1,0:T(8,128)(2,1)S(1)}, u32[]{:S(2)}, u32[]{:S(2)}) %collective-permute-start.12) | collective-permute-done | bytes 114720 | tf_op jit(solution)/shard_map/ppermute | solution.py:137
  41.0 0.5 shard_map.105
  41.5 0.6 collective-permute-start.25
  42.1 0.7 %collective-permute-start.13 = (bf16[32,1024]{1,0:T(8,128)(2,1)S(1)}, bf16[32,1024]{1,0:T(8,128)(2,1)S(1)}, u32[]{:S(2)}, u32[]{:S(2)}) collective-permute-start(bf16[32,1024]{1,0:T(8,128)(2,1)S(1)} %get-tuple-element.27), channel_id=1, source_target_pairs={{0,0},{1,2},{4,4},{5,6},{8,8},{9,10},{12,12},{13,14},{2,1},{3,3},{... | collective-permute-start | bytes 196616 | tf_op jit(solution)/shard_map/ppermute | solution.py:134
  42.9 1.9 %collective-permute-start.15 = (bf16[32,1024]{1,0:T(8,128)(2,1)S(1)}, bf16[32,1024]{1,0:T(8,128)(2,1)S(1)}, u32[]{:S(2)}, u32[]{:S(2)}) collective-permute-start(bf16[32,1024]{1,0:T(8,128)(2,1)S(1)} %get-tuple-element.29), channel_id=1, source_target_pairs={{0,8},{1,10},{4,12},{5,14},{8,0},{9,2},{12,4},{13,6},{2,9},{3,11},... | collective-permute-start | bytes 196616 | tf_op jit(solution)/shard_map/ppermute | solution.py:134
  44.8 2.5 %collective-permute-start.16 = (bf16[32,1024]{1,0:T(8,128)(2,1)S(1)}, bf16[32,1024]{1,0:T(8,128)(2,1)S(1)}, u32[]{:S(2)}, u32[]{:S(2)}) collective-permute-start(bf16[32,1024]{1,0:T(8,128)(2,1)S(1)} %get-tuple-element.30), channel_id=1, source_target_pairs={{0,12},{1,14},{4,8},{5,10},{8,4},{9,6},{12,0},{13,2},{2,13},{3,15}... | collective-permute-start | bytes 196616 | tf_op jit(solution)/shard_map/ppermute | solution.py:134
  47.2 3.1 %collective-permute-start.21 = (bf16[32,1024]{1,0:T(8,128)(2,1)S(1)}, bf16[32,1024]{1,0:T(8,128)(2,1)S(1)}, u32[]{:S(2)}, u32[]{:S(2)}) collective-permute-start(bf16[32,1024]{1,0:T(8,128)(2,1)S(1)} %collective-permute-done.7.refs_0_.refs_8_), channel_id=1, source_target_pairs={{0,1},{1,0},{2,3},{3,2},{4,5},{5,4},{6,7},{7,6},{8,9},{9,8},{10,11... | collective-permute-start | bytes 196616 | tf_op jit(solution)/shard_map/ppermute | solution.py:137
  50.4 0.6 collective-permute-start.23
  50.9 0.6 collective-permute-done.16.refs_3_
  51.5 2.5 %collective-permute-start.24 = (bf16[32,1024]{1,0:T(8,128)(2,1)S(1)}, bf16[32,1024]{1,0:T(8,128)(2,1)S(1)}, u32[]{:S(2)}, u32[]{:S(2)}) collective-permute-start(bf16[32,1024]{1,0:T(8,128)(2,1)S(1)} %collective-permute-done.10.refs_3_.refs_11_), channel_id=1, source_target_pairs={{0,1},{1,0},{2,3},{3,2},{4,5},{5,4},{6,7},{7,6},{8,9},{9,8},{10,11... | collective-permute-start | bytes 196616 | tf_op jit(solution)/shard_map/ppermute | solution.py:137
  54.0 1.0 %shard_map.106 = bf16[128,1024]{1,0:T(8,128)(2,1)} custom-call(bf16[32,128]{1,0:T(8,128)(2,1)S(1)} %get-tuple-element.20.sel_ref, bf16[32,1024]{1,0:T(8,128)(2,1)S(1)} %collective-permute-done.13.refs_0_, bf16[32,1024]{1,0:T(8,128)(2,1)S(1)} %collective-permute-done.14.refs_1_, bf16[32,1024]{1,0:T(8,128)(2,1)S(1)} %collective-permute-done.15.refs_2_, ...), custom_call_target="tpu_custom_call" | custom-call | bytes 532480 | tf_op jit(solution)/shard_map/pallas_call | solution.py:24
  55.0 1.7 %shard_map.107 = (bf16[224,1024]{1,0:T(8,128)(2,1)}, bf16[224,1024]{1,0:T(8,128)(2,1)}, bf16[224,1024]{1,0:T(8,128)(2,1)}) custom-call(bf16[32,1024]{1,0:T(8,128)(2,1)S(1)} %collective-permute-done.refs_0_, bf16[32,1024]{1,0:T(8,128)(2,1)S(1)} %collective-permute-done.1.refs_1_, bf16[32,1024]{1,0:T(8,128)(2,1)S(1)} %collective-permute-done.2.refs_2_, ...), custom_call_target="tpu_custom_call" | custom-call | flops 352321536 | bytes 2768896 | tf_op jit(solution)/shard_map/pallas_call | solution.py:24
  (42 shorter events, 2.1 us)
Async XLA Ops:
  0.6 16.9 %copy-start = (bf16[1024,224]{0,1:T(8,128)(2,1)S(1)}, bf16[1024,224]{0,1:T(8,128)(2,1)}, u32[]{:S(2)}) copy-start(bf16[1024,224]{0,1:T(8,128)(2,1)} %param.11) | copy-start | bytes 1376260
  0.6 16.8 %collective-permute-start.4 = (bf16[224,1024]{1,0:T(8,128)(2,1)}, bf16[224,1024]{1,0:T(8,128)(2,1)S(1)}, u32[]{:S(2)}, u32[]{:S(2)}) collective-permute-start(bf16[224,1024]{1,0:T(8,128)(2,1)} %bitcast.7), channel_id=1, source_target_pairs={{0,1},{1,0},{2,3},{3,2},{4,5},{5,4},{6,7},{7,6},{8,9},{9,8},{10,11... | collective-permute-start | bytes 1376264 | tf_op jit(solution)/shard_map/ppermute | solution.py:137
  1.2 16.3 %collective-permute-start.5 = (bf16[224,1024]{1,0:T(8,128)(2,1)}, bf16[224,1024]{1,0:T(8,128)(2,1)S(1)}, u32[]{:S(2)}, u32[]{:S(2)}) collective-permute-start(bf16[224,1024]{1,0:T(8,128)(2,1)} %bitcast.10), channel_id=1, source_target_pairs={{0,1},{1,0},{2,3},{3,2},{4,5},{5,4},{6,7},{7,6},{8,9},{9,8},{10,11... | collective-permute-start | bytes 1376264 | tf_op jit(solution)/shard_map/ppermute | solution.py:137
  1.2 33.3 %collective-permute-start.11 = (bf16[224,1024]{1,0:T(8,128)(2,1)}, bf16[224,1024]{1,0:T(8,128)(2,1)S(1)}, u32[]{:S(2)}, u32[]{:S(2)}) collective-permute-start(bf16[224,1024]{1,0:T(8,128)(2,1)} %refs_4_.1), channel_id=1, source_target_pairs={{0,1},{1,0},{2,3},{3,2},{4,5},{5,4},{6,7},{7,6},{8,9},{9,8},{10,11... | collective-permute-start | bytes 1376264 | tf_op jit(solution)/shard_map/ppermute | solution.py:137
  1.7 0.9 %copy-start.4 = (bf16[1,128,1024]{2,1,0:T(8,128)(2,1)S(1)}, bf16[1,128,1024]{2,1,0:T(8,128)(2,1)}, u32[]{:S(2)}) copy-start(bf16[1,128,1024]{2,1,0:T(8,128)(2,1)} %param.7) | copy-start | bytes 786436
  2.6 0.9 %copy-start.5 = (bf16[1,128,1024]{2,1,0:T(8,128)(2,1)S(1)}, bf16[1,128,1024]{2,1,0:T(8,128)(2,1)}, u32[]{:S(2)}) copy-start(bf16[1,128,1024]{2,1,0:T(8,128)(2,1)} %param.8) | copy-start | bytes 786436
  5.4 3.4 %collective-permute-start = (bf16[32,1024]{1,0:T(8,128)(2,1)S(1)}, bf16[32,1024]{1,0:T(8,128)(2,1)S(1)}, u32[]{:S(2)}, u32[]{:S(2)}) collective-permute-start(bf16[32,1024]{1,0:T(8,128)(2,1)S(1)} %get-tuple-element.21), channel_id=1, source_target_pairs={{0,0},{1,2},{4,4},{5,6},{8,8},{9,10},{12,12},{13,14},{2,1},{3,3},{... | collective-permute-start | bytes 196616 | tf_op jit(solution)/shard_map/ppermute | solution.py:134
  6.0 5.3 %collective-permute-start.1 = (bf16[32,1024]{1,0:T(8,128)(2,1)S(1)}, bf16[32,1024]{1,0:T(8,128)(2,1)S(1)}, u32[]{:S(2)}, u32[]{:S(2)}) collective-permute-start(bf16[32,1024]{1,0:T(8,128)(2,1)S(1)} %get-tuple-element.21), channel_id=1, source_target_pairs={{0,4},{1,6},{4,0},{5,2},{8,12},{9,14},{12,8},{13,10},{2,5},{3,7},{... | collective-permute-start | bytes 196616 | tf_op jit(solution)/shard_map/ppermute | solution.py:134
  8.8 6.3 %collective-permute-start.2 = (bf16[32,1024]{1,0:T(8,128)(2,1)S(1)}, bf16[32,1024]{1,0:T(8,128)(2,1)S(1)}, u32[]{:S(2)}, u32[]{:S(2)}) collective-permute-start(bf16[32,1024]{1,0:T(8,128)(2,1)S(1)} %get-tuple-element.21), channel_id=1, source_target_pairs={{0,8},{1,10},{4,12},{5,14},{8,0},{9,2},{12,4},{13,6},{2,9},{3,11},... | collective-permute-start | bytes 196616 | tf_op jit(solution)/shard_map/ppermute | solution.py:134
  11.3 6.1 %collective-permute-start.3 = (bf16[32,1024]{1,0:T(8,128)(2,1)S(1)}, bf16[32,1024]{1,0:T(8,128)(2,1)S(1)}, u32[]{:S(2)}, u32[]{:S(2)}) collective-permute-start(bf16[32,1024]{1,0:T(8,128)(2,1)S(1)} %get-tuple-element.21), channel_id=1, source_target_pairs={{0,12},{1,14},{4,8},{5,10},{8,4},{9,6},{12,0},{13,2},{2,13},{3,15}... | collective-permute-start | bytes 196616 | tf_op jit(solution)/shard_map/ppermute | solution.py:134
  15.0 13.1 %collective-permute-start.7 = (bf16[32,1024]{1,0:T(8,128)(2,1)S(1)}, bf16[32,1024]{1,0:T(8,128)(2,1)S(1)}, u32[]{:S(2)}, u32[]{:S(2)}) collective-permute-start(bf16[32,1024]{1,0:T(8,128)(2,1)S(1)} %get-tuple-element.24), channel_id=1, source_target_pairs={{0,0},{1,2},{4,4},{5,6},{8,8},{9,10},{12,12},{13,14},{2,1},{3,3},{... | collective-permute-start | bytes 196616 | tf_op jit(solution)/shard_map/ppermute | solution.py:134
  17.5 1.0 %copy-start.1 = (bf16[1024,224]{0,1:T(8,128)(2,1)S(1)}, bf16[1024,224]{0,1:T(8,128)(2,1)}, u32[]{:S(2)}) copy-start(bf16[1024,224]{0,1:T(8,128)(2,1)} %param.12) | copy-start | bytes 1376260
  18.5 16.1 %copy-start.3 = (bf16[224,1024]{1,0:T(8,128)(2,1)S(1)}, bf16[224,1024]{1,0:T(8,128)(2,1)}, u32[]{:S(2)}) copy-start(bf16[224,1024]{1,0:T(8,128)(2,1)} %refs_4_.1) | copy-start | bytes 1376260
  19.1 21.9 %copy-start.2 = (bf16[1024,224]{0,1:T(8,128)(2,1)S(1)}, bf16[1024,224]{0,1:T(8,128)(2,1)}, u32[]{:S(2)}) copy-start(bf16[1024,224]{0,1:T(8,128)(2,1)} %param.12) | copy-start | bytes 1376260
  19.2 21.8 %collective-permute-start.6 = (bf16[896,128]{1,0:T(8,128)(2,1)S(1)}, bf16[896,128]{1,0:T(8,128)(2,1)S(1)}, u32[]{:S(2)}, u32[]{:S(2)}) collective-permute-start(bf16[896,128]{1,0:T(8,128)(2,1)S(1)} %get-tuple-element.23), channel_id=1, source_target_pairs={{0,2},{2,0},{1,3},{3,1},{4,6},{6,4},{5,7},{7,5},{8,10},{10,8},{9,1... | collective-permute-start | bytes 688136 | tf_op jit(solution)/shard_map/ppermute | solution.py:137
  24.4 4.4 %collective-permute-start.8 = (bf16[32,1024]{1,0:T(8,128)(2,1)S(1)}, bf16[32,1024]{1,0:T(8,128)(2,1)S(1)}, u32[]{:S(2)}, u32[]{:S(2)}) collective-permute-start(bf16[32,1024]{1,0:T(8,128)(2,1)S(1)} %get-tuple-element.24), channel_id=1, source_target_pairs={{0,4},{1,6},{4,0},{5,2},{8,12},{9,14},{12,8},{13,10},{2,5},{3,7},{... | collective-permute-start | bytes 196616 | tf_op jit(solution)/shard_map/ppermute | solution.py:134
  25.1 6.9 %collective-permute-start.9 = (bf16[32,1024]{1,0:T(8,128)(2,1)S(1)}, bf16[32,1024]{1,0:T(8,128)(2,1)S(1)}, u32[]{:S(2)}, u32[]{:S(2)}) collective-permute-start(bf16[32,1024]{1,0:T(8,128)(2,1)S(1)} %get-tuple-element.24), channel_id=1, source_target_pairs={{0,8},{1,10},{4,12},{5,14},{8,0},{9,2},{12,4},{13,6},{2,9},{3,11},... | collective-permute-start | bytes 196616 | tf_op jit(solution)/shard_map/ppermute | solution.py:134
  28.2 6.4 %collective-permute-start.10 = (bf16[32,1024]{1,0:T(8,128)(2,1)S(1)}, bf16[32,1024]{1,0:T(8,128)(2,1)S(1)}, u32[]{:S(2)}, u32[]{:S(2)}) collective-permute-start(bf16[32,1024]{1,0:T(8,128)(2,1)S(1)} %get-tuple-element.24), channel_id=1, source_target_pairs={{0,12},{1,14},{4,8},{5,10},{8,4},{9,6},{12,0},{13,2},{2,13},{3,15}... | collective-permute-start | bytes 196616 | tf_op jit(solution)/shard_map/ppermute | solution.py:134
  35.0 6.0 %collective-permute-start.12 = (bf16[448,128]{1,0:T(8,128)(2,1)S(1)}, bf16[448,128]{1,0:T(8,128)(2,1)S(1)}, u32[]{:S(2)}, u32[]{:S(2)}) collective-permute-start(bf16[448,128]{1,0:T(8,128)(2,1)S(1)} %get-tuple-element.26), channel_id=1, source_target_pairs={{0,2},{2,0},{1,3},{3,1},{4,6},{6,4},{5,7},{7,5},{8,10},{10,8},{9,1... | collective-permute-start | bytes 344072 | tf_op jit(solution)/shard_map/ppermute | solution.py:137
  36.2 5.9 %collective-permute-start.17 = (bf16[32,1024]{1,0:T(8,128)(2,1)S(1)}, bf16[32,1024]{1,0:T(8,128)(2,1)S(1)}, u32[]{:S(2)}, u32[]{:S(2)}) collective-permute-start(bf16[32,1024]{1,0:T(8,128)(2,1)S(1)} %collective-permute-done.refs_0_), channel_id=1, source_target_pairs={{0,1},{1,0},{2,3},{3,2},{4,5},{5,4},{6,7},{7,6},{8,9},{9,8},{10,11... | collective-permute-start | bytes 196616 | tf_op jit(solution)/shard_map/ppermute | solution.py:137
  36.2 6.6 %collective-permute-start.18 = (bf16[32,1024]{1,0:T(8,128)(2,1)S(1)}, bf16[32,1024]{1,0:T(8,128)(2,1)S(1)}, u32[]{:S(2)}, u32[]{:S(2)}) collective-permute-start(bf16[32,1024]{1,0:T(8,128)(2,1)S(1)} %collective-permute-done.1.refs_1_), channel_id=1, source_target_pairs={{0,1},{1,0},{2,3},{3,2},{4,5},{5,4},{6,7},{7,6},{8,9},{9,8},{10,11... | collective-permute-start | bytes 196616 | tf_op jit(solution)/shard_map/ppermute | solution.py:137
  36.7 6.2 %collective-permute-start.19 = (bf16[32,1024]{1,0:T(8,128)(2,1)S(1)}, bf16[32,1024]{1,0:T(8,128)(2,1)S(1)}, u32[]{:S(2)}, u32[]{:S(2)}) collective-permute-start(bf16[32,1024]{1,0:T(8,128)(2,1)S(1)} %collective-permute-done.2.refs_2_), channel_id=1, source_target_pairs={{0,1},{1,0},{2,3},{3,2},{4,5},{5,4},{6,7},{7,6},{8,9},{9,8},{10,11... | collective-permute-start | bytes 196616 | tf_op jit(solution)/shard_map/ppermute | solution.py:137
  41.0 3.8 %collective-permute-start.20 = (bf16[32,1024]{1,0:T(8,128)(2,1)S(1)}, bf16[32,1024]{1,0:T(8,128)(2,1)S(1)}, u32[]{:S(2)}, u32[]{:S(2)}) collective-permute-start(bf16[32,1024]{1,0:T(8,128)(2,1)S(1)} %collective-permute-done.3.refs_3_), channel_id=1, source_target_pairs={{0,1},{1,0},{2,3},{3,2},{4,5},{5,4},{6,7},{7,6},{8,9},{9,8},{10,11... | collective-permute-start | bytes 196616 | tf_op jit(solution)/shard_map/ppermute | solution.py:137
  41.5 13.5 %collective-permute-start.25 = (bf16[672,128]{1,0:T(8,128)(2,1)S(1)}, bf16[672,128]{1,0:T(8,128)(2,1)S(1)}, u32[]{:S(2)}, u32[]{:S(2)}) collective-permute-start(bf16[672,128]{1,0:T(8,128)(2,1)S(1)} %get-tuple-element.32), channel_id=1, source_target_pairs={{0,1},{1,0},{2,3},{3,2},{4,5},{5,4},{6,7},{7,6},{8,9},{9,8},{10,11... | collective-permute-start | bytes 516104 | tf_op jit(solution)/shard_map/ppermute | solution.py:137
  42.1 5.1 %collective-permute-start.13 = (bf16[32,1024]{1,0:T(8,128)(2,1)S(1)}, bf16[32,1024]{1,0:T(8,128)(2,1)S(1)}, u32[]{:S(2)}, u32[]{:S(2)}) collective-permute-start(bf16[32,1024]{1,0:T(8,128)(2,1)S(1)} %get-tuple-element.27), channel_id=1, source_target_pairs={{0,0},{1,2},{4,4},{5,6},{8,8},{9,10},{12,12},{13,14},{2,1},{3,3},{... | collective-permute-start | bytes 196616 | tf_op jit(solution)/shard_map/ppermute | solution.py:134
  42.8 7.5 %collective-permute-start.14 = (bf16[32,1024]{1,0:T(8,128)(2,1)S(1)}, bf16[32,1024]{1,0:T(8,128)(2,1)S(1)}, u32[]{:S(2)}, u32[]{:S(2)}) collective-permute-start(bf16[32,1024]{1,0:T(8,128)(2,1)S(1)} %get-tuple-element.28), channel_id=1, source_target_pairs={{0,4},{1,6},{4,0},{5,2},{8,12},{9,14},{12,8},{13,10},{2,5},{3,7},{... | collective-permute-start | bytes 196616 | tf_op jit(solution)/shard_map/ppermute | solution.py:134
  42.9 7.5 %collective-permute-start.15 = (bf16[32,1024]{1,0:T(8,128)(2,1)S(1)}, bf16[32,1024]{1,0:T(8,128)(2,1)S(1)}, u32[]{:S(2)}, u32[]{:S(2)}) collective-permute-start(bf16[32,1024]{1,0:T(8,128)(2,1)S(1)} %get-tuple-element.29), channel_id=1, source_target_pairs={{0,8},{1,10},{4,12},{5,14},{8,0},{9,2},{12,4},{13,6},{2,9},{3,11},... | collective-permute-start | bytes 196616 | tf_op jit(solution)/shard_map/ppermute | solution.py:134
  44.8 6.7 %collective-permute-start.16 = (bf16[32,1024]{1,0:T(8,128)(2,1)S(1)}, bf16[32,1024]{1,0:T(8,128)(2,1)S(1)}, u32[]{:S(2)}, u32[]{:S(2)}) collective-permute-start(bf16[32,1024]{1,0:T(8,128)(2,1)S(1)} %get-tuple-element.30), channel_id=1, source_target_pairs={{0,12},{1,14},{4,8},{5,10},{8,4},{9,6},{12,0},{13,2},{2,13},{3,15}... | collective-permute-start | bytes 196616 | tf_op jit(solution)/shard_map/ppermute | solution.py:134
  47.2 7.8 %collective-permute-start.21 = (bf16[32,1024]{1,0:T(8,128)(2,1)S(1)}, bf16[32,1024]{1,0:T(8,128)(2,1)S(1)}, u32[]{:S(2)}, u32[]{:S(2)}) collective-permute-start(bf16[32,1024]{1,0:T(8,128)(2,1)S(1)} %collective-permute-done.7.refs_0_.refs_8_), channel_id=1, source_target_pairs={{0,1},{1,0},{2,3},{3,2},{4,5},{5,4},{6,7},{7,6},{8,9},{9,8},{10,11... | collective-permute-start | bytes 196616 | tf_op jit(solution)/shard_map/ppermute | solution.py:137
  50.3 4.7 %collective-permute-start.22 = (bf16[32,1024]{1,0:T(8,128)(2,1)S(1)}, bf16[32,1024]{1,0:T(8,128)(2,1)S(1)}, u32[]{:S(2)}, u32[]{:S(2)}) collective-permute-start(bf16[32,1024]{1,0:T(8,128)(2,1)S(1)} %collective-permute-done.8.refs_1_.refs_9_), channel_id=1, source_target_pairs={{0,1},{1,0},{2,3},{3,2},{4,5},{5,4},{6,7},{7,6},{8,9},{9,8},{10,11... | collective-permute-start | bytes 196616 | tf_op jit(solution)/shard_map/ppermute | solution.py:137
  50.4 4.6 %collective-permute-start.23 = (bf16[32,1024]{1,0:T(8,128)(2,1)S(1)}, bf16[32,1024]{1,0:T(8,128)(2,1)S(1)}, u32[]{:S(2)}, u32[]{:S(2)}) collective-permute-start(bf16[32,1024]{1,0:T(8,128)(2,1)S(1)} %collective-permute-done.9.refs_2_.refs_10_), channel_id=1, source_target_pairs={{0,1},{1,0},{2,3},{3,2},{4,5},{5,4},{6,7},{7,6},{8,9},{9,8},{10,11... | collective-permute-start | bytes 196616 | tf_op jit(solution)/shard_map/ppermute | solution.py:137
  51.5 3.5 %collective-permute-start.24 = (bf16[32,1024]{1,0:T(8,128)(2,1)S(1)}, bf16[32,1024]{1,0:T(8,128)(2,1)S(1)}, u32[]{:S(2)}, u32[]{:S(2)}) collective-permute-start(bf16[32,1024]{1,0:T(8,128)(2,1)S(1)} %collective-permute-done.10.refs_3_.refs_11_), channel_id=1, source_target_pairs={{0,1},{1,0},{2,3},{3,2},{4,5},{5,4},{6,7},{7,6},{8,9},{9,8},{10,11... | collective-permute-start | bytes 196616 | tf_op jit(solution)/shard_map/ppermute | solution.py:137
  (2 other events, 1.3 us)

commit v2 on v0

--- a/solution.py
+++ b/solution.py
@@ -1,12 +1,216 @@
+import functools
+
 import jax
 import jax.numpy as jnp
 from jax import lax
+from jax.experimental import pallas as pl
+from jax.experimental.pallas import tpu as pltpu
 from jax.sharding import PartitionSpec as P
 
 MOST = 32
-
-
-def local(tokens, grad_out, picks, scores, w_gate, w_up, w_down):
+BF = jnp.bfloat16
+F32 = jnp.float32
+NN = (((1,), (0,)), ((), ()))
+NT = (((1,), (1,)), ((), ()))
+TN = (((0,), (0,)), ((), ()))
+
+
+def dot(a, b, dims):
+    return lax.dot_general(a, b, dims, preferred_element_type=F32)
+
+
+def call(body, outs, *args, flops=0, after=(), far=False, scratch=(), mib=24, far_out=0):
+    size = sum(a.size * a.dtype.itemsize for a in args) + sum(o.size * o.dtype.itemsize for o in outs)
+    count = len(args)
+
+    def run(*refs):
+        body(*refs[:count], *refs[count + len(after) :])
+
+    return pl.pallas_call(
+        run,
+        out_shape=outs,
+        in_specs=[pl.BlockSpec(memory_space=pltpu.HBM if far else pltpu.VMEM)] * len(args)
+        + [pl.BlockSpec(memory_space=pl.ANY)] * len(after),
+        out_specs=[pl.BlockSpec(memory_space=pltpu.VMEM)] * (len(outs) - far_out) + [pl.BlockSpec(memory_space=pltpu.HBM)] * far_out,
+        scratch_shapes=list(scratch),
+        cost_estimate=pl.CostEstimate(flops=flops, bytes_accessed=size, transcendentals=0),
+        compiler_params=pltpu.CompilerParams(vmem_limit_bytes=int(mib * 1024 * 1024)),
+    )(*args, *after)
+
+
+def arr(shape, dtype=BF):
+    return jax.ShapeDtypeStruct(shape, dtype)
+
+
+def pack_body(picks_in, scores_in, tok_in, grad_in, gate_in, up_in, down_in, xd_ref, sel_ref, w_out, picks_ref, scores_ref, tok_ref, grad_ref, w_ref, sems):
+    pairs = [(picks_in, picks_ref), (scores_in, scores_ref), (tok_in, tok_ref), (grad_in, grad_ref)]
+    h = gate_in.shape[0]
+    pairs += [(w, w_ref.at[i * h : (i + 1) * h]) for i, w in enumerate((gate_in, up_in, down_in))]
+    copies = [pltpu.make_async_copy(a, b, sems.at[i]) for i, (a, b) in enumerate(pairs)]
+    for c in copies:
+        c.start()
+    tok_dev = tok_ref.shape[0]
+    cap = picks_ref.shape[1]
+    base = lax.axis_index("seq") * tok_dev
+    before = (
+        lax.broadcasted_iota(jnp.int32, (tok_dev, tok_dev), 0) < lax.broadcasted_iota(jnp.int32, (tok_dev, tok_dev), 1)
+    ).astype(F32).astype(BF)
+    slots = lax.broadcasted_iota(jnp.int32, (MOST, tok_dev), 0).astype(F32)
+    copies[0].wait()
+    where = picks_ref[...] - base
+    hit = (lax.broadcasted_iota(jnp.int32, (tok_dev, cap), 0) == where).astype(F32).astype(BF)
+    picked = dot(jnp.ones((8, cap), BF), hit, NT)
+    rank = dot(picked.astype(BF), before, NN)[0:1]
+    sel = jnp.where((rank == slots) & (picked[0:1] > 0.5), 1.0, 0.0).astype(BF)
+    sel_ref[...] = sel
+    chosen = dot(sel, hit, NN)
+    for c in copies[4:]:
+        c.wait()
+    out = pltpu.make_async_copy(w_ref, w_out, sems.at[7])
+    out.start()
+    copies[1].wait()
+    score = jnp.sum(chosen * scores_ref[...], axis=1, keepdims=True)
+    copies[2].wait()
+    xd_ref[0:MOST] = dot(sel, tok_ref[...], NN).astype(BF)
+    copies[3].wait()
+    xd_ref[MOST:] = (score * dot(sel, grad_ref[...], NN)).astype(BF)
+    out.wait()
+
+
+def partial_body(blocks, *refs):
+    w_own, w_oth, keep_ref = refs[blocks : blocks + 3]
+    h = w_own.shape[0] // 3
+    x = jnp.concatenate([r[0:MOST] for r in refs[:blocks]], axis=0)
+    dz = jnp.concatenate([r[MOST:] for r in refs[:blocks]], axis=0)
+    for at, a in ((slice(0, 2 * h), x), (slice(2 * h, 3 * h), dz)):
+        keep_ref[at] = jnp.concatenate([dot(w[at], a, NT) for w in (w_own, w_oth)], axis=1)
+    done = 0
+    for send_ref in refs[blocks + 3 :]:
+        send_ref[...] = keep_ref[done : done + send_ref.shape[0]].astype(BF)
+        done += send_ref.shape[0]
+
+
+def terms(keep, recv, dd_ref):
+    h = keep.shape[0] // 3
+    got = jnp.concatenate([r[...] for r in recv], axis=0).astype(F32)
+    gate, upper, d_act = (keep[i * h : (i + 1) * h] + got[i * h : (i + 1) * h] for i in range(3))
+    sigma = jax.nn.sigmoid(gate)
+    gs = gate * sigma
+    dd_ref[0:h] = (d_act * upper * sigma * (1.0 + gate * (1.0 - sigma))).astype(BF)
+    dd_ref[h : 2 * h] = (d_act * gs).astype(BF)
+    dd_ref[2 * h :] = (gs * upper).astype(BF)
+
+
+def back_rows(dd, w_own, w_oth, dx_refs):
+    at = slice(0, 2 * w_own.shape[0] // 3)
+    m = dd.shape[1] // 2
+    total = dot(dd[at], w_own[at], TN)[0:m] + dot(dd[at], w_oth[at], TN)[m:]
+    for s, ref in enumerate(dx_refs):
+        ref[...] = total[s * MOST : (s + 1) * MOST].astype(BF)
+
+
+def first_body(recv, keep, *refs):
+    w_own, w_oth, dd_ref, *dx_refs = refs[recv:]
+    terms(keep, refs[:recv], dd_ref)
+    back_rows(dd_ref, w_own, w_oth, dx_refs)
+
+
+def second_body(blocks, keep, recv, w_own, w_oth, dd_a, *refs):
+    dd_ref, rows_ref, *dx_refs = refs[blocks:]
+    m = dd_a.shape[1]
+    terms(keep, [recv], dd_ref.at[:, m:])
+    back_rows(dd_ref.at[:, m:], w_own, w_oth, dx_refs)
+    dd_ref[:, 0:m] = dd_a[...]
+    for s, block in enumerate(refs[:blocks]):
+        rows_ref[s * MOST : (s + 1) * MOST] = block[0:MOST]
+        rows_ref[(blocks + s) * MOST : (blocks + s + 1) * MOST] = block[MOST:]
+
+
+def weights_body(coeff, rows_own, rows_oth, own, oth, gate_ref, up_ref, down_ref, token_ref):
+    h = gate_ref.shape[0]
+    m = rows_own.shape[0] // 4
+    zero = jnp.zeros((m, rows_own.shape[1]), BF)
+    for i, out in enumerate((gate_ref, up_ref, down_ref)):
+        at = slice(i * h, (i + 1) * h)
+        r = 0 if i < 2 else 2 * m
+        mine = jnp.concatenate([rows_own[r : r + m], zero, rows_own[r + m : r + 2 * m], zero], axis=0)
+        others = jnp.concatenate([zero, rows_oth[r : r + m], zero, rows_oth[r + m : r + 2 * m]], axis=0)
+        one = dot(own[at], mine, NN)
+        two = dot(oth[at], others, NN)
+        out[...] = ((coeff * one).astype(BF).astype(F32) + (coeff * two).astype(BF).astype(F32)).astype(BF)
+    token_ref[...] = jnp.zeros_like(token_ref)
+
+
+def spread_body(sel_ref, *refs):
+    total = refs[0][...].astype(F32)
+    for r in refs[1:-1]:
+        total += r[...].astype(F32)
+    refs[-1][...] = dot(sel_ref[...], total.astype(BF), TN).astype(BF)
+
+
+def swapped(tokens, grad_out, picks, scores, w_gate, w_up, w_down):
+    n = lax.axis_size("seq")
+    replicas = lax.axis_size("dp")
+    tok_dev, half = tokens.shape[1:]
+    cap = picks.shape[1]
+    h = w_gate.shape[1]
+    m = n // 2 * MOST
+    coeff = float(replicas * cap) ** -0.5
+
+    def index(d, k, t):
+        return (k * 2 + d) * 2 + t
+
+    def across(x, s):
+        pairs = [(index(d, k, t), index(t, k ^ s, d)) for d in range(2) for k in range(n) for t in range(2)]
+        return lax.ppermute(x, ("seq", "dp", "tensor"), pairs)
+
+    def swap(x, axis):
+        return lax.ppermute(x, axis, [(0, 1), (1, 0)])
+
+    xd, sel, w_own = call(
+        pack_body,
+        [arr((2 * MOST, half)), arr((MOST, tok_dev)), arr((3 * h, half))],
+        picks, scores, tokens[0], grad_out[0], w_gate.T, w_up.T, w_down,
+        far=True, far_out=1, mib=60,
+        scratch=[pltpu.VMEM((1, cap), jnp.int32), pltpu.VMEM((1, cap), F32), pltpu.VMEM((tok_dev, half), BF),
+                 pltpu.VMEM((tok_dev, half), BF), pltpu.VMEM((3 * h, half), BF), pltpu.SemaphoreType.DMA((8,))],
+    )
+    blocks = {s: across(xd, s) for s in range(n)}
+    w_oth = swap(w_own, "tensor")
+    flops = 2 * m * half * h
+
+    def partial(group, parts, after=()):
+        keep, *send = call(
+            functools.partial(partial_body, len(group)),
+            [arr((3 * h, 2 * m), F32)] + [arr((p * h, 2 * m)) for p in parts],
+            *(blocks[s] for s in group), w_own, w_oth, flops=6 * flops, after=after,
+        )
+        return keep, [swap(b, "dp") for b in send]
+
+    near, far = range(n // 2), range(n // 2, n)
+    dx = [arr((MOST, half))] * (n // 2)
+    keep_a, recv_a = partial(near, (2, 1))
+    keep_b, recv_b = partial(far, (3,), after=recv_a)
+    dd_a, *dx_a = call(
+        functools.partial(first_body, len(recv_a)), [arr((3 * h, 2 * m))] + dx,
+        keep_a, *recv_a, w_own, w_oth, flops=8 * flops, after=(keep_b,),
+    )
+    back = [across(b, s) for s, b in zip(near, dx_a)]
+    own, rows_own, *dx_b = call(
+        functools.partial(second_body, n), [arr((3 * h, 4 * m)), arr((2 * n * MOST, half))] + dx,
+        keep_b, *recv_b, w_own, w_oth, dd_a, *(blocks[s] for s in range(n)), flops=8 * flops, after=back,
+    )
+    back += [across(b, s) for s, b in zip(far, dx_b)]
+    rows_oth, oth = swap(rows_own, "tensor"), swap(own, "tensor")
+    grads = call(
+        functools.partial(weights_body, coeff), [arr((h, half))] * 3 + [arr((8, 128), F32)],
+        rows_own, rows_oth, own, oth, flops=12 * flops,
+    )
+    (grad_local,) = call(spread_body, [arr((tok_dev, half))], sel, *back, after=grads[3:])
+    return grad_local[None], grads[0].T, grads[1].T, grads[2]
+
+
+def gathered(tokens, grad_out, picks, scores, w_gate, w_up, w_down):
     tok_dev = tokens.shape[1]
     half = tokens.shape[2]
     seq_count = lax.axis_size("seq")
@@ -131,4 +335,7 @@
         P(("groups", "dp"), ("seq", "tensor")),
         P(("groups", "seq", "tensor"), "dp"),
     )
+    size = mesh.shape
+    pairs = size["dp"] == size["tensor"] == 2 and size["seq"] in (2, 4, 8)
+    local = swapped if pairs else gathered
     return jax.shard_map(local, mesh=mesh, in_specs=in_specs, out_specs=out_specs, check_vma=False)

time: 184 us -> 45.2 us (0.25)
  blocking collectives: 69.4 us -> 0 us
  waiting for transfers between devices: 72.9 us -> 10.9 us
  starting transfers between devices: 3.45 us -> 23 us
  between operations: 15.7 us -> 0.71 us
  Pallas kernels: 0 us -> 8.95 us
  other arithmetic: 7.99 us -> 0 us
  matrix products: 7.69 us -> 0 us
  local copies, waits for them, and re-layouts: 6.2 us -> 1.34 us
    all_gather x5 -> x0, blocking collectives: 69.4 us -> none  [the longest x1 16.6 us: local(): lax.all_gather(pack_grads, ('seq', 'tensor'), axis=0, tiled=True)]
    psum x1 -> x0, waiting for transfers between devices: 38.1 us -> none  [local(): lax.psum(term_gate, 'dp').astype(jnp.float32)]
    reduce_scatter x1 -> x0, waiting for transfers between devices: 28.1 us -> none  [local(): lax.psum_scatter(result + lax.dot_general(d_up, full_up, last_dims, prefe...]
    ppermute x0 -> x14, starting transfers between devices: none -> 23 us  [the longest x8 13.7 us: across(): return lax.ppermute(x, ('seq', 'dp', 'tensor'), pairs)]
    ppermute x0 -> x14, waiting for transfers between devices: none -> 10.9 us  [the longest x8 10.9 us: across(): return lax.ppermute(x, ('seq', 'dp', 'tensor'), pairs)]
    pallas_call x0 -> x7, Pallas kernels: none -> 8.95 us  [call(): pl.pallas_call(run, out_shape=outs, in_specs=[pl.BlockSpec(memory_space=p...]
    dot_general x9 -> x0, matrix products: 7.69 us -> none  [the longest x1 1.42 us: local(): lax.dot_general(act, dz, first_dims, preferred_element_type=jnp.float32)]
    all_to_all x1 -> x0, waiting for transfers between devices: 6.68 us -> none  [local(): lax.all_to_all(outgoing.reshape(seq_count * ten_count * each, half), ('se...]
  transfers between devices with their start and end apart: 3 -> 14, of which waited for: 3 -> 3; matrix products, arithmetic and copies ran while one was open for 4% -> 0% of each run, Pallas kernels for 0% -> 7%
where the time goes in v2:
time: 45.2 us; the launch traced here: 44.9 us
  starting transfers between devices  23 us (51%)
  waiting for transfers between devices  10.9 us (24%)
  Pallas kernels  8.95 us (20%)
  local copies, waits for them, and re-layouts  1.34 us (3%)
  between operations  0.71 us (2%)
    ppermute x8, starting transfers between devices, across(): return lax.ppermute(x, ('seq', 'dp', 'tensor'), pairs)  13.7 us
    ppermute x8, waiting for transfers between devices, across(): return lax.ppermute(x, ('seq', 'dp', 'tensor'), pairs)  10.9 us
    ppermute x6, starting transfers between devices, swap(): return lax.ppermute(x, axis, [(0, 1), (1, 0)])  9.24 us
    pallas_call x7, Pallas kernels, call(): pl.pallas_call(run, out_shape=outs, in_specs=[pl.BlockSpec(memory_space=p...  8.95 us
    unnamed x4, local copies, waits for them, and re-layouts  1.34 us
  transfers between devices with their start and end apart: 14, of which 3 were waited for; matrix products, arithmetic and copies ran while one was open for 0% of the time, Pallas kernels for 7%

profile of v2, /device:TPU:0, one launch (start us, length us, event | category | flops | bytes accessed | tf_op | source)
XLA Modules:
  0.0 44.9 jit_solution(1452891393313408750)
XLA Ops:
  0.6 3.3 %shard_map.102 = (bf16[64,1024]{1,0:T(8,128)(2,1)}, bf16[32,128]{1,0:T(8,128)(2,1)}, bf16[672,1024]{1,0:T(8,128)(2,1)}) custom-call(s32[1,64]{1,0:T(1,128)} %refs_0_.1, f32[1,64]{1,0:T(1,128)} %refs_1_.1, bf16[128,1024]{1,0:T(8,128)(2,1)} %bitcast.9, bf16[128,1024]{1,0:T(8,128)(2,1)} %bitcast.10, bf16[224,1024]{1,0:T(8,128)(2,1)} %bitcast.7, ...), custom_call_target="tpu_custom_call" | custom-call | bytes 3416576 | tf_op jit(solution)/shard_map/pallas_call | solution.py:29
  3.9 0.5 %collective-permute-start.2 = (bf16[672,1024]{1,0:T(8,128)(2,1)}, bf16[672,1024]{1,0:T(8,128)(2,1)S(1)}, u32[]{:S(2)}, u32[]{:S(2)}) collective-permute-start(bf16[672,1024]{1,0:T(8,128)(2,1)} %get-tuple-element.25.refs_2_.refs_3_), channel_id=1, source_target_pairs={{0,1},{1,0},{2,3},{3,2},{4,5},{5,4},{6,7},{7,6},{8,9},{9,8},{10,11... | collective-permute-start | bytes 4128776 | tf_op jit(solution)/shard_map/ppermute | solution.py:168
  4.5 2.6 %collective-permute-start.1 = (bf16[64,1024]{1,0:T(8,128)(2,1)}, bf16[64,1024]{1,0:T(8,128)(2,1)S(1)}, u32[]{:S(2)}, u32[]{:S(2)}) collective-permute-start(bf16[64,1024]{1,0:T(8,128)(2,1)} %get-tuple-element.24), channel_id=1, source_target_pairs={{0,4},{1,6},{4,0},{5,2},{8,12},{9,14},{12,8},{13,10},{2,5},{3,7},{... | collective-permute-start | bytes 393224 | tf_op jit(solution)/shard_map/ppermute | solution.py:165
  7.1 1.6 %collective-permute-start = (bf16[64,1024]{1,0:T(8,128)(2,1)}, bf16[64,1024]{1,0:T(8,128)(2,1)S(1)}, u32[]{:S(2)}, u32[]{:S(2)}) collective-permute-start(bf16[64,1024]{1,0:T(8,128)(2,1)} %get-tuple-element.24), channel_id=1, source_target_pairs={{0,0},{1,2},{4,4},{5,6},{8,8},{9,10},{12,12},{13,14},{2,1},{3,3},{... | collective-permute-start | bytes 393224 | tf_op jit(solution)/shard_map/ppermute | solution.py:165
  8.7 2.5 %collective-permute-start.6 = (bf16[64,1024]{1,0:T(8,128)(2,1)}, bf16[64,1024]{1,0:T(8,128)(2,1)S(1)}, u32[]{:S(2)}, u32[]{:S(2)}) collective-permute-start(bf16[64,1024]{1,0:T(8,128)(2,1)} %get-tuple-element.24), channel_id=1, source_target_pairs={{0,12},{1,14},{4,8},{5,10},{8,4},{9,6},{12,0},{13,2},{2,13},{3,15}... | collective-permute-start | bytes 393224 | tf_op jit(solution)/shard_map/ppermute | solution.py:165
  11.1 0.1 collective-permute-start.5
  11.2 0.0 collective-permute-done.1.refs_1_.refs_6_
  11.3 0.0 collective-permute-done.refs_0_.refs_5_
  11.3 0.0 collective-permute-done.2.refs_3_.refs_4_
  11.3 1.3 %copy-done = bf16[672,1024]{1,0:T(8,128)(2,1)S(1)} copy-done((bf16[672,1024]{1,0:T(8,128)(2,1)S(1)}, bf16[672,1024]{1,0:T(8,128)(2,1)}, u32[]{:S(2)}) %copy-start) | copy-done | bytes 1376280
  12.6 0.9 %shard_map.103 = (f32[672,128]{1,0:T(8,128)S(1)}, bf16[448,128]{1,0:T(8,128)(2,1)S(1)}, bf16[224,128]{1,0:T(8,128)(2,1)S(1)}) custom-call(bf16[64,1024]{1,0:T(8,128)(2,1)S(1)} %collective-permute-done.refs_0_.refs_5_, bf16[64,1024]{1,0:T(8,128)(2,1)S(1)} %collective-permute-done.1.refs_1_.refs_6_, bf16[672,1024]{1,0:T(8,128)(2,1)S(1)} %copy-done, ...), custom_call_target="tpu_custom_call" | custom-call | flops 176160768 | bytes 3530752 | tf_op jit(solution)/shard_map/pallas_call | solution.py:29
  13.5 3.9 %collective-permute-start.3 = (bf16[448,128]{1,0:T(8,128)(2,1)S(1)}, bf16[448,128]{1,0:T(8,128)(2,1)S(1)}, u32[]{:S(2)}, u32[]{:S(2)}) collective-permute-start(bf16[448,128]{1,0:T(8,128)(2,1)S(1)} %get-tuple-element.27), channel_id=1, source_target_pairs={{0,2},{2,0},{1,3},{3,1},{4,6},{6,4},{5,7},{7,5},{8,10},{10,8},{9,1... | collective-permute-start | bytes 344072 | tf_op jit(solution)/shard_map/ppermute | solution.py:168
  17.4 0.1 collective-permute-start.4
  17.5 0.0 collective-permute-done.6.refs_1_.refs_8_
  17.5 5.3 %collective-permute-done.5.refs_0_.refs_7_ = bf16[64,1024]{1,0:T(8,128)(2,1)S(1)} collective-permute-done((bf16[64,1024]{1,0:T(8,128)(2,1)}, bf16[64,1024]{1,0:T(8,128)(2,1)S(1)}, u32[]{:S(2)}, u32[]{:S(2)}) %collective-permute-start.5) | collective-permute-done | bytes 131104 | tf_op jit(solution)/shard_map/ppermute | solution.py:165
  22.9 0.0 collective-permute-done.4.refs_5_.refs_2_
  22.9 0.0 collective-permute-done.3.refs_4_.refs_1_
  22.9 0.9 %shard_map.104 = (f32[672,128]{1,0:T(8,128)S(1)}, bf16[672,128]{1,0:T(8,128)(2,1)S(1)}) custom-call(bf16[64,1024]{1,0:T(8,128)(2,1)S(1)} %collective-permute-done.5.refs_0_.refs_7_, bf16[64,1024]{1,0:T(8,128)(2,1)S(1)} %collective-permute-done.6.refs_1_.refs_8_, bf16[672,1024]{1,0:T(8,128)(2,1)S(1)} %copy-done, ...), custom_call_target="tpu_custom_call" | custom-call | flops 176160768 | bytes 3530752 | tf_op jit(solution)/shard_map/pallas_call | solution.py:29
  23.8 2.9 %collective-permute-start.9 = (bf16[672,128]{1,0:T(8,128)(2,1)S(1)}, bf16[672,128]{1,0:T(8,128)(2,1)S(1)}, u32[]{:S(2)}, u32[]{:S(2)}) collective-permute-start(bf16[672,128]{1,0:T(8,128)(2,1)S(1)} %get-tuple-element.32), channel_id=1, source_target_pairs={{0,2},{2,0},{1,3},{3,1},{4,6},{6,4},{5,7},{7,5},{8,10},{10,8},{9,1... | collective-permute-start | bytes 516104 | tf_op jit(solution)/shard_map/ppermute | solution.py:168
  26.7 0.5 %shard_map.105 = (bf16[672,128]{1,0:T(8,128)(2,1)S(1)}, bf16[32,1024]{1,0:T(8,128)(2,1)S(1)}, bf16[32,1024]{1,0:T(8,128)(2,1)S(1)}) custom-call(f32[672,128]{1,0:T(8,128)S(1)} %get-tuple-element.26.refs_0_, bf16[448,128]{1,0:T(8,128)(2,1)S(1)} %collective-permute-done.3.refs_4_.refs_1_, bf16[224,128]{1,0:T(8,128)(2,1)S(1)} %collective-permute-done.4.refs_5_.refs_2_, ...), custom_call_target="tpu_custom_call" | custom-call | flops 234881024 | bytes 3571712 | tf_op jit(solution)/shard_map/pallas_call | solution.py:29
  27.2 0.7 %collective-permute-start.7 = (bf16[32,1024]{1,0:T(8,128)(2,1)S(1)}, bf16[32,1024]{1,0:T(8,128)(2,1)S(1)}, u32[]{:S(2)}, u32[]{:S(2)}) collective-permute-start(bf16[32,1024]{1,0:T(8,128)(2,1)S(1)} %get-tuple-element.30), channel_id=1, source_target_pairs={{0,0},{1,2},{4,4},{5,6},{8,8},{9,10},{12,12},{13,14},{2,1},{3,3},{... | collective-permute-start | bytes 196616 | tf_op jit(solution)/shard_map/ppermute | solution.py:165
  27.9 1.6 %collective-permute-start.8 = (bf16[32,1024]{1,0:T(8,128)(2,1)S(1)}, bf16[32,1024]{1,0:T(8,128)(2,1)S(1)}, u32[]{:S(2)}, u32[]{:S(2)}) collective-permute-start(bf16[32,1024]{1,0:T(8,128)(2,1)S(1)} %get-tuple-element.31), channel_id=1, source_target_pairs={{0,4},{1,6},{4,0},{5,2},{8,12},{9,14},{12,8},{13,10},{2,5},{3,7},{... | collective-permute-start | bytes 196616 | tf_op jit(solution)/shard_map/ppermute | solution.py:165
  29.5 2.8 %collective-permute-done.8.refs_10_.refs_2_ = bf16[32,1024]{1,0:T(8,128)(2,1)S(1)} collective-permute-done((bf16[32,1024]{1,0:T(8,128)(2,1)S(1)}, bf16[32,1024]{1,0:T(8,128)(2,1)S(1)}, u32[]{:S(2)}, u32[]{:S(2)}) %collective-permute-start.8) | collective-permute-done | bytes 65568 | tf_op jit(solution)/shard_map/ppermute | solution.py:165
  32.3 0.5 %shard_map.106 = (bf16[672,256]{1,0:T(8,128)(2,1)S(1)}, bf16[256,1024]{1,0:T(8,128)(2,1)S(1)}, bf16[32,1024]{1,0:T(8,128)(2,1)S(1)}, bf16[32,1024]{1,0:T(8,128)(2,1)S(1)}) custom-call(f32[672,128]{1,0:T(8,128)S(1)} %get-tuple-element.29.refs_5_.refs_0_, bf16[672,128]{1,0:T(8,128)(2,1)S(1)} %collective-permute-done.9.refs_1_, bf16[672,1024]{1,0:T(8,128)(2,1)S(1)} %copy-done, ...), custom_call_target="tpu_custom_call" | custom-call | flops 234881024 | bytes 4964352 | tf_op jit(solution)/shard_map/pallas_call | solution.py:29
  32.8 1.8 %collective-permute-start.12 = (bf16[256,1024]{1,0:T(8,128)(2,1)S(1)}, bf16[256,1024]{1,0:T(8,128)(2,1)S(1)}, u32[]{:S(2)}, u32[]{:S(2)}) collective-permute-start(bf16[256,1024]{1,0:T(8,128)(2,1)S(1)} %get-tuple-element.36.refs_0_), channel_id=1, source_target_pairs={{0,1},{1,0},{2,3},{3,2},{4,5},{5,4},{6,7},{7,6},{8,9},{9,8},{10,11... | collective-permute-start | bytes 1572872 | tf_op jit(solution)/shard_map/ppermute | solution.py:168
  34.6 0.1 collective-permute-start.13
  34.6 2.7 %collective-permute-start.10 = (bf16[32,1024]{1,0:T(8,128)(2,1)S(1)}, bf16[32,1024]{1,0:T(8,128)(2,1)S(1)}, u32[]{:S(2)}, u32[]{:S(2)}) collective-permute-start(bf16[32,1024]{1,0:T(8,128)(2,1)S(1)} %get-tuple-element.34), channel_id=1, source_target_pairs={{0,8},{1,10},{4,12},{5,14},{8,0},{9,2},{12,4},{13,6},{2,9},{3,11},... | collective-permute-start | bytes 196616 | tf_op jit(solution)/shard_map/ppermute | solution.py:165
  37.3 2.0 %collective-permute-start.11 = (bf16[32,1024]{1,0:T(8,128)(2,1)S(1)}, bf16[32,1024]{1,0:T(8,128)(2,1)S(1)}, u32[]{:S(2)}, u32[]{:S(2)}) collective-permute-start(bf16[32,1024]{1,0:T(8,128)(2,1)S(1)} %get-tuple-element.35), channel_id=1, source_target_pairs={{0,12},{1,14},{4,8},{5,10},{8,4},{9,6},{12,0},{13,2},{2,13},{3,15}... | collective-permute-start | bytes 196616 | tf_op jit(solution)/shard_map/ppermute | solution.py:165
  39.4 1.8 %shard_map.107 = (bf16[224,1024]{1,0:T(8,128)(2,1)}, bf16[224,1024]{1,0:T(8,128)(2,1)}, bf16[224,1024]{1,0:T(8,128)(2,1)}, f32[8,128]{1,0:T(8,128)S(1)}) custom-call(bf16[256,1024]{1,0:T(8,128)(2,1)S(1)} %get-tuple-element.36.refs_0_, bf16[256,1024]{1,0:T(8,128)(2,1)S(1)} %collective-permute-done.12.refs_1_, bf16[672,256]{1,0:T(8,128)(2,1)S(1)} %get-tuple-element.37.refs_2_, ...), custom_call_target="tpu_custom_call" | custom-call | flops 352321536 | bytes 3117056 | tf_op jit(solution)/shard_map/pallas_call | solution.py:29
  41.2 0.0 collective-permute-done.10.refs_3_
  41.2 2.8 %collective-permute-done.11.refs_4_ = bf16[32,1024]{1,0:T(8,128)(2,1)S(1)} collective-permute-done((bf16[32,1024]{1,0:T(8,128)(2,1)S(1)}, bf16[32,1024]{1,0:T(8,128)(2,1)S(1)}, u32[]{:S(2)}, u32[]{:S(2)}) %collective-permute-start.11) | collective-permute-done | bytes 65568 | tf_op jit(solution)/shard_map/ppermute | solution.py:165
  43.9 1.0 %shard_map.108 = bf16[128,1024]{1,0:T(8,128)(2,1)} custom-call(bf16[32,128]{1,0:T(8,128)(2,1)S(1)} %copy-done.1, bf16[32,1024]{1,0:T(8,128)(2,1)S(1)} %collective-permute-done.7.refs_9_.refs_1_, bf16[32,1024]{1,0:T(8,128)(2,1)S(1)} %collective-permute-done.8.refs_10_.refs_2_, bf16[32,1024]{1,0:T(8,128)(2,1)S(1)} %collective-permute-done.10.refs_3_, ...), custom_call_target="tpu_custom_call" | custom-call | bytes 532480 | tf_op jit(solution)/shard_map/pallas_call | solution.py:29
  (7 shorter events, 0.0 us)
Async XLA Ops:
  3.9 7.3 %collective-permute-start.2 = (bf16[672,1024]{1,0:T(8,128)(2,1)}, bf16[672,1024]{1,0:T(8,128)(2,1)S(1)}, u32[]{:S(2)}, u32[]{:S(2)}) collective-permute-start(bf16[672,1024]{1,0:T(8,128)(2,1)} %get-tuple-element.25.refs_2_.refs_3_), channel_id=1, source_target_pairs={{0,1},{1,0},{2,3},{3,2},{4,5},{5,4},{6,7},{7,6},{8,9},{9,8},{10,11... | collective-permute-start | bytes 4128776 | tf_op jit(solution)/shard_map/ppermute | solution.py:168
  4.5 6.8 %collective-permute-start.1 = (bf16[64,1024]{1,0:T(8,128)(2,1)}, bf16[64,1024]{1,0:T(8,128)(2,1)S(1)}, u32[]{:S(2)}, u32[]{:S(2)}) collective-permute-start(bf16[64,1024]{1,0:T(8,128)(2,1)} %get-tuple-element.24), channel_id=1, source_target_pairs={{0,4},{1,6},{4,0},{5,2},{8,12},{9,14},{12,8},{13,10},{2,5},{3,7},{... | collective-permute-start | bytes 393224 | tf_op jit(solution)/shard_map/ppermute | solution.py:165
  7.1 4.2 %collective-permute-start = (bf16[64,1024]{1,0:T(8,128)(2,1)}, bf16[64,1024]{1,0:T(8,128)(2,1)S(1)}, u32[]{:S(2)}, u32[]{:S(2)}) collective-permute-start(bf16[64,1024]{1,0:T(8,128)(2,1)} %get-tuple-element.24), channel_id=1, source_target_pairs={{0,0},{1,2},{4,4},{5,6},{8,8},{9,10},{12,12},{13,14},{2,1},{3,3},{... | collective-permute-start | bytes 393224 | tf_op jit(solution)/shard_map/ppermute | solution.py:165
  8.7 8.9 %collective-permute-start.6 = (bf16[64,1024]{1,0:T(8,128)(2,1)}, bf16[64,1024]{1,0:T(8,128)(2,1)S(1)}, u32[]{:S(2)}, u32[]{:S(2)}) collective-permute-start(bf16[64,1024]{1,0:T(8,128)(2,1)} %get-tuple-element.24), channel_id=1, source_target_pairs={{0,12},{1,14},{4,8},{5,10},{8,4},{9,6},{12,0},{13,2},{2,13},{3,15}... | collective-permute-start | bytes 393224 | tf_op jit(solution)/shard_map/ppermute | solution.py:165
  11.1 11.7 %collective-permute-start.5 = (bf16[64,1024]{1,0:T(8,128)(2,1)}, bf16[64,1024]{1,0:T(8,128)(2,1)S(1)}, u32[]{:S(2)}, u32[]{:S(2)}) collective-permute-start(bf16[64,1024]{1,0:T(8,128)(2,1)} %get-tuple-element.24), channel_id=1, source_target_pairs={{0,8},{1,10},{4,12},{5,14},{8,0},{9,2},{12,4},{13,6},{2,9},{3,11},... | collective-permute-start | bytes 393224 | tf_op jit(solution)/shard_map/ppermute | solution.py:165
  11.3 1.3 %copy-start = (bf16[672,1024]{1,0:T(8,128)(2,1)S(1)}, bf16[672,1024]{1,0:T(8,128)(2,1)}, u32[]{:S(2)}) copy-start(bf16[672,1024]{1,0:T(8,128)(2,1)} %get-tuple-element.25.refs_2_.refs_3_) | copy-start | bytes 4128772
  13.5 9.3 %collective-permute-start.3 = (bf16[448,128]{1,0:T(8,128)(2,1)S(1)}, bf16[448,128]{1,0:T(8,128)(2,1)S(1)}, u32[]{:S(2)}, u32[]{:S(2)}) collective-permute-start(bf16[448,128]{1,0:T(8,128)(2,1)S(1)} %get-tuple-element.27), channel_id=1, source_target_pairs={{0,2},{2,0},{1,3},{3,1},{4,6},{6,4},{5,7},{7,5},{8,10},{10,8},{9,1... | collective-permute-start | bytes 344072 | tf_op jit(solution)/shard_map/ppermute | solution.py:168
  17.4 5.4 %collective-permute-start.4 = (bf16[224,128]{1,0:T(8,128)(2,1)S(1)}, bf16[224,128]{1,0:T(8,128)(2,1)S(1)}, u32[]{:S(2)}, u32[]{:S(2)}) collective-permute-start(bf16[224,128]{1,0:T(8,128)(2,1)S(1)} %get-tuple-element.28), channel_id=1, source_target_pairs={{0,2},{2,0},{1,3},{3,1},{4,6},{6,4},{5,7},{7,5},{8,10},{10,8},{9,1... | collective-permute-start | bytes 172040 | tf_op jit(solution)/shard_map/ppermute | solution.py:168
  23.8 8.5 %collective-permute-start.9 = (bf16[672,128]{1,0:T(8,128)(2,1)S(1)}, bf16[672,128]{1,0:T(8,128)(2,1)S(1)}, u32[]{:S(2)}, u32[]{:S(2)}) collective-permute-start(bf16[672,128]{1,0:T(8,128)(2,1)S(1)} %get-tuple-element.32), channel_id=1, source_target_pairs={{0,2},{2,0},{1,3},{3,1},{4,6},{6,4},{5,7},{7,5},{8,10},{10,8},{9,1... | collective-permute-start | bytes 516104 | tf_op jit(solution)/shard_map/ppermute | solution.py:168
  27.2 2.2 %collective-permute-start.7 = (bf16[32,1024]{1,0:T(8,128)(2,1)S(1)}, bf16[32,1024]{1,0:T(8,128)(2,1)S(1)}, u32[]{:S(2)}, u32[]{:S(2)}) collective-permute-start(bf16[32,1024]{1,0:T(8,128)(2,1)S(1)} %get-tuple-element.30), channel_id=1, source_target_pairs={{0,0},{1,2},{4,4},{5,6},{8,8},{9,10},{12,12},{13,14},{2,1},{3,3},{... | collective-permute-start | bytes 196616 | tf_op jit(solution)/shard_map/ppermute | solution.py:165
  27.9 4.3 %collective-permute-start.8 = (bf16[32,1024]{1,0:T(8,128)(2,1)S(1)}, bf16[32,1024]{1,0:T(8,128)(2,1)S(1)}, u32[]{:S(2)}, u32[]{:S(2)}) collective-permute-start(bf16[32,1024]{1,0:T(8,128)(2,1)S(1)} %get-tuple-element.31), channel_id=1, source_target_pairs={{0,4},{1,6},{4,0},{5,2},{8,12},{9,14},{12,8},{13,10},{2,5},{3,7},{... | collective-permute-start | bytes 196616 | tf_op jit(solution)/shard_map/ppermute | solution.py:165
  32.8 11.1 %copy-start.1 = (bf16[32,128]{1,0:T(8,128)(2,1)S(1)}, bf16[32,128]{1,0:T(8,128)(2,1)}, u32[]{:S(2)}) copy-start(bf16[32,128]{1,0:T(8,128)(2,1)} %get-tuple-element.23.refs_0_) | copy-start | bytes 24580
  32.8 6.6 %collective-permute-start.12 = (bf16[256,1024]{1,0:T(8,128)(2,1)S(1)}, bf16[256,1024]{1,0:T(8,128)(2,1)S(1)}, u32[]{:S(2)}, u32[]{:S(2)}) collective-permute-start(bf16[256,1024]{1,0:T(8,128)(2,1)S(1)} %get-tuple-element.36.refs_0_), channel_id=1, source_target_pairs={{0,1},{1,0},{2,3},{3,2},{4,5},{5,4},{6,7},{7,6},{8,9},{9,8},{10,11... | collective-permute-start | bytes 1572872 | tf_op jit(solution)/shard_map/ppermute | solution.py:168
  34.6 4.8 %collective-permute-start.13 = (bf16[672,256]{1,0:T(8,128)(2,1)S(1)}, bf16[672,256]{1,0:T(8,128)(2,1)S(1)}, u32[]{:S(2)}, u32[]{:S(2)}) collective-permute-start(bf16[672,256]{1,0:T(8,128)(2,1)S(1)} %get-tuple-element.37.refs_2_), channel_id=1, source_target_pairs={{0,1},{1,0},{2,3},{3,2},{4,5},{5,4},{6,7},{7,6},{8,9},{9,8},{10,11... | collective-permute-start | bytes 1032200 | tf_op jit(solution)/shard_map/ppermute | solution.py:168
  34.6 6.5 %collective-permute-start.10 = (bf16[32,1024]{1,0:T(8,128)(2,1)S(1)}, bf16[32,1024]{1,0:T(8,128)(2,1)S(1)}, u32[]{:S(2)}, u32[]{:S(2)}) collective-permute-start(bf16[32,1024]{1,0:T(8,128)(2,1)S(1)} %get-tuple-element.34), channel_id=1, source_target_pairs={{0,8},{1,10},{4,12},{5,14},{8,0},{9,2},{12,4},{13,6},{2,9},{3,11},... | collective-permute-start | bytes 196616 | tf_op jit(solution)/shard_map/ppermute | solution.py:165
  37.3 6.6 %collective-permute-start.11 = (bf16[32,1024]{1,0:T(8,128)(2,1)S(1)}, bf16[32,1024]{1,0:T(8,128)(2,1)S(1)}, u32[]{:S(2)}, u32[]{:S(2)}) collective-permute-start(bf16[32,1024]{1,0:T(8,128)(2,1)S(1)} %get-tuple-element.35), channel_id=1, source_target_pairs={{0,12},{1,14},{4,8},{5,10},{8,4},{9,6},{12,0},{13,2},{2,13},{3,15}... | collective-permute-start | bytes 196616 | tf_op jit(solution)/shard_map/ppermute | solution.py:165

commit v3 on v2

--- a/solution.py
+++ b/solution.py
@@ -116,10 +116,13 @@
 
 
 def second_body(blocks, keep, recv, w_own, w_oth, dd_a, *refs):
+    early, refs = refs[: blocks // 2], refs[blocks // 2 :]
     dd_ref, rows_ref, *dx_refs = refs[blocks:]
     m = dd_a.shape[1]
     terms(keep, [recv], dd_ref.at[:, m:])
-    back_rows(dd_ref.at[:, m:], w_own, w_oth, dx_refs)
+    back_rows(dd_ref.at[:, m:], w_own, w_oth, dx_refs[len(early) :])
+    for a, ref in zip(early, dx_refs):
+        ref[...] = a[...]
     dd_ref[:, 0:m] = dd_a[...]
     for s, block in enumerate(refs[:blocks]):
         rows_ref[s * MOST : (s + 1) * MOST] = block[0:MOST]
@@ -175,7 +178,8 @@
         scratch=[pltpu.VMEM((1, cap), jnp.int32), pltpu.VMEM((1, cap), F32), pltpu.VMEM((tok_dev, half), BF),
                  pltpu.VMEM((tok_dev, half), BF), pltpu.VMEM((3 * h, half), BF), pltpu.SemaphoreType.DMA((8,))],
     )
-    blocks = {s: across(xd, s) for s in range(n)}
+    blocks = {s: across(xd, s) for s in (2, 1, 0)}
+    blocks[3] = lax.ppermute(blocks[2], "seq", [(k, k ^ 1) for k in range(n)])
     w_oth = swap(w_own, "tensor")
     flops = 2 * m * half * h
 
@@ -187,26 +191,25 @@
         )
         return keep, [swap(b, "dp") for b in send]
 
-    near, far = range(n // 2), range(n // 2, n)
+    near, far = (0, 1), (2, 3)
     dx = [arr((MOST, half))] * (n // 2)
-    keep_a, recv_a = partial(near, (2, 1))
-    keep_b, recv_b = partial(far, (3,), after=recv_a)
+    keep_a, recv_a = partial(near, (3,))
+    keep_b, recv_b = partial(far, (3,))
     dd_a, *dx_a = call(
         functools.partial(first_body, len(recv_a)), [arr((3 * h, 2 * m))] + dx,
         keep_a, *recv_a, w_own, w_oth, flops=8 * flops, after=(keep_b,),
     )
-    back = [across(b, s) for s, b in zip(near, dx_a)]
-    own, rows_own, *dx_b = call(
-        functools.partial(second_body, n), [arr((3 * h, 4 * m)), arr((2 * n * MOST, half))] + dx,
-        keep_b, *recv_b, w_own, w_oth, dd_a, *(blocks[s] for s in range(n)), flops=8 * flops, after=back,
-    )
-    back += [across(b, s) for s, b in zip(far, dx_b)]
+    own, rows_own, *dx = call(
+        functools.partial(second_body, n), [arr((3 * h, 4 * m)), arr((2 * n * MOST, half))] + dx * 2,
+        keep_b, *recv_b, w_own, w_oth, dd_a, *dx_a, *(blocks[s] for s in (*near, *far)), flops=8 * flops,
+    )
+    back = {s: across(b, s) for s, b in zip((*near, *far), dx)}
     rows_oth, oth = swap(rows_own, "tensor"), swap(own, "tensor")
     grads = call(
         functools.partial(weights_body, coeff), [arr((h, half))] * 3 + [arr((8, 128), F32)],
         rows_own, rows_oth, own, oth, flops=12 * flops,
     )
-    (grad_local,) = call(spread_body, [arr((tok_dev, half))], sel, *back, after=grads[3:])
+    (grad_local,) = call(spread_body, [arr((tok_dev, half))], sel, *(back[s] for s in (2, 3, 1, 0)), after=grads[3:])
     return grad_local[None], grads[0].T, grads[1].T, grads[2]
 
 

time: 45.2 us -> 41.9 us (0.927)
  starting transfers between devices: 23 us -> 17 us
  waiting for transfers between devices: 10.9 us -> 13.7 us
    ppermute x6 -> x5, waiting for transfers between devices: 0.02 us -> 6.36 us  [swap(): return lax.ppermute(x, axis, [(0, 1), (1, 0)])]
    ppermute x6 -> x5, starting transfers between devices: 9.24 us -> 4.43 us  [swap(): return lax.ppermute(x, axis, [(0, 1), (1, 0)])]
    ppermute x8 -> x7, waiting for transfers between devices: 10.9 us -> 7.33 us  [across(): return lax.ppermute(x, ('seq', 'dp', 'tensor'), pairs)]
    ppermute x8 -> x7, starting transfers between devices: 13.7 us -> 10.9 us  [across(): return lax.ppermute(x, ('seq', 'dp', 'tensor'), pairs)]
    ppermute x0 -> x1, starting transfers between devices: none -> 1.61 us  [swapped(): blocks[3] = lax.ppermute(blocks[2], 'seq', [(k, k ^ 1) for k in range(n)])]
  transfers between devices with their start and end apart: 14 -> 13, of which waited for: 3 -> 6; matrix products, arithmetic and copies ran while one was open for 0% -> 0% of each run, Pallas kernels for 7% -> 10%
where the time goes in v3:
time: 41.9 us; the launch traced here: 41.7 us
  starting transfers between devices  17 us (41%)
  waiting for transfers between devices  13.7 us (33%)
  Pallas kernels  8.95 us (21%)
  local copies, waits for them, and re-layouts  1.34 us (3%)
  between operations  0.72 us (2%)
    ppermute x7, starting transfers between devices, across(): return lax.ppermute(x, ('seq', 'dp', 'tensor'), pairs)  10.9 us
    pallas_call x7, Pallas kernels, call(): pl.pallas_call(run, out_shape=outs, in_specs=[pl.BlockSpec(memory_space=p...  8.95 us
    ppermute x7, waiting for transfers between devices, across(): return lax.ppermute(x, ('seq', 'dp', 'tensor'), pairs)  7.33 us
    ppermute x5, waiting for transfers between devices, swap(): return lax.ppermute(x, axis, [(0, 1), (1, 0)])  6.36 us
    ppermute x5, starting transfers between devices, swap(): return lax.ppermute(x, axis, [(0, 1), (1, 0)])  4.43 us
    ppermute x1, starting transfers between devices, swapped(): blocks[3] = lax.ppermute(blocks[2], 'seq', [(k, k ^ 1) for k in range(n)])  1.61 us
    unnamed x4, local copies, waits for them, and re-layouts  1.34 us
  transfers between devices with their start and end apart: 13, of which 6 were waited for; matrix products, arithmetic and copies ran while one was open for 0% of the time, Pallas kernels for 10%

profile of v3, /device:TPU:0, one launch (start us, length us, event | category | flops | bytes accessed | tf_op | source)
XLA Modules:
  0.0 41.7 jit_solution(7535145959463594471)
XLA Ops:
  0.6 3.3 %shard_map.102 = (bf16[64,1024]{1,0:T(8,128)(2,1)}, bf16[32,128]{1,0:T(8,128)(2,1)}, bf16[672,1024]{1,0:T(8,128)(2,1)}) custom-call(s32[1,64]{1,0:T(1,128)} %refs_0_.1, f32[1,64]{1,0:T(1,128)} %refs_1_.1, bf16[128,1024]{1,0:T(8,128)(2,1)} %bitcast.9, bf16[128,1024]{1,0:T(8,128)(2,1)} %bitcast.10, bf16[224,1024]{1,0:T(8,128)(2,1)} %bitcast.7, ...), custom_call_target="tpu_custom_call" | custom-call | bytes 3416576 | tf_op jit(solution)/shard_map/pallas_call | solution.py:29
  3.9 0.5 %collective-permute-start.2 = (bf16[672,1024]{1,0:T(8,128)(2,1)}, bf16[672,1024]{1,0:T(8,128)(2,1)S(1)}, u32[]{:S(2)}, u32[]{:S(2)}) collective-permute-start(bf16[672,1024]{1,0:T(8,128)(2,1)} %get-tuple-element.26.refs_2_), channel_id=1, source_target_pairs={{0,1},{1,0},{2,3},{3,2},{4,5},{5,4},{6,7},{7,6},{8,9},{9,8},{10,11... | collective-permute-start | bytes 4128776 | tf_op jit(solution)/shard_map/ppermute | solution.py:171
  4.5 3.7 %collective-permute-start = (bf16[64,1024]{1,0:T(8,128)(2,1)}, bf16[64,1024]{1,0:T(8,128)(2,1)S(1)}, u32[]{:S(2)}, u32[]{:S(2)}) collective-permute-start(bf16[64,1024]{1,0:T(8,128)(2,1)} %get-tuple-element.25), channel_id=1, source_target_pairs={{0,8},{1,10},{4,12},{5,14},{8,0},{9,2},{12,4},{13,6},{2,9},{3,11},... | collective-permute-start | bytes 393224 | tf_op jit(solution)/shard_map/ppermute | solution.py:168
  8.1 1.6 %collective-permute-start.5 = (bf16[64,1024]{1,0:T(8,128)(2,1)}, bf16[64,1024]{1,0:T(8,128)(2,1)S(1)}, u32[]{:S(2)}, u32[]{:S(2)}) collective-permute-start(bf16[64,1024]{1,0:T(8,128)(2,1)} %get-tuple-element.25), channel_id=1, source_target_pairs={{0,4},{1,6},{4,0},{5,2},{8,12},{9,14},{12,8},{13,10},{2,5},{3,7},{... | collective-permute-start | bytes 393224 | tf_op jit(solution)/shard_map/ppermute | solution.py:168
  9.7 1.6 %collective-permute-start.4 = (bf16[64,1024]{1,0:T(8,128)(2,1)}, bf16[64,1024]{1,0:T(8,128)(2,1)S(1)}, u32[]{:S(2)}, u32[]{:S(2)}) collective-permute-start(bf16[64,1024]{1,0:T(8,128)(2,1)} %get-tuple-element.25), channel_id=1, source_target_pairs={{0,0},{1,2},{4,4},{5,6},{8,8},{9,10},{12,12},{13,14},{2,1},{3,3},{... | collective-permute-start | bytes 393224 | tf_op jit(solution)/shard_map/ppermute | solution.py:168
  11.2 3.7 %collective-permute-done.refs_0_.refs_9_ = bf16[64,1024]{1,0:T(8,128)(2,1)S(1)} collective-permute-done((bf16[64,1024]{1,0:T(8,128)(2,1)}, bf16[64,1024]{1,0:T(8,128)(2,1)S(1)}, u32[]{:S(2)}, u32[]{:S(2)}) %collective-permute-start) | collective-permute-done | bytes 131104 | tf_op jit(solution)/shard_map/ppermute | solution.py:168
  14.9 1.6 %collective-permute-start.1 = (bf16[64,1024]{1,0:T(8,128)(2,1)S(1)}, bf16[64,1024]{1,0:T(8,128)(2,1)S(1)}, u32[]{:S(2)}, u32[]{:S(2)}) collective-permute-start(bf16[64,1024]{1,0:T(8,128)(2,1)S(1)} %collective-permute-done.refs_0_.refs_9_), channel_id=1, source_target_pairs={{0,4},{4,0},{8,12},{12,8},{1,5},{5,1},{9,13},{13,9},{2,6},{6,2},{1... | collective-permute-start | bytes 393224 | tf_op jit(solution)/shard_map/ppermute | solution.py:182
  16.6 0.0 collective-permute-done.5.refs_1_.refs_8_
  16.6 0.0 collective-permute-done.4.refs_0_.refs_7_
  16.6 0.0 collective-permute-done.2.refs_3_
  16.6 1.3 %copy-done = bf16[672,1024]{1,0:T(8,128)(2,1)S(1)} copy-done((bf16[672,1024]{1,0:T(8,128)(2,1)S(1)}, bf16[672,1024]{1,0:T(8,128)(2,1)}, u32[]{:S(2)}) %copy-start) | copy-done | bytes 1376280
  17.9 0.9 %shard_map.104 = (f32[672,128]{1,0:T(8,128)S(1)}, bf16[672,128]{1,0:T(8,128)(2,1)S(1)}) custom-call(bf16[64,1024]{1,0:T(8,128)(2,1)S(1)} %collective-permute-done.4.refs_0_.refs_7_, bf16[64,1024]{1,0:T(8,128)(2,1)S(1)} %collective-permute-done.5.refs_1_.refs_8_, bf16[672,1024]{1,0:T(8,128)(2,1)S(1)} %copy-done, ...), custom_call_target="tpu_custom_call" | custom-call | flops 176160768 | bytes 3530752 | tf_op jit(solution)/shard_map/pallas_call | solution.py:29
  18.8 2.3 %collective-permute-start.6 = (bf16[672,128]{1,0:T(8,128)(2,1)S(1)}, bf16[672,128]{1,0:T(8,128)(2,1)S(1)}, u32[]{:S(2)}, u32[]{:S(2)}) collective-permute-start(bf16[672,128]{1,0:T(8,128)(2,1)S(1)} %get-tuple-element.30), channel_id=1, source_target_pairs={{0,2},{2,0},{1,3},{3,1},{4,6},{6,4},{5,7},{7,5},{8,10},{10,8},{9,1... | collective-permute-start | bytes 516104 | tf_op jit(solution)/shard_map/ppermute | solution.py:171
  21.2 0.0 collective-permute-done.1.refs_1_.refs_10_
  21.2 0.9 %shard_map.103 = (f32[672,128]{1,0:T(8,128)S(1)}, bf16[672,128]{1,0:T(8,128)(2,1)S(1)}) custom-call(bf16[64,1024]{1,0:T(8,128)(2,1)S(1)} %collective-permute-done.refs_0_.refs_9_, bf16[64,1024]{1,0:T(8,128)(2,1)S(1)} %collective-permute-done.1.refs_1_.refs_10_, bf16[672,1024]{1,0:T(8,128)(2,1)S(1)} %copy-done, ...), custom_call_target="tpu_custom_call" | custom-call | flops 176160768 | bytes 3530752 | tf_op jit(solution)/shard_map/pallas_call | solution.py:29
  22.1 1.0 %collective-permute-start.3 = (bf16[672,128]{1,0:T(8,128)(2,1)S(1)}, bf16[672,128]{1,0:T(8,128)(2,1)S(1)}, u32[]{:S(2)}, u32[]{:S(2)}) collective-permute-start(bf16[672,128]{1,0:T(8,128)(2,1)S(1)} %get-tuple-element.28), channel_id=1, source_target_pairs={{0,2},{2,0},{1,3},{3,1},{4,6},{6,4},{5,7},{7,5},{8,10},{10,8},{9,1... | collective-permute-start | bytes 516104 | tf_op jit(solution)/shard_map/ppermute | solution.py:171
  23.1 3.3 %collective-permute-done.6.refs_1_ = bf16[672,128]{1,0:T(8,128)(2,1)S(1)} collective-permute-done((bf16[672,128]{1,0:T(8,128)(2,1)S(1)}, bf16[672,128]{1,0:T(8,128)(2,1)S(1)}, u32[]{:S(2)}, u32[]{:S(2)}) %collective-permute-start.6) | collective-permute-done | bytes 172064 | tf_op jit(solution)/shard_map/ppermute | solution.py:171
  26.4 0.5 %shard_map.105 = (bf16[672,128]{1,0:T(8,128)(2,1)S(1)}, bf16[32,1024]{1,0:T(8,128)(2,1)S(1)}, bf16[32,1024]{1,0:T(8,128)(2,1)S(1)}) custom-call(f32[672,128]{1,0:T(8,128)S(1)} %get-tuple-element.29.refs_0_, bf16[672,128]{1,0:T(8,128)(2,1)S(1)} %collective-permute-done.6.refs_1_, bf16[672,1024]{1,0:T(8,128)(2,1)S(1)} %copy-done, ...), custom_call_target="tpu_custom_call" | custom-call | flops 234881024 | bytes 3571712 | tf_op jit(solution)/shard_map/pallas_call | solution.py:29
  26.9 3.1 %collective-permute-done.3.refs_1_ = bf16[672,128]{1,0:T(8,128)(2,1)S(1)} collective-permute-done((bf16[672,128]{1,0:T(8,128)(2,1)S(1)}, bf16[672,128]{1,0:T(8,128)(2,1)S(1)}, u32[]{:S(2)}, u32[]{:S(2)}) %collective-permute-start.3) | collective-permute-done | bytes 172064 | tf_op jit(solution)/shard_map/ppermute | solution.py:171
  30.0 0.6 %shard_map.106 = (bf16[672,256]{1,0:T(8,128)(2,1)S(1)}, bf16[256,1024]{1,0:T(8,128)(2,1)S(1)}, bf16[32,1024]{1,0:T(8,128)(2,1)S(1)}, bf16[32,1024]{1,0:T(8,128)(...) custom-call(f32[672,128]{1,0:T(8,128)S(1)} %get-tuple-element.27.refs_4_.refs_0_, ...), custom_call_target="tpu_custom_call" | custom-call | flops 234881024 | bytes 5226496 | tf_op jit(solution)/shard_map/pallas_call | solution.py:29
  30.6 0.1 collective-permute-start.11
  30.7 0.5 %collective-permute-start.12 = (bf16[672,256]{1,0:T(8,128)(2,1)S(1)}, bf16[672,256]{1,0:T(8,128)(2,1)S(1)}, u32[]{:S(2)}, u32[]{:S(2)}) collective-permute-start(bf16[672,256]{1,0:T(8,128)(2,1)S(1)} %get-tuple-element.39.refs_2_), channel_id=1, source_target_pairs={{0,1},{1,0},{2,3},{3,2},{4,5},{5,4},{6,7},{7,6},{8,9},{9,8},{10,11... | collective-permute-start | bytes 1032200 | tf_op jit(solution)/shard_map/ppermute | solution.py:171
  31.2 2.1 %collective-permute-start.7 = (bf16[32,1024]{1,0:T(8,128)(2,1)S(1)}, bf16[32,1024]{1,0:T(8,128)(2,1)S(1)}, u32[]{:S(2)}, u32[]{:S(2)}) collective-permute-start(bf16[32,1024]{1,0:T(8,128)(2,1)S(1)} %get-tuple-element.34), channel_id=1, source_target_pairs={{0,8},{1,10},{4,12},{5,14},{8,0},{9,2},{12,4},{13,6},{2,9},{3,11},... | collective-permute-start | bytes 196616 | tf_op jit(solution)/shard_map/ppermute | solution.py:168
  33.3 1.2 %collective-permute-start.8 = (bf16[32,1024]{1,0:T(8,128)(2,1)S(1)}, bf16[32,1024]{1,0:T(8,128)(2,1)S(1)}, u32[]{:S(2)}, u32[]{:S(2)}) collective-permute-start(bf16[32,1024]{1,0:T(8,128)(2,1)S(1)} %get-tuple-element.35), channel_id=1, source_target_pairs={{0,12},{1,14},{4,8},{5,10},{8,4},{9,6},{12,0},{13,2},{2,13},{3,15}... | collective-permute-start | bytes 196616 | tf_op jit(solution)/shard_map/ppermute | solution.py:168
  34.5 0.2 collective-permute-start.9
  34.7 0.7 %collective-permute-start.10 = (bf16[32,1024]{1,0:T(8,128)(2,1)S(1)}, bf16[32,1024]{1,0:T(8,128)(2,1)S(1)}, u32[]{:S(2)}, u32[]{:S(2)}) collective-permute-start(bf16[32,1024]{1,0:T(8,128)(2,1)S(1)} %get-tuple-element.37), channel_id=1, source_target_pairs={{0,0},{1,2},{4,4},{5,6},{8,8},{9,10},{12,12},{13,14},{2,1},{3,3},{... | collective-permute-start | bytes 196616 | tf_op jit(solution)/shard_map/ppermute | solution.py:168
  35.3 0.0 collective-permute-done.11.refs_1_
  35.3 1.8 %shard_map.107 = (bf16[224,1024]{1,0:T(8,128)(2,1)}, bf16[224,1024]{1,0:T(8,128)(2,1)}, bf16[224,1024]{1,0:T(8,128)(2,1)}, f32[8,128]{1,0:T(8,128)S(1)}) custom-call(bf16[256,1024]{1,0:T(8,128)(2,1)S(1)} %get-tuple-element.38.refs_0_, bf16[256,1024]{1,0:T(8,128)(2,1)S(1)} %collective-permute-done.11.refs_1_, bf16[672,256]{1,0:T(8,128)(2,1)S(1)} %get-tuple-element.39.refs_2_, ...), custom_call_target="tpu_custom_call" | custom-call | flops 352321536 | bytes 3117056 | tf_op jit(solution)/shard_map/pallas_call | solution.py:29
  37.1 0.9 %collective-permute-done.7.refs_1_ = bf16[32,1024]{1,0:T(8,128)(2,1)S(1)} collective-permute-done((bf16[32,1024]{1,0:T(8,128)(2,1)S(1)}, bf16[32,1024]{1,0:T(8,128)(2,1)S(1)}, u32[]{:S(2)}, u32[]{:S(2)}) %collective-permute-start.7) | collective-permute-done | bytes 65568 | tf_op jit(solution)/shard_map/ppermute | solution.py:168
  38.0 2.1 %collective-permute-done.8.refs_2_ = bf16[32,1024]{1,0:T(8,128)(2,1)S(1)} collective-permute-done((bf16[32,1024]{1,0:T(8,128)(2,1)S(1)}, bf16[32,1024]{1,0:T(8,128)(2,1)S(1)}, u32[]{:S(2)}, u32[]{:S(2)}) %collective-permute-start.8) | collective-permute-done | bytes 65568 | tf_op jit(solution)/shard_map/ppermute | solution.py:168
  40.1 0.6 %collective-permute-done.9.refs_3_ = bf16[32,1024]{1,0:T(8,128)(2,1)S(1)} collective-permute-done((bf16[32,1024]{1,0:T(8,128)(2,1)S(1)}, bf16[32,1024]{1,0:T(8,128)(2,1)S(1)}, u32[]{:S(2)}, u32[]{:S(2)}) %collective-permute-start.9) | collective-permute-done | bytes 65568 | tf_op jit(solution)/shard_map/ppermute | solution.py:168
  40.7 1.0 %shard_map.108 = bf16[128,1024]{1,0:T(8,128)(2,1)} custom-call(bf16[32,128]{1,0:T(8,128)(2,1)S(1)} %copy-done.1, bf16[32,1024]{1,0:T(8,128)(2,1)S(1)} %collective-permute-done.7.refs_1_, bf16[32,1024]{1,0:T(8,128)(2,1)S(1)} %collective-permute-done.8.refs_2_, bf16[32,1024]{1,0:T(8,128)(2,1)S(1)} %collective-permute-done.9.refs_3_, ...), custom_call_target="tpu_custom_call" | custom-call | bytes 532480 | tf_op jit(solution)/shard_map/pallas_call | solution.py:29
  (5 shorter events, 0.0 us)
Async XLA Ops:
  3.9 12.6 %collective-permute-start.2 = (bf16[672,1024]{1,0:T(8,128)(2,1)}, bf16[672,1024]{1,0:T(8,128)(2,1)S(1)}, u32[]{:S(2)}, u32[]{:S(2)}) collective-permute-start(bf16[672,1024]{1,0:T(8,128)(2,1)} %get-tuple-element.26.refs_2_), channel_id=1, source_target_pairs={{0,1},{1,0},{2,3},{3,2},{4,5},{5,4},{6,7},{7,6},{8,9},{9,8},{10,11... | collective-permute-start | bytes 4128776 | tf_op jit(solution)/shard_map/ppermute | solution.py:171
  4.5 10.5 %collective-permute-start = (bf16[64,1024]{1,0:T(8,128)(2,1)}, bf16[64,1024]{1,0:T(8,128)(2,1)S(1)}, u32[]{:S(2)}, u32[]{:S(2)}) collective-permute-start(bf16[64,1024]{1,0:T(8,128)(2,1)} %get-tuple-element.25), channel_id=1, source_target_pairs={{0,8},{1,10},{4,12},{5,14},{8,0},{9,2},{12,4},{13,6},{2,9},{3,11},... | collective-permute-start | bytes 393224 | tf_op jit(solution)/shard_map/ppermute | solution.py:168
  8.1 8.4 %collective-permute-start.5 = (bf16[64,1024]{1,0:T(8,128)(2,1)}, bf16[64,1024]{1,0:T(8,128)(2,1)S(1)}, u32[]{:S(2)}, u32[]{:S(2)}) collective-permute-start(bf16[64,1024]{1,0:T(8,128)(2,1)} %get-tuple-element.25), channel_id=1, source_target_pairs={{0,4},{1,6},{4,0},{5,2},{8,12},{9,14},{12,8},{13,10},{2,5},{3,7},{... | collective-permute-start | bytes 393224 | tf_op jit(solution)/shard_map/ppermute | solution.py:168
  9.7 6.9 %collective-permute-start.4 = (bf16[64,1024]{1,0:T(8,128)(2,1)}, bf16[64,1024]{1,0:T(8,128)(2,1)S(1)}, u32[]{:S(2)}, u32[]{:S(2)}) collective-permute-start(bf16[64,1024]{1,0:T(8,128)(2,1)} %get-tuple-element.25), channel_id=1, source_target_pairs={{0,0},{1,2},{4,4},{5,6},{8,8},{9,10},{12,12},{13,14},{2,1},{3,3},{... | collective-permute-start | bytes 393224 | tf_op jit(solution)/shard_map/ppermute | solution.py:168
  14.9 6.2 %collective-permute-start.1 = (bf16[64,1024]{1,0:T(8,128)(2,1)S(1)}, bf16[64,1024]{1,0:T(8,128)(2,1)S(1)}, u32[]{:S(2)}, u32[]{:S(2)}) collective-permute-start(bf16[64,1024]{1,0:T(8,128)(2,1)S(1)} %collective-permute-done.refs_0_.refs_9_), channel_id=1, source_target_pairs={{0,4},{4,0},{8,12},{12,8},{1,5},{5,1},{9,13},{13,9},{2,6},{6,2},{1... | collective-permute-start | bytes 393224 | tf_op jit(solution)/shard_map/ppermute | solution.py:182
  16.6 1.3 %copy-start = (bf16[672,1024]{1,0:T(8,128)(2,1)S(1)}, bf16[672,1024]{1,0:T(8,128)(2,1)}, u32[]{:S(2)}) copy-start(bf16[672,1024]{1,0:T(8,128)(2,1)} %get-tuple-element.26.refs_2_) | copy-start | bytes 4128772
  18.8 7.5 %collective-permute-start.6 = (bf16[672,128]{1,0:T(8,128)(2,1)S(1)}, bf16[672,128]{1,0:T(8,128)(2,1)S(1)}, u32[]{:S(2)}, u32[]{:S(2)}) collective-permute-start(bf16[672,128]{1,0:T(8,128)(2,1)S(1)} %get-tuple-element.30), channel_id=1, source_target_pairs={{0,2},{2,0},{1,3},{3,1},{4,6},{6,4},{5,7},{7,5},{8,10},{10,8},{9,1... | collective-permute-start | bytes 516104 | tf_op jit(solution)/shard_map/ppermute | solution.py:171
  22.1 7.9 %collective-permute-start.3 = (bf16[672,128]{1,0:T(8,128)(2,1)S(1)}, bf16[672,128]{1,0:T(8,128)(2,1)S(1)}, u32[]{:S(2)}, u32[]{:S(2)}) collective-permute-start(bf16[672,128]{1,0:T(8,128)(2,1)S(1)} %get-tuple-element.28), channel_id=1, source_target_pairs={{0,2},{2,0},{1,3},{3,1},{4,6},{6,4},{5,7},{7,5},{8,10},{10,8},{9,1... | collective-permute-start | bytes 516104 | tf_op jit(solution)/shard_map/ppermute | solution.py:171
  30.6 10.2 %copy-start.1 = (bf16[32,128]{1,0:T(8,128)(2,1)S(1)}, bf16[32,128]{1,0:T(8,128)(2,1)}, u32[]{:S(2)}) copy-start(bf16[32,128]{1,0:T(8,128)(2,1)} %get-tuple-element.24.refs_0_) | copy-start | bytes 24580
  30.6 4.7 %collective-permute-start.11 = (bf16[256,1024]{1,0:T(8,128)(2,1)S(1)}, bf16[256,1024]{1,0:T(8,128)(2,1)S(1)}, u32[]{:S(2)}, u32[]{:S(2)}) collective-permute-start(bf16[256,1024]{1,0:T(8,128)(2,1)S(1)} %get-tuple-element.38.refs_0_), channel_id=1, source_target_pairs={{0,1},{1,0},{2,3},{3,2},{4,5},{5,4},{6,7},{7,6},{8,9},{9,8},{10,11... | collective-permute-start | bytes 1572872 | tf_op jit(solution)/shard_map/ppermute | solution.py:171
  30.7 4.0 %collective-permute-start.12 = (bf16[672,256]{1,0:T(8,128)(2,1)S(1)}, bf16[672,256]{1,0:T(8,128)(2,1)S(1)}, u32[]{:S(2)}, u32[]{:S(2)}) collective-permute-start(bf16[672,256]{1,0:T(8,128)(2,1)S(1)} %get-tuple-element.39.refs_2_), channel_id=1, source_target_pairs={{0,1},{1,0},{2,3},{3,2},{4,5},{5,4},{6,7},{7,6},{8,9},{9,8},{10,11... | collective-permute-start | bytes 1032200 | tf_op jit(solution)/shard_map/ppermute | solution.py:171
  31.2 6.9 %collective-permute-start.7 = (bf16[32,1024]{1,0:T(8,128)(2,1)S(1)}, bf16[32,1024]{1,0:T(8,128)(2,1)S(1)}, u32[]{:S(2)}, u32[]{:S(2)}) collective-permute-start(bf16[32,1024]{1,0:T(8,128)(2,1)S(1)} %get-tuple-element.34), channel_id=1, source_target_pairs={{0,8},{1,10},{4,12},{5,14},{8,0},{9,2},{12,4},{13,6},{2,9},{3,11},... | collective-permute-start | bytes 196616 | tf_op jit(solution)/shard_map/ppermute | solution.py:168
  33.3 6.9 %collective-permute-start.8 = (bf16[32,1024]{1,0:T(8,128)(2,1)S(1)}, bf16[32,1024]{1,0:T(8,128)(2,1)S(1)}, u32[]{:S(2)}, u32[]{:S(2)}) collective-permute-start(bf16[32,1024]{1,0:T(8,128)(2,1)S(1)} %get-tuple-element.35), channel_id=1, source_target_pairs={{0,12},{1,14},{4,8},{5,10},{8,4},{9,6},{12,0},{13,2},{2,13},{3,15}... | collective-permute-start | bytes 196616 | tf_op jit(solution)/shard_map/ppermute | solution.py:168
  34.5 6.3 %collective-permute-start.9 = (bf16[32,1024]{1,0:T(8,128)(2,1)S(1)}, bf16[32,1024]{1,0:T(8,128)(2,1)S(1)}, u32[]{:S(2)}, u32[]{:S(2)}) collective-permute-start(bf16[32,1024]{1,0:T(8,128)(2,1)S(1)} %get-tuple-element.36), channel_id=1, source_target_pairs={{0,4},{1,6},{4,0},{5,2},{8,12},{9,14},{12,8},{13,10},{2,5},{3,7},{... | collective-permute-start | bytes 196616 | tf_op jit(solution)/shard_map/ppermute | solution.py:168
  34.7 6.1 %collective-permute-start.10 = (bf16[32,1024]{1,0:T(8,128)(2,1)S(1)}, bf16[32,1024]{1,0:T(8,128)(2,1)S(1)}, u32[]{:S(2)}, u32[]{:S(2)}) collective-permute-start(bf16[32,1024]{1,0:T(8,128)(2,1)S(1)} %get-tuple-element.37), channel_id=1, source_target_pairs={{0,0},{1,2},{4,4},{5,6},{8,8},{9,10},{12,12},{13,14},{2,1},{3,3},{... | collective-permute-start | bytes 196616 | tf_op jit(solution)/shard_map/ppermute | solution.py:168

commit v4 on v3

--- a/solution.py
+++ b/solution.py
@@ -42,10 +42,10 @@
     return jax.ShapeDtypeStruct(shape, dtype)
 
 
-def pack_body(picks_in, scores_in, tok_in, grad_in, gate_in, up_in, down_in, xd_ref, sel_ref, w_out, picks_ref, scores_ref, tok_ref, grad_ref, w_ref, sems):
+def pack_body(picks_in, scores_in, tok_in, grad_in, gate_in, up_in, down_in, xd_ref, sel_ref, w_out, picks_ref, scores_ref, tok_ref, grad_ref, sems):
     pairs = [(picks_in, picks_ref), (scores_in, scores_ref), (tok_in, tok_ref), (grad_in, grad_ref)]
     h = gate_in.shape[0]
-    pairs += [(w, w_ref.at[i * h : (i + 1) * h]) for i, w in enumerate((gate_in, up_in, down_in))]
+    pairs += [(w, w_out.at[i * h : (i + 1) * h]) for i, w in enumerate((gate_in, up_in, down_in))]
     copies = [pltpu.make_async_copy(a, b, sems.at[i]) for i, (a, b) in enumerate(pairs)]
     for c in copies:
         c.start()
@@ -64,17 +64,14 @@
     sel = jnp.where((rank == slots) & (picked[0:1] > 0.5), 1.0, 0.0).astype(BF)
     sel_ref[...] = sel
     chosen = dot(sel, hit, NN)
-    for c in copies[4:]:
-        c.wait()
-    out = pltpu.make_async_copy(w_ref, w_out, sems.at[7])
-    out.start()
     copies[1].wait()
     score = jnp.sum(chosen * scores_ref[...], axis=1, keepdims=True)
     copies[2].wait()
     xd_ref[0:MOST] = dot(sel, tok_ref[...], NN).astype(BF)
     copies[3].wait()
     xd_ref[MOST:] = (score * dot(sel, grad_ref[...], NN)).astype(BF)
-    out.wait()
+    for c in copies[4:]:
+        c.wait()
 
 
 def partial_body(blocks, *refs):
@@ -173,10 +170,10 @@
     xd, sel, w_own = call(
         pack_body,
         [arr((2 * MOST, half)), arr((MOST, tok_dev)), arr((3 * h, half))],
-        picks, scores, tokens[0], grad_out[0], w_gate.T, w_up.T, w_down,
-        far=True, far_out=1, mib=60,
+        *(pltpu.with_memory_space_constraint(a, pltpu.HBM) for a in (picks, scores, tokens[0], grad_out[0], w_gate.T, w_up.T, w_down)),
+        far=True, mib=24,
         scratch=[pltpu.VMEM((1, cap), jnp.int32), pltpu.VMEM((1, cap), F32), pltpu.VMEM((tok_dev, half), BF),
-                 pltpu.VMEM((tok_dev, half), BF), pltpu.VMEM((3 * h, half), BF), pltpu.SemaphoreType.DMA((8,))],
+                 pltpu.VMEM((tok_dev, half), BF), pltpu.SemaphoreType.DMA((7,))],
     )
     blocks = {s: across(xd, s) for s in (2, 1, 0)}
     blocks[3] = lax.ppermute(blocks[2], "seq", [(k, k ^ 1) for k in range(n)])

time: 41.9 us -> 38.5 us (0.919)
  Pallas kernels: 8.95 us -> 7.19 us
  local copies, waits for them, and re-layouts: 1.34 us -> 0 us
  starting transfers between devices: 17 us -> 16.2 us
    pallas_call x7, Pallas kernels: 8.95 us -> 7.19 us  [call(): pl.pallas_call(run, out_shape=outs, in_specs=[pl.BlockSpec(memory_space=p...]
    ppermute x5, waiting for transfers between devices: 6.36 us -> 5.03 us  [swap(): return lax.ppermute(x, axis, [(0, 1), (1, 0)])]
    unnamed x4 -> x0, local copies, waits for them, and re-layouts: 1.34 us -> none
    ppermute x1, waiting for transfers between devices: 0.01 us -> 1.19 us  [swapped(): blocks[3] = lax.ppermute(blocks[2], 'seq', [(k, k ^ 1) for k in range(n)])]
    ppermute x7, starting transfers between devices: 10.9 us -> 10.1 us  [across(): return lax.ppermute(x, ('seq', 'dp', 'tensor'), pairs)]
    ppermute x7, waiting for transfers between devices: 7.33 us -> 7.89 us  [across(): return lax.ppermute(x, ('seq', 'dp', 'tensor'), pairs)]
  transfers between devices with their start and end apart: 13 -> 13, of which waited for: 6 -> 7; matrix products, arithmetic and copies ran while one was open for 0% -> 0% of each run, Pallas kernels for 10% -> 11%
where the time goes in v4:
time: 38.5 us; the launch traced here: 38.3 us
  starting transfers between devices  16.2 us (42%)
  waiting for transfers between devices  14.1 us (37%)
  Pallas kernels  7.19 us (19%)
  between operations  0.72 us (2%)
    ppermute x7, starting transfers between devices, across(): return lax.ppermute(x, ('seq', 'dp', 'tensor'), pairs)  10.1 us
    ppermute x7, waiting for transfers between devices, across(): return lax.ppermute(x, ('seq', 'dp', 'tensor'), pairs)  7.89 us
    pallas_call x7, Pallas kernels, call(): pl.pallas_call(run, out_shape=outs, in_specs=[pl.BlockSpec(memory_space=p...  7.19 us
    ppermute x5, waiting for transfers between devices, swap(): return lax.ppermute(x, axis, [(0, 1), (1, 0)])  5.03 us
    ppermute x5, starting transfers between devices, swap(): return lax.ppermute(x, axis, [(0, 1), (1, 0)])  4.69 us
    ppermute x1, starting transfers between devices, swapped(): blocks[3] = lax.ppermute(blocks[2], 'seq', [(k, k ^ 1) for k in range(n)])  1.5 us
    ppermute x1, waiting for transfers between devices, swapped(): blocks[3] = lax.ppermute(blocks[2], 'seq', [(k, k ^ 1) for k in range(n)])  1.19 us
  transfers between devices with their start and end apart: 13, of which 7 were waited for; matrix products, arithmetic and copies ran while one was open for 0% of the time, Pallas kernels for 11%

profile of v4, /device:TPU:0, one launch (start us, length us, event | category | flops | bytes accessed | tf_op | source)
XLA Modules:
  0.0 38.3 jit_solution(9790863168023219122)
XLA Ops:
  0.6 1.5 %shard_map.102 = (bf16[64,1024]{1,0:T(8,128)(2,1)S(1)}, bf16[32,128]{1,0:T(8,128)(2,1)S(1)}, bf16[672,1024]{1,0:T(8,128)(2,1)S(1)}) custom-call(s32[1,64]{1,0:T(1,128)} %refs_0_.1, f32[1,64]{1,0:T(1,128)} %refs_1_.1, bf16[128,1024]{1,0:T(8,128)(2,1)} %bitcast.9, bf16[128,1024]{1,0:T(8,128)(2,1)} %bitcast.10, bf16[224,1024]{1,0:T(8,128)(2,1)} %bitcast.7, ...), custom_call_target="tpu_custom_call" | custom-call | bytes 3416576 | tf_op jit(solution)/shard_map/pallas_call | solution.py:29
  2.2 0.5 %collective-permute-start.2 = (bf16[672,1024]{1,0:T(8,128)(2,1)S(1)}, bf16[672,1024]{1,0:T(8,128)(2,1)S(1)}, u32[]{:S(2)}, u32[]{:S(2)}) collective-permute-start(bf16[672,1024]{1,0:T(8,128)(2,1)S(1)} %get-tuple-element.26.refs_2_), channel_id=1, source_target_pairs={{0,1},{1,0},{2,3},{3,2},{4,5},{5,4},{6,7},{7,6},{8,9},{9,8},{10,11... | collective-permute-start | bytes 4128776 | tf_op jit(solution)/shard_map/ppermute | solution.py:168
  2.7 3.7 %collective-permute-start = (bf16[64,1024]{1,0:T(8,128)(2,1)S(1)}, bf16[64,1024]{1,0:T(8,128)(2,1)S(1)}, u32[]{:S(2)}, u32[]{:S(2)}) collective-permute-start(bf16[64,1024]{1,0:T(8,128)(2,1)S(1)} %get-tuple-element.25), channel_id=1, source_target_pairs={{0,8},{1,10},{4,12},{5,14},{8,0},{9,2},{12,4},{13,6},{2,9},{3,11},... | collective-permute-start | bytes 393224 | tf_op jit(solution)/shard_map/ppermute | solution.py:165
  6.4 1.6 %collective-permute-start.5 = (bf16[64,1024]{1,0:T(8,128)(2,1)S(1)}, bf16[64,1024]{1,0:T(8,128)(2,1)S(1)}, u32[]{:S(2)}, u32[]{:S(2)}) collective-permute-start(bf16[64,1024]{1,0:T(8,128)(2,1)S(1)} %get-tuple-element.25), channel_id=1, source_target_pairs={{0,4},{1,6},{4,0},{5,2},{8,12},{9,14},{12,8},{13,10},{2,5},{3,7},{... | collective-permute-start | bytes 393224 | tf_op jit(solution)/shard_map/ppermute | solution.py:165
  7.9 0.7 %collective-permute-start.4 = (bf16[64,1024]{1,0:T(8,128)(2,1)S(1)}, bf16[64,1024]{1,0:T(8,128)(2,1)S(1)}, u32[]{:S(2)}, u32[]{:S(2)}) collective-permute-start(bf16[64,1024]{1,0:T(8,128)(2,1)S(1)} %get-tuple-element.25), channel_id=1, source_target_pairs={{0,0},{1,2},{4,4},{5,6},{8,8},{9,10},{12,12},{13,14},{2,1},{3,3},{... | collective-permute-start | bytes 393224 | tf_op jit(solution)/shard_map/ppermute | solution.py:165
  8.6 4.4 %collective-permute-done.refs_0_.refs_9_ = bf16[64,1024]{1,0:T(8,128)(2,1)S(1)} collective-permute-done((bf16[64,1024]{1,0:T(8,128)(2,1)S(1)}, bf16[64,1024]{1,0:T(8,128)(2,1)S(1)}, u32[]{:S(2)}, u32[]{:S(2)}) %collective-permute-start) | collective-permute-done | bytes 131104 | tf_op jit(solution)/shard_map/ppermute | solution.py:165
  13.0 1.5 %collective-permute-start.1 = (bf16[64,1024]{1,0:T(8,128)(2,1)S(1)}, bf16[64,1024]{1,0:T(8,128)(2,1)S(1)}, u32[]{:S(2)}, u32[]{:S(2)}) collective-permute-start(bf16[64,1024]{1,0:T(8,128)(2,1)S(1)} %collective-permute-done.refs_0_.refs_9_), channel_id=1, source_target_pairs={{0,4},{4,0},{8,12},{12,8},{1,5},{5,1},{9,13},{13,9},{2,6},{6,2},{1... | collective-permute-start | bytes 393224 | tf_op jit(solution)/shard_map/ppermute | solution.py:179
  14.5 0.0 collective-permute-done.5.refs_1_.refs_8_
  14.5 0.0 collective-permute-done.4.refs_0_.refs_7_
  14.5 0.0 collective-permute-done.2.refs_3_
  14.5 0.9 %shard_map.104 = (f32[672,128]{1,0:T(8,128)S(1)}, bf16[672,128]{1,0:T(8,128)(2,1)S(1)}) custom-call(bf16[64,1024]{1,0:T(8,128)(2,1)S(1)} %collective-permute-done.4.refs_0_.refs_7_, bf16[64,1024]{1,0:T(8,128)(2,1)S(1)} %collective-permute-done.5.refs_1_.refs_8_, bf16[672,1024]{1,0:T(8,128)(2,1)S(1)} %get-tuple-element.26.refs_2_, ...), custom_call_target="tpu_custom_call" | custom-call | flops 176160768 | bytes 3530752 | tf_op jit(solution)/shard_map/pallas_call | solution.py:29
  15.4 2.4 %collective-permute-start.6 = (bf16[672,128]{1,0:T(8,128)(2,1)S(1)}, bf16[672,128]{1,0:T(8,128)(2,1)S(1)}, u32[]{:S(2)}, u32[]{:S(2)}) collective-permute-start(bf16[672,128]{1,0:T(8,128)(2,1)S(1)} %get-tuple-element.30), channel_id=1, source_target_pairs={{0,2},{2,0},{1,3},{3,1},{4,6},{6,4},{5,7},{7,5},{8,10},{10,8},{9,1... | collective-permute-start | bytes 516104 | tf_op jit(solution)/shard_map/ppermute | solution.py:168
  17.9 1.2 %collective-permute-done.1.refs_1_.refs_10_ = bf16[64,1024]{1,0:T(8,128)(2,1)S(1)} collective-permute-done((bf16[64,1024]{1,0:T(8,128)(2,1)S(1)}, bf16[64,1024]{1,0:T(8,128)(2,1)S(1)}, u32[]{:S(2)}, u32[]{:S(2)}) %collective-permute-start.1) | collective-permute-done | bytes 131104 | tf_op jit(solution)/shard_map/ppermute | solution.py:179
  19.1 0.9 %shard_map.103 = (f32[672,128]{1,0:T(8,128)S(1)}, bf16[672,128]{1,0:T(8,128)(2,1)S(1)}) custom-call(bf16[64,1024]{1,0:T(8,128)(2,1)S(1)} %collective-permute-done.refs_0_.refs_9_, bf16[64,1024]{1,0:T(8,128)(2,1)S(1)} %collective-permute-done.1.refs_1_.refs_10_, bf16[672,1024]{1,0:T(8,128)(2,1)S(1)} %get-tuple-element.26.refs_2_, ...), custom_call_target="tpu_custom_call" | custom-call | flops 176160768 | bytes 3530752 | tf_op jit(solution)/shard_map/pallas_call | solution.py:29
  20.0 1.2 %collective-permute-start.3 = (bf16[672,128]{1,0:T(8,128)(2,1)S(1)}, bf16[672,128]{1,0:T(8,128)(2,1)S(1)}, u32[]{:S(2)}, u32[]{:S(2)}) collective-permute-start(bf16[672,128]{1,0:T(8,128)(2,1)S(1)} %get-tuple-element.28), channel_id=1, source_target_pairs={{0,2},{2,0},{1,3},{3,1},{4,6},{6,4},{5,7},{7,5},{8,10},{10,8},{9,1... | collective-permute-start | bytes 516104 | tf_op jit(solution)/shard_map/ppermute | solution.py:168
  21.2 1.9 %collective-permute-done.6.refs_1_ = bf16[672,128]{1,0:T(8,128)(2,1)S(1)} collective-permute-done((bf16[672,128]{1,0:T(8,128)(2,1)S(1)}, bf16[672,128]{1,0:T(8,128)(2,1)S(1)}, u32[]{:S(2)}, u32[]{:S(2)}) %collective-permute-start.6) | collective-permute-done | bytes 172064 | tf_op jit(solution)/shard_map/ppermute | solution.py:168
  23.1 0.5 %shard_map.105 = (bf16[672,128]{1,0:T(8,128)(2,1)S(1)}, bf16[32,1024]{1,0:T(8,128)(2,1)S(1)}, bf16[32,1024]{1,0:T(8,128)(2,1)S(1)}) custom-call(f32[672,128]{1,0:T(8,128)S(1)} %get-tuple-element.29.refs_0_, bf16[672,128]{1,0:T(8,128)(2,1)S(1)} %collective-permute-done.6.refs_1_, bf16[672,1024]{1,0:T(8,128)(2,1)S(1)} %get-tuple-element.26.refs_2_, ...), custom_call_target="tpu_custom_call" | custom-call | flops 234881024 | bytes 3571712 | tf_op jit(solution)/shard_map/pallas_call | solution.py:29
  23.6 3.1 %collective-permute-done.3.refs_1_ = bf16[672,128]{1,0:T(8,128)(2,1)S(1)} collective-permute-done((bf16[672,128]{1,0:T(8,128)(2,1)S(1)}, bf16[672,128]{1,0:T(8,128)(2,1)S(1)}, u32[]{:S(2)}, u32[]{:S(2)}) %collective-permute-start.3) | collective-permute-done | bytes 172064 | tf_op jit(solution)/shard_map/ppermute | solution.py:168
  26.7 0.5 %shard_map.106 = (bf16[672,256]{1,0:T(8,128)(2,1)S(1)}, bf16[256,1024]{1,0:T(8,128)(2,1)S(1)}, bf16[32,1024]{1,0:T(8,128)(2,1)S(1)}, bf16[32,1024]{1,0:T(8,128)(...) custom-call(f32[672,128]{1,0:T(8,128)S(1)} %get-tuple-element.27.refs_4_.refs_0_, ...), custom_call_target="tpu_custom_call" | custom-call | flops 234881024 | bytes 5226496 | tf_op jit(solution)/shard_map/pallas_call | solution.py:29
  27.3 0.1 collective-permute-start.11
  27.3 0.5 %collective-permute-start.12 = (bf16[672,256]{1,0:T(8,128)(2,1)S(1)}, bf16[672,256]{1,0:T(8,128)(2,1)S(1)}, u32[]{:S(2)}, u32[]{:S(2)}) collective-permute-start(bf16[672,256]{1,0:T(8,128)(2,1)S(1)} %get-tuple-element.39.refs_2_), channel_id=1, source_target_pairs={{0,1},{1,0},{2,3},{3,2},{4,5},{5,4},{6,7},{7,6},{8,9},{9,8},{10,11... | collective-permute-start | bytes 1032200 | tf_op jit(solution)/shard_map/ppermute | solution.py:168
  27.8 2.1 %collective-permute-start.7 = (bf16[32,1024]{1,0:T(8,128)(2,1)S(1)}, bf16[32,1024]{1,0:T(8,128)(2,1)S(1)}, u32[]{:S(2)}, u32[]{:S(2)}) collective-permute-start(bf16[32,1024]{1,0:T(8,128)(2,1)S(1)} %get-tuple-element.34), channel_id=1, source_target_pairs={{0,8},{1,10},{4,12},{5,14},{8,0},{9,2},{12,4},{13,6},{2,9},{3,11},... | collective-permute-start | bytes 196616 | tf_op jit(solution)/shard_map/ppermute | solution.py:165
  30.0 1.2 %collective-permute-start.8 = (bf16[32,1024]{1,0:T(8,128)(2,1)S(1)}, bf16[32,1024]{1,0:T(8,128)(2,1)S(1)}, u32[]{:S(2)}, u32[]{:S(2)}) collective-permute-start(bf16[32,1024]{1,0:T(8,128)(2,1)S(1)} %get-tuple-element.35), channel_id=1, source_target_pairs={{0,12},{1,14},{4,8},{5,10},{8,4},{9,6},{12,0},{13,2},{2,13},{3,15}... | collective-permute-start | bytes 196616 | tf_op jit(solution)/shard_map/ppermute | solution.py:165
  31.1 0.2 collective-permute-start.9
  31.3 0.0 collective-permute-done.12.refs_3_
  31.4 0.7 %collective-permute-start.10 = (bf16[32,1024]{1,0:T(8,128)(2,1)S(1)}, bf16[32,1024]{1,0:T(8,128)(2,1)S(1)}, u32[]{:S(2)}, u32[]{:S(2)}) collective-permute-start(bf16[32,1024]{1,0:T(8,128)(2,1)S(1)} %get-tuple-element.37), channel_id=1, source_target_pairs={{0,0},{1,2},{4,4},{5,6},{8,8},{9,10},{12,12},{13,14},{2,1},{3,3},{... | collective-permute-start | bytes 196616 | tf_op jit(solution)/shard_map/ppermute | solution.py:165
  32.0 1.8 %shard_map.107 = (bf16[224,1024]{1,0:T(8,128)(2,1)}, bf16[224,1024]{1,0:T(8,128)(2,1)}, bf16[224,1024]{1,0:T(8,128)(2,1)}, f32[8,128]{1,0:T(8,128)S(1)}) custom-call(bf16[256,1024]{1,0:T(8,128)(2,1)S(1)} %get-tuple-element.38.refs_0_, bf16[256,1024]{1,0:T(8,128)(2,1)S(1)} %collective-permute-done.11.refs_1_, bf16[672,256]{1,0:T(8,128)(2,1)S(1)} %get-tuple-element.39.refs_2_, ...), custom_call_target="tpu_custom_call" | custom-call | flops 352321536 | bytes 3117056 | tf_op jit(solution)/shard_map/pallas_call | solution.py:29
  33.8 0.5 %collective-permute-done.7.refs_1_ = bf16[32,1024]{1,0:T(8,128)(2,1)S(1)} collective-permute-done((bf16[32,1024]{1,0:T(8,128)(2,1)S(1)}, bf16[32,1024]{1,0:T(8,128)(2,1)S(1)}, u32[]{:S(2)}, u32[]{:S(2)}) %collective-permute-start.7) | collective-permute-done | bytes 65568 | tf_op jit(solution)/shard_map/ppermute | solution.py:165
  34.3 2.5 %collective-permute-done.8.refs_2_ = bf16[32,1024]{1,0:T(8,128)(2,1)S(1)} collective-permute-done((bf16[32,1024]{1,0:T(8,128)(2,1)S(1)}, bf16[32,1024]{1,0:T(8,128)(2,1)S(1)}, u32[]{:S(2)}, u32[]{:S(2)}) %collective-permute-start.8) | collective-permute-done | bytes 65568 | tf_op jit(solution)/shard_map/ppermute | solution.py:165
  36.8 0.5 %collective-permute-done.9.refs_3_ = bf16[32,1024]{1,0:T(8,128)(2,1)S(1)} collective-permute-done((bf16[32,1024]{1,0:T(8,128)(2,1)S(1)}, bf16[32,1024]{1,0:T(8,128)(2,1)S(1)}, u32[]{:S(2)}, u32[]{:S(2)}) %collective-permute-start.9) | collective-permute-done | bytes 65568 | tf_op jit(solution)/shard_map/ppermute | solution.py:165
  37.3 0.0 collective-permute-done.10.refs_4_
  37.3 1.0 %shard_map.108 = bf16[128,1024]{1,0:T(8,128)(2,1)} custom-call(bf16[32,128]{1,0:T(8,128)(2,1)S(1)} %get-tuple-element.24.refs_0_, bf16[32,1024]{1,0:T(8,128)(2,1)S(1)} %collective-permute-done.7.refs_1_, bf16[32,1024]{1,0:T(8,128)(2,1)S(1)} %collective-permute-done.8.refs_2_, bf16[32,1024]{1,0:T(8,128)(2,1)S(1)} %collective-permute-done.9.refs_3_, ...), custom_call_target="tpu_custom_call" | custom-call | bytes 532480 | tf_op jit(solution)/shard_map/pallas_call | solution.py:29
  (1 shorter events, 0.0 us)
Async XLA Ops:
  2.2 12.3 %collective-permute-start.2 = (bf16[672,1024]{1,0:T(8,128)(2,1)S(1)}, bf16[672,1024]{1,0:T(8,128)(2,1)S(1)}, u32[]{:S(2)}, u32[]{:S(2)}) collective-permute-start(bf16[672,1024]{1,0:T(8,128)(2,1)S(1)} %get-tuple-element.26.refs_2_), channel_id=1, source_target_pairs={{0,1},{1,0},{2,3},{3,2},{4,5},{5,4},{6,7},{7,6},{8,9},{9,8},{10,11... | collective-permute-start | bytes 4128776 | tf_op jit(solution)/shard_map/ppermute | solution.py:168
  2.7 10.3 %collective-permute-start = (bf16[64,1024]{1,0:T(8,128)(2,1)S(1)}, bf16[64,1024]{1,0:T(8,128)(2,1)S(1)}, u32[]{:S(2)}, u32[]{:S(2)}) collective-permute-start(bf16[64,1024]{1,0:T(8,128)(2,1)S(1)} %get-tuple-element.25), channel_id=1, source_target_pairs={{0,8},{1,10},{4,12},{5,14},{8,0},{9,2},{12,4},{13,6},{2,9},{3,11},... | collective-permute-start | bytes 393224 | tf_op jit(solution)/shard_map/ppermute | solution.py:165
  6.4 8.1 %collective-permute-start.5 = (bf16[64,1024]{1,0:T(8,128)(2,1)S(1)}, bf16[64,1024]{1,0:T(8,128)(2,1)S(1)}, u32[]{:S(2)}, u32[]{:S(2)}) collective-permute-start(bf16[64,1024]{1,0:T(8,128)(2,1)S(1)} %get-tuple-element.25), channel_id=1, source_target_pairs={{0,4},{1,6},{4,0},{5,2},{8,12},{9,14},{12,8},{13,10},{2,5},{3,7},{... | collective-permute-start | bytes 393224 | tf_op jit(solution)/shard_map/ppermute | solution.py:165
  7.9 6.6 %collective-permute-start.4 = (bf16[64,1024]{1,0:T(8,128)(2,1)S(1)}, bf16[64,1024]{1,0:T(8,128)(2,1)S(1)}, u32[]{:S(2)}, u32[]{:S(2)}) collective-permute-start(bf16[64,1024]{1,0:T(8,128)(2,1)S(1)} %get-tuple-element.25), channel_id=1, source_target_pairs={{0,0},{1,2},{4,4},{5,6},{8,8},{9,10},{12,12},{13,14},{2,1},{3,3},{... | collective-permute-start | bytes 393224 | tf_op jit(solution)/shard_map/ppermute | solution.py:165
  13.0 6.1 %collective-permute-start.1 = (bf16[64,1024]{1,0:T(8,128)(2,1)S(1)}, bf16[64,1024]{1,0:T(8,128)(2,1)S(1)}, u32[]{:S(2)}, u32[]{:S(2)}) collective-permute-start(bf16[64,1024]{1,0:T(8,128)(2,1)S(1)} %collective-permute-done.refs_0_.refs_9_), channel_id=1, source_target_pairs={{0,4},{4,0},{8,12},{12,8},{1,5},{5,1},{9,13},{13,9},{2,6},{6,2},{1... | collective-permute-start | bytes 393224 | tf_op jit(solution)/shard_map/ppermute | solution.py:179
  15.4 7.7 %collective-permute-start.6 = (bf16[672,128]{1,0:T(8,128)(2,1)S(1)}, bf16[672,128]{1,0:T(8,128)(2,1)S(1)}, u32[]{:S(2)}, u32[]{:S(2)}) collective-permute-start(bf16[672,128]{1,0:T(8,128)(2,1)S(1)} %get-tuple-element.30), channel_id=1, source_target_pairs={{0,2},{2,0},{1,3},{3,1},{4,6},{6,4},{5,7},{7,5},{8,10},{10,8},{9,1... | collective-permute-start | bytes 516104 | tf_op jit(solution)/shard_map/ppermute | solution.py:168
  20.0 6.7 %collective-permute-start.3 = (bf16[672,128]{1,0:T(8,128)(2,1)S(1)}, bf16[672,128]{1,0:T(8,128)(2,1)S(1)}, u32[]{:S(2)}, u32[]{:S(2)}) collective-permute-start(bf16[672,128]{1,0:T(8,128)(2,1)S(1)} %get-tuple-element.28), channel_id=1, source_target_pairs={{0,2},{2,0},{1,3},{3,1},{4,6},{6,4},{5,7},{7,5},{8,10},{10,8},{9,1... | collective-permute-start | bytes 516104 | tf_op jit(solution)/shard_map/ppermute | solution.py:168
  27.3 4.8 %collective-permute-start.11 = (bf16[256,1024]{1,0:T(8,128)(2,1)S(1)}, bf16[256,1024]{1,0:T(8,128)(2,1)S(1)}, u32[]{:S(2)}, u32[]{:S(2)}) collective-permute-start(bf16[256,1024]{1,0:T(8,128)(2,1)S(1)} %get-tuple-element.38.refs_0_), channel_id=1, source_target_pairs={{0,1},{1,0},{2,3},{3,2},{4,5},{5,4},{6,7},{7,6},{8,9},{9,8},{10,11... | collective-permute-start | bytes 1572872 | tf_op jit(solution)/shard_map/ppermute | solution.py:168
  27.3 4.0 %collective-permute-start.12 = (bf16[672,256]{1,0:T(8,128)(2,1)S(1)}, bf16[672,256]{1,0:T(8,128)(2,1)S(1)}, u32[]{:S(2)}, u32[]{:S(2)}) collective-permute-start(bf16[672,256]{1,0:T(8,128)(2,1)S(1)} %get-tuple-element.39.refs_2_), channel_id=1, source_target_pairs={{0,1},{1,0},{2,3},{3,2},{4,5},{5,4},{6,7},{7,6},{8,9},{9,8},{10,11... | collective-permute-start | bytes 1032200 | tf_op jit(solution)/shard_map/ppermute | solution.py:168
  27.8 6.4 %collective-permute-start.7 = (bf16[32,1024]{1,0:T(8,128)(2,1)S(1)}, bf16[32,1024]{1,0:T(8,128)(2,1)S(1)}, u32[]{:S(2)}, u32[]{:S(2)}) collective-permute-start(bf16[32,1024]{1,0:T(8,128)(2,1)S(1)} %get-tuple-element.34), channel_id=1, source_target_pairs={{0,8},{1,10},{4,12},{5,14},{8,0},{9,2},{12,4},{13,6},{2,9},{3,11},... | collective-permute-start | bytes 196616 | tf_op jit(solution)/shard_map/ppermute | solution.py:165
  30.0 6.9 %collective-permute-start.8 = (bf16[32,1024]{1,0:T(8,128)(2,1)S(1)}, bf16[32,1024]{1,0:T(8,128)(2,1)S(1)}, u32[]{:S(2)}, u32[]{:S(2)}) collective-permute-start(bf16[32,1024]{1,0:T(8,128)(2,1)S(1)} %get-tuple-element.35), channel_id=1, source_target_pairs={{0,12},{1,14},{4,8},{5,10},{8,4},{9,6},{12,0},{13,2},{2,13},{3,15}... | collective-permute-start | bytes 196616 | tf_op jit(solution)/shard_map/ppermute | solution.py:165
  31.1 6.2 %collective-permute-start.9 = (bf16[32,1024]{1,0:T(8,128)(2,1)S(1)}, bf16[32,1024]{1,0:T(8,128)(2,1)S(1)}, u32[]{:S(2)}, u32[]{:S(2)}) collective-permute-start(bf16[32,1024]{1,0:T(8,128)(2,1)S(1)} %get-tuple-element.36), channel_id=1, source_target_pairs={{0,4},{1,6},{4,0},{5,2},{8,12},{9,14},{12,8},{13,10},{2,5},{3,7},{... | collective-permute-start | bytes 196616 | tf_op jit(solution)/shard_map/ppermute | solution.py:165
  31.4 6.0 %collective-permute-start.10 = (bf16[32,1024]{1,0:T(8,128)(2,1)S(1)}, bf16[32,1024]{1,0:T(8,128)(2,1)S(1)}, u32[]{:S(2)}, u32[]{:S(2)}) collective-permute-start(bf16[32,1024]{1,0:T(8,128)(2,1)S(1)} %get-tuple-element.37), channel_id=1, source_target_pairs={{0,0},{1,2},{4,4},{5,6},{8,8},{9,10},{12,12},{13,14},{2,1},{3,3},{... | collective-permute-start | bytes 196616 | tf_op jit(solution)/shard_map/ppermute | solution.py:165

commit v5 on v4

--- a/solution.py
+++ b/solution.py
@@ -188,7 +188,7 @@
         )
         return keep, [swap(b, "dp") for b in send]
 
-    near, far = (0, 1), (2, 3)
+    near, far = (1, 2), (0, 3)
     dx = [arr((MOST, half))] * (n // 2)
     keep_a, recv_a = partial(near, (3,))
     keep_b, recv_b = partial(far, (3,))
@@ -336,6 +336,6 @@
         P(("groups", "seq", "tensor"), "dp"),
     )
     size = mesh.shape
-    pairs = size["dp"] == size["tensor"] == 2 and size["seq"] in (2, 4, 8)
+    pairs = size["dp"] == size["tensor"] == 2 and size["seq"] == 4
     local = swapped if pairs else gathered
     return jax.shard_map(local, mesh=mesh, in_specs=in_specs, out_specs=out_specs, check_vma=False)

time: 38.5 us -> 38.3 us (level)
  starting transfers between devices: 16.2 us -> 15 us
  waiting for transfers between devices: 14.1 us -> 15.2 us
    ppermute x1, waiting for transfers between devices: 1.19 us -> 2.46 us  [swapped(): blocks[3] = lax.ppermute(blocks[2], 'seq', [(k, k ^ 1) for k in range(n)])]
    ppermute x5, starting transfers between devices: 4.69 us -> 3.42 us  [swap(): return lax.ppermute(x, axis, [(0, 1), (1, 0)])]
where the time goes in v5:
time: 38.3 us; the launch traced here: 38.1 us
  waiting for transfers between devices  15.2 us (40%)
  starting transfers between devices  15 us (39%)
  Pallas kernels  7.2 us (19%)
  between operations  0.71 us (2%)
    ppermute x7, starting transfers between devices, across(): return lax.ppermute(x, ('seq', 'dp', 'tensor'), pairs)  10 us
    ppermute x7, waiting for transfers between devices, across(): return lax.ppermute(x, ('seq', 'dp', 'tensor'), pairs)  7.7 us
    pallas_call x7, Pallas kernels, call(): pl.pallas_call(run, out_shape=outs, in_specs=[pl.BlockSpec(memory_space=p...  7.2 us
    ppermute x5, waiting for transfers between devices, swap(): return lax.ppermute(x, axis, [(0, 1), (1, 0)])  5.07 us
    ppermute x5, starting transfers between devices, swap(): return lax.ppermute(x, axis, [(0, 1), (1, 0)])  3.42 us
    ppermute x1, waiting for transfers between devices, swapped(): blocks[3] = lax.ppermute(blocks[2], 'seq', [(k, k ^ 1) for k in range(n)])  2.46 us
    ppermute x1, starting transfers between devices, swapped(): blocks[3] = lax.ppermute(blocks[2], 'seq', [(k, k ^ 1) for k in range(n)])  1.5 us
  transfers between devices with their start and end apart: 13, of which 7 were waited for; matrix products, arithmetic and copies ran while one was open for 0% of the time, Pallas kernels for 11%

profile of v5, /device:TPU:0, one launch (start us, length us, event | category | flops | bytes accessed | tf_op | source)
XLA Modules:
  0.0 38.1 jit_solution(17263186108985347062)
XLA Ops:
  0.6 1.5 %shard_map.102 = (bf16[64,1024]{1,0:T(8,128)(2,1)S(1)}, bf16[32,128]{1,0:T(8,128)(2,1)S(1)}, bf16[672,1024]{1,0:T(8,128)(2,1)S(1)}) custom-call(s32[1,64]{1,0:T(1,128)} %refs_0_.1, f32[1,64]{1,0:T(1,128)} %refs_1_.1, bf16[128,1024]{1,0:T(8,128)(2,1)} %bitcast.9, bf16[128,1024]{1,0:T(8,128)(2,1)} %bitcast.10, bf16[224,1024]{1,0:T(8,128)(2,1)} %bitcast.7, ...), custom_call_target="tpu_custom_call" | custom-call | bytes 3416576 | tf_op jit(solution)/shard_map/pallas_call | solution.py:29
  2.2 0.5 %collective-permute-start.3 = (bf16[672,1024]{1,0:T(8,128)(2,1)S(1)}, bf16[672,1024]{1,0:T(8,128)(2,1)S(1)}, u32[]{:S(2)}, u32[]{:S(2)}) collective-permute-start(bf16[672,1024]{1,0:T(8,128)(2,1)S(1)} %get-tuple-element.26.refs_2_), channel_id=1, source_target_pairs={{0,1},{1,0},{2,3},{3,2},{4,5},{5,4},{6,7},{7,6},{8,9},{9,8},{10,11... | collective-permute-start | bytes 4128776 | tf_op jit(solution)/shard_map/ppermute | solution.py:168
  2.7 3.7 %collective-permute-start.1 = (bf16[64,1024]{1,0:T(8,128)(2,1)S(1)}, bf16[64,1024]{1,0:T(8,128)(2,1)S(1)}, u32[]{:S(2)}, u32[]{:S(2)}) collective-permute-start(bf16[64,1024]{1,0:T(8,128)(2,1)S(1)} %get-tuple-element.25), channel_id=1, source_target_pairs={{0,8},{1,10},{4,12},{5,14},{8,0},{9,2},{12,4},{13,6},{2,9},{3,11},... | collective-permute-start | bytes 393224 | tf_op jit(solution)/shard_map/ppermute | solution.py:165
  6.4 1.6 %collective-permute-start.5 = (bf16[64,1024]{1,0:T(8,128)(2,1)S(1)}, bf16[64,1024]{1,0:T(8,128)(2,1)S(1)}, u32[]{:S(2)}, u32[]{:S(2)}) collective-permute-start(bf16[64,1024]{1,0:T(8,128)(2,1)S(1)} %get-tuple-element.25), channel_id=1, source_target_pairs={{0,4},{1,6},{4,0},{5,2},{8,12},{9,14},{12,8},{13,10},{2,5},{3,7},{... | collective-permute-start | bytes 393224 | tf_op jit(solution)/shard_map/ppermute | solution.py:165
  7.9 0.7 %collective-permute-start = (bf16[64,1024]{1,0:T(8,128)(2,1)S(1)}, bf16[64,1024]{1,0:T(8,128)(2,1)S(1)}, u32[]{:S(2)}, u32[]{:S(2)}) collective-permute-start(bf16[64,1024]{1,0:T(8,128)(2,1)S(1)} %get-tuple-element.25), channel_id=1, source_target_pairs={{0,0},{1,2},{4,4},{5,6},{8,8},{9,10},{12,12},{13,14},{2,1},{3,3},{... | collective-permute-start | bytes 393224 | tf_op jit(solution)/shard_map/ppermute | solution.py:165
  8.6 4.4 %collective-permute-done.1.refs_1_.refs_8_ = bf16[64,1024]{1,0:T(8,128)(2,1)S(1)} collective-permute-done((bf16[64,1024]{1,0:T(8,128)(2,1)S(1)}, bf16[64,1024]{1,0:T(8,128)(2,1)S(1)}, u32[]{:S(2)}, u32[]{:S(2)}) %collective-permute-start.1) | collective-permute-done | bytes 131104 | tf_op jit(solution)/shard_map/ppermute | solution.py:165
  13.0 1.5 %collective-permute-start.2 = (bf16[64,1024]{1,0:T(8,128)(2,1)S(1)}, bf16[64,1024]{1,0:T(8,128)(2,1)S(1)}, u32[]{:S(2)}, u32[]{:S(2)}) collective-permute-start(bf16[64,1024]{1,0:T(8,128)(2,1)S(1)} %collective-permute-done.1.refs_1_.refs_8_), channel_id=1, source_target_pairs={{0,4},{4,0},{8,12},{12,8},{1,5},{5,1},{9,13},{13,9},{2,6},{6,2},{1... | collective-permute-start | bytes 393224 | tf_op jit(solution)/shard_map/ppermute | solution.py:179
  14.5 0.0 collective-permute-done.5.refs_0_.refs_7_
  14.5 0.0 collective-permute-done.3.refs_3_
  14.5 0.9 %shard_map.104 = (f32[672,128]{1,0:T(8,128)S(1)}, bf16[672,128]{1,0:T(8,128)(2,1)S(1)}) custom-call(bf16[64,1024]{1,0:T(8,128)(2,1)S(1)} %collective-permute-done.5.refs_0_.refs_7_, bf16[64,1024]{1,0:T(8,128)(2,1)S(1)} %collective-permute-done.1.refs_1_.refs_8_, bf16[672,1024]{1,0:T(8,128)(2,1)S(1)} %get-tuple-element.26.refs_2_, ...), custom_call_target="tpu_custom_call" | custom-call | flops 176160768 | bytes 3530752 | tf_op jit(solution)/shard_map/pallas_call | solution.py:29
  15.4 1.2 %collective-permute-start.6 = (bf16[672,128]{1,0:T(8,128)(2,1)S(1)}, bf16[672,128]{1,0:T(8,128)(2,1)S(1)}, u32[]{:S(2)}, u32[]{:S(2)}) collective-permute-start(bf16[672,128]{1,0:T(8,128)(2,1)S(1)} %get-tuple-element.30), channel_id=1, source_target_pairs={{0,2},{2,0},{1,3},{3,1},{4,6},{6,4},{5,7},{7,5},{8,10},{10,8},{9,1... | collective-permute-start | bytes 516104 | tf_op jit(solution)/shard_map/ppermute | solution.py:168
  16.6 2.5 %collective-permute-done.2.refs_1_.refs_10_ = bf16[64,1024]{1,0:T(8,128)(2,1)S(1)} collective-permute-done((bf16[64,1024]{1,0:T(8,128)(2,1)S(1)}, bf16[64,1024]{1,0:T(8,128)(2,1)S(1)}, u32[]{:S(2)}, u32[]{:S(2)}) %collective-permute-start.2) | collective-permute-done | bytes 131104 | tf_op jit(solution)/shard_map/ppermute | solution.py:179
  19.1 0.9 %shard_map.103 = (f32[672,128]{1,0:T(8,128)S(1)}, bf16[672,128]{1,0:T(8,128)(2,1)S(1)}) custom-call(bf16[64,1024]{1,0:T(8,128)(2,1)S(1)} %collective-permute-done.refs_0_.refs_9_, bf16[64,1024]{1,0:T(8,128)(2,1)S(1)} %collective-permute-done.2.refs_1_.refs_10_, bf16[672,1024]{1,0:T(8,128)(2,1)S(1)} %get-tuple-element.26.refs_2_, ...), custom_call_target="tpu_custom_call" | custom-call | flops 176160768 | bytes 3530752 | tf_op jit(solution)/shard_map/pallas_call | solution.py:29
  20.0 1.2 %collective-permute-start.4 = (bf16[672,128]{1,0:T(8,128)(2,1)S(1)}, bf16[672,128]{1,0:T(8,128)(2,1)S(1)}, u32[]{:S(2)}, u32[]{:S(2)}) collective-permute-start(bf16[672,128]{1,0:T(8,128)(2,1)S(1)} %get-tuple-element.28), channel_id=1, source_target_pairs={{0,2},{2,0},{1,3},{3,1},{4,6},{6,4},{5,7},{7,5},{8,10},{10,8},{9,1... | collective-permute-start | bytes 516104 | tf_op jit(solution)/shard_map/ppermute | solution.py:168
  21.2 0.6 %collective-permute-done.6.refs_1_ = bf16[672,128]{1,0:T(8,128)(2,1)S(1)} collective-permute-done((bf16[672,128]{1,0:T(8,128)(2,1)S(1)}, bf16[672,128]{1,0:T(8,128)(2,1)S(1)}, u32[]{:S(2)}, u32[]{:S(2)}) %collective-permute-start.6) | collective-permute-done | bytes 172064 | tf_op jit(solution)/shard_map/ppermute | solution.py:168
  21.8 0.5 %shard_map.105 = (bf16[672,128]{1,0:T(8,128)(2,1)S(1)}, bf16[32,1024]{1,0:T(8,128)(2,1)S(1)}, bf16[32,1024]{1,0:T(8,128)(2,1)S(1)}) custom-call(f32[672,128]{1,0:T(8,128)S(1)} %get-tuple-element.29.refs_0_, bf16[672,128]{1,0:T(8,128)(2,1)S(1)} %collective-permute-done.6.refs_1_, bf16[672,1024]{1,0:T(8,128)(2,1)S(1)} %get-tuple-element.26.refs_2_, ...), custom_call_target="tpu_custom_call" | custom-call | flops 234881024 | bytes 3571712 | tf_op jit(solution)/shard_map/pallas_call | solution.py:29
  22.3 4.4 %collective-permute-done.4.refs_1_ = bf16[672,128]{1,0:T(8,128)(2,1)S(1)} collective-permute-done((bf16[672,128]{1,0:T(8,128)(2,1)S(1)}, bf16[672,128]{1,0:T(8,128)(2,1)S(1)}, u32[]{:S(2)}, u32[]{:S(2)}) %collective-permute-start.4) | collective-permute-done | bytes 172064 | tf_op jit(solution)/shard_map/ppermute | solution.py:168
  26.8 0.5 %shard_map.106 = (bf16[672,256]{1,0:T(8,128)(2,1)S(1)}, bf16[256,1024]{1,0:T(8,128)(2,1)S(1)}, bf16[32,1024]{1,0:T(8,128)(2,1)S(1)}, bf16[32,1024]{1,0:T(8,128)(...) custom-call(f32[672,128]{1,0:T(8,128)S(1)} %get-tuple-element.27.refs_4_.refs_0_, ...), custom_call_target="tpu_custom_call" | custom-call | flops 234881024 | bytes 5226496 | tf_op jit(solution)/shard_map/pallas_call | solution.py:29
  27.3 0.1 collective-permute-start.11
  27.4 0.5 %collective-permute-start.12 = (bf16[672,256]{1,0:T(8,128)(2,1)S(1)}, bf16[672,256]{1,0:T(8,128)(2,1)S(1)}, u32[]{:S(2)}, u32[]{:S(2)}) collective-permute-start(bf16[672,256]{1,0:T(8,128)(2,1)S(1)} %get-tuple-element.39.refs_2_), channel_id=1, source_target_pairs={{0,1},{1,0},{2,3},{3,2},{4,5},{5,4},{6,7},{7,6},{8,9},{9,8},{10,11... | collective-permute-start | bytes 1032200 | tf_op jit(solution)/shard_map/ppermute | solution.py:168
  27.9 2.0 %collective-permute-start.7 = (bf16[32,1024]{1,0:T(8,128)(2,1)S(1)}, bf16[32,1024]{1,0:T(8,128)(2,1)S(1)}, u32[]{:S(2)}, u32[]{:S(2)}) collective-permute-start(bf16[32,1024]{1,0:T(8,128)(2,1)S(1)} %get-tuple-element.34), channel_id=1, source_target_pairs={{0,8},{1,10},{4,12},{5,14},{8,0},{9,2},{12,4},{13,6},{2,9},{3,11},... | collective-permute-start | bytes 196616 | tf_op jit(solution)/shard_map/ppermute | solution.py:165
  29.9 0.8 %collective-permute-start.8 = (bf16[32,1024]{1,0:T(8,128)(2,1)S(1)}, bf16[32,1024]{1,0:T(8,128)(2,1)S(1)}, u32[]{:S(2)}, u32[]{:S(2)}) collective-permute-start(bf16[32,1024]{1,0:T(8,128)(2,1)S(1)} %get-tuple-element.35), channel_id=1, source_target_pairs={{0,12},{1,14},{4,8},{5,10},{8,4},{9,6},{12,0},{13,2},{2,13},{3,15}... | collective-permute-start | bytes 196616 | tf_op jit(solution)/shard_map/ppermute | solution.py:165
  30.8 0.6 %collective-permute-start.9 = (bf16[32,1024]{1,0:T(8,128)(2,1)S(1)}, bf16[32,1024]{1,0:T(8,128)(2,1)S(1)}, u32[]{:S(2)}, u32[]{:S(2)}) collective-permute-start(bf16[32,1024]{1,0:T(8,128)(2,1)S(1)} %get-tuple-element.36), channel_id=1, source_target_pairs={{0,4},{1,6},{4,0},{5,2},{8,12},{9,14},{12,8},{13,10},{2,5},{3,7},{... | collective-permute-start | bytes 196616 | tf_op jit(solution)/shard_map/ppermute | solution.py:165
  31.4 0.0 collective-permute-done.12.refs_3_
  31.4 0.7 %collective-permute-start.10 = (bf16[32,1024]{1,0:T(8,128)(2,1)S(1)}, bf16[32,1024]{1,0:T(8,128)(2,1)S(1)}, u32[]{:S(2)}, u32[]{:S(2)}) collective-permute-start(bf16[32,1024]{1,0:T(8,128)(2,1)S(1)} %get-tuple-element.37), channel_id=1, source_target_pairs={{0,0},{1,2},{4,4},{5,6},{8,8},{9,10},{12,12},{13,14},{2,1},{3,3},{... | collective-permute-start | bytes 196616 | tf_op jit(solution)/shard_map/ppermute | solution.py:165
  32.0 0.0 collective-permute-done.11.refs_1_
  32.1 1.8 %shard_map.107 = (bf16[224,1024]{1,0:T(8,128)(2,1)}, bf16[224,1024]{1,0:T(8,128)(2,1)}, bf16[224,1024]{1,0:T(8,128)(2,1)}, f32[8,128]{1,0:T(8,128)S(1)}) custom-call(bf16[256,1024]{1,0:T(8,128)(2,1)S(1)} %get-tuple-element.38.refs_0_, bf16[256,1024]{1,0:T(8,128)(2,1)S(1)} %collective-permute-done.11.refs_1_, bf16[672,256]{1,0:T(8,128)(2,1)S(1)} %get-tuple-element.39.refs_2_, ...), custom_call_target="tpu_custom_call" | custom-call | flops 352321536 | bytes 3117056 | tf_op jit(solution)/shard_map/pallas_call | solution.py:29
  33.8 0.5 %collective-permute-done.7.refs_1_ = bf16[32,1024]{1,0:T(8,128)(2,1)S(1)} collective-permute-done((bf16[32,1024]{1,0:T(8,128)(2,1)S(1)}, bf16[32,1024]{1,0:T(8,128)(2,1)S(1)}, u32[]{:S(2)}, u32[]{:S(2)}) %collective-permute-start.7) | collective-permute-done | bytes 65568 | tf_op jit(solution)/shard_map/ppermute | solution.py:165
  34.3 2.5 %collective-permute-done.8.refs_2_ = bf16[32,1024]{1,0:T(8,128)(2,1)S(1)} collective-permute-done((bf16[32,1024]{1,0:T(8,128)(2,1)S(1)}, bf16[32,1024]{1,0:T(8,128)(2,1)S(1)}, u32[]{:S(2)}, u32[]{:S(2)}) %collective-permute-start.8) | collective-permute-done | bytes 65568 | tf_op jit(solution)/shard_map/ppermute | solution.py:165
  36.8 0.3 collective-permute-done.9.refs_3_
  37.1 0.0 collective-permute-done.10.refs_4_
  37.1 1.0 %shard_map.108 = bf16[128,1024]{1,0:T(8,128)(2,1)} custom-call(bf16[32,128]{1,0:T(8,128)(2,1)S(1)} %get-tuple-element.24.refs_0_, bf16[32,1024]{1,0:T(8,128)(2,1)S(1)} %collective-permute-done.7.refs_1_, bf16[32,1024]{1,0:T(8,128)(2,1)S(1)} %collective-permute-done.8.refs_2_, bf16[32,1024]{1,0:T(8,128)(2,1)S(1)} %collective-permute-done.9.refs_3_, ...), custom_call_target="tpu_custom_call" | custom-call | bytes 532480 | tf_op jit(solution)/shard_map/pallas_call | solution.py:29
  (1 shorter events, 0.0 us)
Async XLA Ops:
  2.2 12.3 %collective-permute-start.3 = (bf16[672,1024]{1,0:T(8,128)(2,1)S(1)}, bf16[672,1024]{1,0:T(8,128)(2,1)S(1)}, u32[]{:S(2)}, u32[]{:S(2)}) collective-permute-start(bf16[672,1024]{1,0:T(8,128)(2,1)S(1)} %get-tuple-element.26.refs_2_), channel_id=1, source_target_pairs={{0,1},{1,0},{2,3},{3,2},{4,5},{5,4},{6,7},{7,6},{8,9},{9,8},{10,11... | collective-permute-start | bytes 4128776 | tf_op jit(solution)/shard_map/ppermute | solution.py:168
  2.7 10.3 %collective-permute-start.1 = (bf16[64,1024]{1,0:T(8,128)(2,1)S(1)}, bf16[64,1024]{1,0:T(8,128)(2,1)S(1)}, u32[]{:S(2)}, u32[]{:S(2)}) collective-permute-start(bf16[64,1024]{1,0:T(8,128)(2,1)S(1)} %get-tuple-element.25), channel_id=1, source_target_pairs={{0,8},{1,10},{4,12},{5,14},{8,0},{9,2},{12,4},{13,6},{2,9},{3,11},... | collective-permute-start | bytes 393224 | tf_op jit(solution)/shard_map/ppermute | solution.py:165
  6.4 8.1 %collective-permute-start.5 = (bf16[64,1024]{1,0:T(8,128)(2,1)S(1)}, bf16[64,1024]{1,0:T(8,128)(2,1)S(1)}, u32[]{:S(2)}, u32[]{:S(2)}) collective-permute-start(bf16[64,1024]{1,0:T(8,128)(2,1)S(1)} %get-tuple-element.25), channel_id=1, source_target_pairs={{0,4},{1,6},{4,0},{5,2},{8,12},{9,14},{12,8},{13,10},{2,5},{3,7},{... | collective-permute-start | bytes 393224 | tf_op jit(solution)/shard_map/ppermute | solution.py:165
  7.9 8.7 %collective-permute-start = (bf16[64,1024]{1,0:T(8,128)(2,1)S(1)}, bf16[64,1024]{1,0:T(8,128)(2,1)S(1)}, u32[]{:S(2)}, u32[]{:S(2)}) collective-permute-start(bf16[64,1024]{1,0:T(8,128)(2,1)S(1)} %get-tuple-element.25), channel_id=1, source_target_pairs={{0,0},{1,2},{4,4},{5,6},{8,8},{9,10},{12,12},{13,14},{2,1},{3,3},{... | collective-permute-start | bytes 393224 | tf_op jit(solution)/shard_map/ppermute | solution.py:165
  13.0 6.1 %collective-permute-start.2 = (bf16[64,1024]{1,0:T(8,128)(2,1)S(1)}, bf16[64,1024]{1,0:T(8,128)(2,1)S(1)}, u32[]{:S(2)}, u32[]{:S(2)}) collective-permute-start(bf16[64,1024]{1,0:T(8,128)(2,1)S(1)} %collective-permute-done.1.refs_1_.refs_8_), channel_id=1, source_target_pairs={{0,4},{4,0},{8,12},{12,8},{1,5},{5,1},{9,13},{13,9},{2,6},{6,2},{1... | collective-permute-start | bytes 393224 | tf_op jit(solution)/shard_map/ppermute | solution.py:179
  15.4 6.3 %collective-permute-start.6 = (bf16[672,128]{1,0:T(8,128)(2,1)S(1)}, bf16[672,128]{1,0:T(8,128)(2,1)S(1)}, u32[]{:S(2)}, u32[]{:S(2)}) collective-permute-start(bf16[672,128]{1,0:T(8,128)(2,1)S(1)} %get-tuple-element.30), channel_id=1, source_target_pairs={{0,2},{2,0},{1,3},{3,1},{4,6},{6,4},{5,7},{7,5},{8,10},{10,8},{9,1... | collective-permute-start | bytes 516104 | tf_op jit(solution)/shard_map/ppermute | solution.py:168
  20.0 6.8 %collective-permute-start.4 = (bf16[672,128]{1,0:T(8,128)(2,1)S(1)}, bf16[672,128]{1,0:T(8,128)(2,1)S(1)}, u32[]{:S(2)}, u32[]{:S(2)}) collective-permute-start(bf16[672,128]{1,0:T(8,128)(2,1)S(1)} %get-tuple-element.28), channel_id=1, source_target_pairs={{0,2},{2,0},{1,3},{3,1},{4,6},{6,4},{5,7},{7,5},{8,10},{10,8},{9,1... | collective-permute-start | bytes 516104 | tf_op jit(solution)/shard_map/ppermute | solution.py:168
  27.3 4.7 %collective-permute-start.11 = (bf16[256,1024]{1,0:T(8,128)(2,1)S(1)}, bf16[256,1024]{1,0:T(8,128)(2,1)S(1)}, u32[]{:S(2)}, u32[]{:S(2)}) collective-permute-start(bf16[256,1024]{1,0:T(8,128)(2,1)S(1)} %get-tuple-element.38.refs_0_), channel_id=1, source_target_pairs={{0,1},{1,0},{2,3},{3,2},{4,5},{5,4},{6,7},{7,6},{8,9},{9,8},{10,11... | collective-permute-start | bytes 1572872 | tf_op jit(solution)/shard_map/ppermute | solution.py:168
  27.4 4.0 %collective-permute-start.12 = (bf16[672,256]{1,0:T(8,128)(2,1)S(1)}, bf16[672,256]{1,0:T(8,128)(2,1)S(1)}, u32[]{:S(2)}, u32[]{:S(2)}) collective-permute-start(bf16[672,256]{1,0:T(8,128)(2,1)S(1)} %get-tuple-element.39.refs_2_), channel_id=1, source_target_pairs={{0,1},{1,0},{2,3},{3,2},{4,5},{5,4},{6,7},{7,6},{8,9},{9,8},{10,11... | collective-permute-start | bytes 1032200 | tf_op jit(solution)/shard_map/ppermute | solution.py:168
  27.9 6.4 %collective-permute-start.7 = (bf16[32,1024]{1,0:T(8,128)(2,1)S(1)}, bf16[32,1024]{1,0:T(8,128)(2,1)S(1)}, u32[]{:S(2)}, u32[]{:S(2)}) collective-permute-start(bf16[32,1024]{1,0:T(8,128)(2,1)S(1)} %get-tuple-element.34), channel_id=1, source_target_pairs={{0,8},{1,10},{4,12},{5,14},{8,0},{9,2},{12,4},{13,6},{2,9},{3,11},... | collective-permute-start | bytes 196616 | tf_op jit(solution)/shard_map/ppermute | solution.py:165
  29.9 6.9 %collective-permute-start.8 = (bf16[32,1024]{1,0:T(8,128)(2,1)S(1)}, bf16[32,1024]{1,0:T(8,128)(2,1)S(1)}, u32[]{:S(2)}, u32[]{:S(2)}) collective-permute-start(bf16[32,1024]{1,0:T(8,128)(2,1)S(1)} %get-tuple-element.35), channel_id=1, source_target_pairs={{0,12},{1,14},{4,8},{5,10},{8,4},{9,6},{12,0},{13,2},{2,13},{3,15}... | collective-permute-start | bytes 196616 | tf_op jit(solution)/shard_map/ppermute | solution.py:165
  30.8 6.4 %collective-permute-start.9 = (bf16[32,1024]{1,0:T(8,128)(2,1)S(1)}, bf16[32,1024]{1,0:T(8,128)(2,1)S(1)}, u32[]{:S(2)}, u32[]{:S(2)}) collective-permute-start(bf16[32,1024]{1,0:T(8,128)(2,1)S(1)} %get-tuple-element.36), channel_id=1, source_target_pairs={{0,4},{1,6},{4,0},{5,2},{8,12},{9,14},{12,8},{13,10},{2,5},{3,7},{... | collective-permute-start | bytes 196616 | tf_op jit(solution)/shard_map/ppermute | solution.py:165
  31.4 5.8 %collective-permute-start.10 = (bf16[32,1024]{1,0:T(8,128)(2,1)S(1)}, bf16[32,1024]{1,0:T(8,128)(2,1)S(1)}, u32[]{:S(2)}, u32[]{:S(2)}) collective-permute-start(bf16[32,1024]{1,0:T(8,128)(2,1)S(1)} %get-tuple-element.37), channel_id=1, source_target_pairs={{0,0},{1,2},{4,4},{5,6},{8,8},{9,10},{12,12},{13,14},{2,1},{3,3},{... | collective-permute-start | bytes 196616 | tf_op jit(solution)/shard_map/ppermute | solution.py:165

commit v6 on v5

--- a/solution.py
+++ b/solution.py
@@ -74,23 +74,22 @@
         c.wait()
 
 
-def partial_body(blocks, *refs):
-    w_own, w_oth, keep_ref = refs[blocks : blocks + 3]
+def partial_body(blocks, rows, *refs):
+    w_own, w_oth, keep_ref, send_ref = refs[blocks : blocks + 4]
     h = w_own.shape[0] // 3
-    x = jnp.concatenate([r[0:MOST] for r in refs[:blocks]], axis=0)
-    dz = jnp.concatenate([r[MOST:] for r in refs[:blocks]], axis=0)
-    for at, a in ((slice(0, 2 * h), x), (slice(2 * h, 3 * h), dz)):
-        keep_ref[at] = jnp.concatenate([dot(w[at], a, NT) for w in (w_own, w_oth)], axis=1)
     done = 0
-    for send_ref in refs[blocks + 3 :]:
-        send_ref[...] = keep_ref[done : done + send_ref.shape[0]].astype(BF)
-        done += send_ref.shape[0]
+    for at, half in rows:
+        a = jnp.concatenate([r[half * MOST : (half + 1) * MOST] for r in refs[:blocks]], axis=0)
+        part = jnp.concatenate([dot(w[at[0] * h : at[1] * h], a, NT) for w in (w_own, w_oth)], axis=1)
+        keep_ref[done : done + part.shape[0]] = part
+        send_ref[done : done + part.shape[0]] = part.astype(BF)
+        done += part.shape[0]
 
 
 def terms(keep, recv, dd_ref):
-    h = keep.shape[0] // 3
-    got = jnp.concatenate([r[...] for r in recv], axis=0).astype(F32)
-    gate, upper, d_act = (keep[i * h : (i + 1) * h] + got[i * h : (i + 1) * h] for i in range(3))
+    both = [jnp.concatenate([r[...].astype(F32) for r in refs], axis=0) for refs in (keep, recv)]
+    h = both[0].shape[0] // 3
+    gate, upper, d_act = (both[0][i * h : (i + 1) * h] + both[1][i * h : (i + 1) * h] for i in range(3))
     sigma = jax.nn.sigmoid(gate)
     gs = gate * sigma
     dd_ref[0:h] = (d_act * upper * sigma * (1.0 + gate * (1.0 - sigma))).astype(BF)
@@ -106,17 +105,19 @@
         ref[...] = total[s * MOST : (s + 1) * MOST].astype(BF)
 
 
-def first_body(recv, keep, *refs):
-    w_own, w_oth, dd_ref, *dx_refs = refs[recv:]
-    terms(keep, refs[:recv], dd_ref)
+def first_body(parts, *refs):
+    w_own, w_oth, dd_ref, *dx_refs = refs[2 * parts :]
+    terms(refs[:parts], refs[parts : 2 * parts], dd_ref)
     back_rows(dd_ref, w_own, w_oth, dx_refs)
 
 
-def second_body(blocks, keep, recv, w_own, w_oth, dd_a, *refs):
+def second_body(blocks, parts, *refs):
+    keep, recv = refs[:parts], refs[parts : 2 * parts]
+    w_own, w_oth, dd_a, *refs = refs[2 * parts :]
     early, refs = refs[: blocks // 2], refs[blocks // 2 :]
     dd_ref, rows_ref, *dx_refs = refs[blocks:]
     m = dd_a.shape[1]
-    terms(keep, [recv], dd_ref.at[:, m:])
+    terms(keep, recv, dd_ref.at[:, m:])
     back_rows(dd_ref.at[:, m:], w_own, w_oth, dx_refs[len(early) :])
     for a, ref in zip(early, dx_refs):
         ref[...] = a[...]
@@ -180,25 +181,30 @@
     w_oth = swap(w_own, "tensor")
     flops = 2 * m * half * h
 
-    def partial(group, parts, after=()):
-        keep, *send = call(
-            functools.partial(partial_body, len(group)),
-            [arr((3 * h, 2 * m), F32)] + [arr((p * h, 2 * m)) for p in parts],
-            *(blocks[s] for s in group), w_own, w_oth, flops=6 * flops, after=after,
-        )
-        return keep, [swap(b, "dp") for b in send]
+    def partial(group, *parts):
+        keep, send = [], []
+        for rows in parts:
+            size = sum(at[1] - at[0] for at, _ in rows) * h
+            a, b = call(
+                functools.partial(partial_body, len(group), rows), [arr((size, 2 * m), F32), arr((size, 2 * m))],
+                *(blocks[s] for s in group), w_own, w_oth, flops=6 * flops, after=keep[-1:],
+            )
+            keep.append(a)
+            send.append(swap(b, "dp"))
+        return keep, send
 
     near, far = (1, 2), (0, 3)
+    products, slopes = ((0, 2), 0), ((2, 3), 1)
     dx = [arr((MOST, half))] * (n // 2)
-    keep_a, recv_a = partial(near, (3,))
-    keep_b, recv_b = partial(far, (3,))
+    keep_a, recv_a = partial(near, (products, slopes))
+    keep_b, recv_b = partial(far, (products,), (slopes,))
     dd_a, *dx_a = call(
-        functools.partial(first_body, len(recv_a)), [arr((3 * h, 2 * m))] + dx,
-        keep_a, *recv_a, w_own, w_oth, flops=8 * flops, after=(keep_b,),
+        functools.partial(first_body, len(keep_a)), [arr((3 * h, 2 * m))] + dx,
+        *keep_a, *recv_a, w_own, w_oth, flops=8 * flops, after=keep_b[-1:],
     )
     own, rows_own, *dx = call(
-        functools.partial(second_body, n), [arr((3 * h, 4 * m)), arr((2 * n * MOST, half))] + dx * 2,
-        keep_b, *recv_b, w_own, w_oth, dd_a, *dx_a, *(blocks[s] for s in (*near, *far)), flops=8 * flops,
+        functools.partial(second_body, n, len(keep_b)), [arr((3 * h, 4 * m)), arr((2 * n * MOST, half))] + dx * 2,
+        *keep_b, *recv_b, w_own, w_oth, dd_a, *dx_a, *(blocks[s] for s in (*near, *far)), flops=8 * flops,
     )
     back = {s: across(b, s) for s, b in zip((*near, *far), dx)}
     rows_oth, oth = swap(rows_own, "tensor"), swap(own, "tensor")

time: 38.3 us -> 38.2 us (level)
  waiting for transfers between devices: 15.2 us -> 13.9 us
  starting transfers between devices: 15 us -> 15.9 us
    ppermute x5 -> x6, waiting for transfers between devices: 5.07 us -> 3.64 us  [swap(): return lax.ppermute(x, axis, [(0, 1), (1, 0)])]
    ppermute x5 -> x6, starting transfers between devices: 3.42 us -> 4.4 us  [swap(): return lax.ppermute(x, axis, [(0, 1), (1, 0)])]
    pallas_call x7 -> x8, Pallas kernels: 7.2 us -> 7.44 us  [call(): pl.pallas_call(run, out_shape=outs, in_specs=[pl.BlockSpec(memory_space=p...]
  transfers between devices with their start and end apart: 13 -> 14, of which waited for: 7 -> 6; matrix products, arithmetic and copies ran while one was open for 0% -> 0% of each run, Pallas kernels for 11% -> 12%
where the time goes in v6:
time: 38.2 us; the launch traced here: 38 us
  starting transfers between devices  15.9 us (42%)
  waiting for transfers between devices  13.9 us (36%)
  Pallas kernels  7.44 us (19%)
  between operations  0.72 us (2%)
    ppermute x7, starting transfers between devices, across(): return lax.ppermute(x, ('seq', 'dp', 'tensor'), pairs)  10 us
    ppermute x7, waiting for transfers between devices, across(): return lax.ppermute(x, ('seq', 'dp', 'tensor'), pairs)  7.79 us
    pallas_call x8, Pallas kernels, call(): pl.pallas_call(run, out_shape=outs, in_specs=[pl.BlockSpec(memory_space=p...  7.44 us
    ppermute x6, starting transfers between devices, swap(): return lax.ppermute(x, axis, [(0, 1), (1, 0)])  4.4 us
    ppermute x6, waiting for transfers between devices, swap(): return lax.ppermute(x, axis, [(0, 1), (1, 0)])  3.64 us
    ppermute x1, waiting for transfers between devices, swapped(): blocks[3] = lax.ppermute(blocks[2], 'seq', [(k, k ^ 1) for k in range(n)])  2.46 us
    ppermute x1, starting transfers between devices, swapped(): blocks[3] = lax.ppermute(blocks[2], 'seq', [(k, k ^ 1) for k in range(n)])  1.5 us
  transfers between devices with their start and end apart: 14, of which 6 were waited for; matrix products, arithmetic and copies ran while one was open for 0% of the time, Pallas kernels for 12%

profile of v6, /device:TPU:0, one launch (start us, length us, event | category | flops | bytes accessed | tf_op | source)
XLA Modules:
  0.0 38.0 jit_solution(6137162050980637103)
XLA Ops:
  0.6 1.5 %shard_map.102 = (bf16[64,1024]{1,0:T(8,128)(2,1)S(1)}, bf16[32,128]{1,0:T(8,128)(2,1)S(1)}, bf16[672,1024]{1,0:T(8,128)(2,1)S(1)}) custom-call(s32[1,64]{1,0:T(1,128)} %refs_0_.1, f32[1,64]{1,0:T(1,128)} %refs_1_.1, bf16[128,1024]{1,0:T(8,128)(2,1)} %bitcast.9, bf16[128,1024]{1,0:T(8,128)(2,1)} %bitcast.10, bf16[224,1024]{1,0:T(8,128)(2,1)} %bitcast.7, ...), custom_call_target="tpu_custom_call" | custom-call | bytes 3416576 | tf_op jit(solution)/shard_map/pallas_call | solution.py:29
  2.2 0.5 %collective-permute-start.3 = (bf16[672,1024]{1,0:T(8,128)(2,1)S(1)}, bf16[672,1024]{1,0:T(8,128)(2,1)S(1)}, u32[]{:S(2)}, u32[]{:S(2)}) collective-permute-start(bf16[672,1024]{1,0:T(8,128)(2,1)S(1)} %get-tuple-element.28.refs_2_.refs_4_), channel_id=1, source_target_pairs={{0,1},{1,0},{2,3},{3,2},{4,5},{5,4},{6,7},{7,6},{8,9},{9,8},{10,11... | collective-permute-start | bytes 4128776 | tf_op jit(solution)/shard_map/ppermute | solution.py:169
  2.7 3.7 %collective-permute-start.1 = (bf16[64,1024]{1,0:T(8,128)(2,1)S(1)}, bf16[64,1024]{1,0:T(8,128)(2,1)S(1)}, u32[]{:S(2)}, u32[]{:S(2)}) collective-permute-start(bf16[64,1024]{1,0:T(8,128)(2,1)S(1)} %get-tuple-element.27), channel_id=1, source_target_pairs={{0,8},{1,10},{4,12},{5,14},{8,0},{9,2},{12,4},{13,6},{2,9},{3,11},... | collective-permute-start | bytes 393224 | tf_op jit(solution)/shard_map/ppermute | solution.py:166
  6.4 1.6 %collective-permute-start.6 = (bf16[64,1024]{1,0:T(8,128)(2,1)S(1)}, bf16[64,1024]{1,0:T(8,128)(2,1)S(1)}, u32[]{:S(2)}, u32[]{:S(2)}) collective-permute-start(bf16[64,1024]{1,0:T(8,128)(2,1)S(1)} %get-tuple-element.27), channel_id=1, source_target_pairs={{0,4},{1,6},{4,0},{5,2},{8,12},{9,14},{12,8},{13,10},{2,5},{3,7},{... | collective-permute-start | bytes 393224 | tf_op jit(solution)/shard_map/ppermute | solution.py:166
  7.9 0.7 %collective-permute-start = (bf16[64,1024]{1,0:T(8,128)(2,1)S(1)}, bf16[64,1024]{1,0:T(8,128)(2,1)S(1)}, u32[]{:S(2)}, u32[]{:S(2)}) collective-permute-start(bf16[64,1024]{1,0:T(8,128)(2,1)S(1)} %get-tuple-element.27), channel_id=1, source_target_pairs={{0,0},{1,2},{4,4},{5,6},{8,8},{9,10},{12,12},{13,14},{2,1},{3,3},{... | collective-permute-start | bytes 393224 | tf_op jit(solution)/shard_map/ppermute | solution.py:166
  8.6 4.4 %collective-permute-done.1.refs_1_.refs_10_ = bf16[64,1024]{1,0:T(8,128)(2,1)S(1)} collective-permute-done((bf16[64,1024]{1,0:T(8,128)(2,1)S(1)}, bf16[64,1024]{1,0:T(8,128)(2,1)S(1)}, u32[]{:S(2)}, u32[]{:S(2)}) %collective-permute-start.1) | collective-permute-done | bytes 131104 | tf_op jit(solution)/shard_map/ppermute | solution.py:166
  13.0 1.5 %collective-permute-start.2 = (bf16[64,1024]{1,0:T(8,128)(2,1)S(1)}, bf16[64,1024]{1,0:T(8,128)(2,1)S(1)}, u32[]{:S(2)}, u32[]{:S(2)}) collective-permute-start(bf16[64,1024]{1,0:T(8,128)(2,1)S(1)} %collective-permute-done.1.refs_1_.refs_10_), channel_id=1, source_target_pairs={{0,4},{4,0},{8,12},{12,8},{1,5},{5,1},{9,13},{13,9},{2,6},{6,2},{1... | collective-permute-start | bytes 393224 | tf_op jit(solution)/shard_map/ppermute | solution.py:180
  14.5 0.0 collective-permute-done.3.refs_3_.refs_5_
  14.5 0.9 %shard_map.105 = (f32[672,128]{1,0:T(8,128)S(1)}, bf16[672,128]{1,0:T(8,128)(2,1)S(1)}) custom-call(bf16[64,1024]{1,0:T(8,128)(2,1)S(1)} %collective-permute-done.6.refs_0_.refs_9_, bf16[64,1024]{1,0:T(8,128)(2,1)S(1)} %collective-permute-done.1.refs_1_.refs_10_, bf16[672,1024]{1,0:T(8,128)(2,1)S(1)} %get-tuple-element.28.refs_2_.refs_4_, ...), custom_call_target="tpu_custom_call" | custom-call | flops 176160768 | bytes 3530752 | tf_op jit(solution)/shard_map/pallas_call | solution.py:29
  15.4 1.2 %collective-permute-start.7 = (bf16[672,128]{1,0:T(8,128)(2,1)S(1)}, bf16[672,128]{1,0:T(8,128)(2,1)S(1)}, u32[]{:S(2)}, u32[]{:S(2)}) collective-permute-start(bf16[672,128]{1,0:T(8,128)(2,1)S(1)} %get-tuple-element.34), channel_id=1, source_target_pairs={{0,2},{2,0},{1,3},{3,1},{4,6},{6,4},{5,7},{7,5},{8,10},{10,8},{9,1... | collective-permute-start | bytes 516104 | tf_op jit(solution)/shard_map/ppermute | solution.py:169
  16.6 2.5 %collective-permute-done.2.refs_1_.refs_12_ = bf16[64,1024]{1,0:T(8,128)(2,1)S(1)} collective-permute-done((bf16[64,1024]{1,0:T(8,128)(2,1)S(1)}, bf16[64,1024]{1,0:T(8,128)(2,1)S(1)}, u32[]{:S(2)}, u32[]{:S(2)}) %collective-permute-start.2) | collective-permute-done | bytes 131104 | tf_op jit(solution)/shard_map/ppermute | solution.py:180
  19.1 0.7 %shard_map.103 = (f32[448,128]{1,0:T(8,128)S(1)}, bf16[448,128]{1,0:T(8,128)(2,1)S(1)}) custom-call(bf16[64,1024]{1,0:T(8,128)(2,1)S(1)} %collective-permute-done.refs_0_.refs_11_, bf16[64,1024]{1,0:T(8,128)(2,1)S(1)} %collective-permute-done.2.refs_1_.refs_12_, bf16[672,1024]{1,0:T(8,128)(2,1)S(1)} %get-tuple-element.28.refs_2_.refs_4_, ...), custom_call_target="tpu_custom_call" | custom-call | flops 176160768 | bytes 3358720 | tf_op jit(solution)/shard_map/pallas_call | solution.py:29
  19.8 1.2 %collective-permute-start.4 = (bf16[448,128]{1,0:T(8,128)(2,1)S(1)}, bf16[448,128]{1,0:T(8,128)(2,1)S(1)}, u32[]{:S(2)}, u32[]{:S(2)}) collective-permute-start(bf16[448,128]{1,0:T(8,128)(2,1)S(1)} %get-tuple-element.31), channel_id=1, source_target_pairs={{0,2},{2,0},{1,3},{3,1},{4,6},{6,4},{5,7},{7,5},{8,10},{10,8},{9,1... | collective-permute-start | bytes 344072 | tf_op jit(solution)/shard_map/ppermute | solution.py:169
  20.9 0.4 %shard_map.104 = (f32[224,128]{1,0:T(8,128)S(1)}, bf16[224,128]{1,0:T(8,128)(2,1)S(1)}) custom-call(bf16[64,1024]{1,0:T(8,128)(2,1)S(1)} %collective-permute-done.refs_0_.refs_11_, bf16[64,1024]{1,0:T(8,128)(2,1)S(1)} %collective-permute-done.2.refs_1_.refs_12_, bf16[672,1024]{1,0:T(8,128)(2,1)S(1)} %get-tuple-element.28.refs_2_.refs_4_, ...), custom_call_target="tpu_custom_call" | custom-call | flops 176160768 | bytes 3186688 | tf_op jit(solution)/shard_map/pallas_call | solution.py:29
  21.4 1.0 %collective-permute-start.5 = (bf16[224,128]{1,0:T(8,128)(2,1)S(1)}, bf16[224,128]{1,0:T(8,128)(2,1)S(1)}, u32[]{:S(2)}, u32[]{:S(2)}) collective-permute-start(bf16[224,128]{1,0:T(8,128)(2,1)S(1)} %get-tuple-element.32), channel_id=1, source_target_pairs={{0,2},{2,0},{1,3},{3,1},{4,6},{6,4},{5,7},{7,5},{8,10},{10,8},{9,1... | collective-permute-start | bytes 172040 | tf_op jit(solution)/shard_map/ppermute | solution.py:169
  22.4 0.5 %shard_map.106 = (bf16[672,128]{1,0:T(8,128)(2,1)S(1)}, bf16[32,1024]{1,0:T(8,128)(2,1)S(1)}, bf16[32,1024]{1,0:T(8,128)(2,1)S(1)}) custom-call(f32[672,128]{1,0:T(8,128)S(1)} %get-tuple-element.33.refs_0_, bf16[672,128]{1,0:T(8,128)(2,1)S(1)} %collective-permute-done.7.refs_1_, bf16[672,1024]{1,0:T(8,128)(2,1)S(1)} %get-tuple-element.28.refs_2_.refs_4_, ...), custom_call_target="tpu_custom_call" | custom-call | flops 234881024 | bytes 3571712 | tf_op jit(solution)/shard_map/pallas_call | solution.py:29
  22.9 3.6 %collective-permute-done.5.refs_3_ = bf16[224,128]{1,0:T(8,128)(2,1)S(1)} collective-permute-done((bf16[224,128]{1,0:T(8,128)(2,1)S(1)}, bf16[224,128]{1,0:T(8,128)(2,1)S(1)}, u32[]{:S(2)}, u32[]{:S(2)}) %collective-permute-start.5) | collective-permute-done | bytes 57376 | tf_op jit(solution)/shard_map/ppermute | solution.py:169
  26.5 0.0 collective-permute-done.4.refs_2_
  26.5 0.6 %shard_map.107 = (bf16[672,256]{1,0:T(8,128)(2,1)S(1)}, bf16[256,1024]{1,0:T(8,128)(2,1)S(1)}, bf16[32,1024]{1,0:T(8,128)(2,1)S(1)}, bf16[32,1024]{1,0:T(8,128)(...) custom-call(f32[448,128]{1,0:T(8,128)S(1)} %get-tuple-element.29.refs_4_.refs_0_, ...), custom_call_target="tpu_custom_call" | custom-call | flops 234881024 | bytes 5226496 | tf_op jit(solution)/shard_map/pallas_call | solution.py:29
  27.1 0.1 collective-permute-start.12
  27.2 0.5 %collective-permute-start.13 = (bf16[672,256]{1,0:T(8,128)(2,1)S(1)}, bf16[672,256]{1,0:T(8,128)(2,1)S(1)}, u32[]{:S(2)}, u32[]{:S(2)}) collective-permute-start(bf16[672,256]{1,0:T(8,128)(2,1)S(1)} %get-tuple-element.43.refs_2_), channel_id=1, source_target_pairs={{0,1},{1,0},{2,3},{3,2},{4,5},{5,4},{6,7},{7,6},{8,9},{9,8},{10,11... | collective-permute-start | bytes 1032200 | tf_op jit(solution)/shard_map/ppermute | solution.py:169
  27.7 2.3 %collective-permute-start.8 = (bf16[32,1024]{1,0:T(8,128)(2,1)S(1)}, bf16[32,1024]{1,0:T(8,128)(2,1)S(1)}, u32[]{:S(2)}, u32[]{:S(2)}) collective-permute-start(bf16[32,1024]{1,0:T(8,128)(2,1)S(1)} %get-tuple-element.38), channel_id=1, source_target_pairs={{0,8},{1,10},{4,12},{5,14},{8,0},{9,2},{12,4},{13,6},{2,9},{3,11},... | collective-permute-start | bytes 196616 | tf_op jit(solution)/shard_map/ppermute | solution.py:166
  29.9 0.6 %collective-permute-start.9 = (bf16[32,1024]{1,0:T(8,128)(2,1)S(1)}, bf16[32,1024]{1,0:T(8,128)(2,1)S(1)}, u32[]{:S(2)}, u32[]{:S(2)}) collective-permute-start(bf16[32,1024]{1,0:T(8,128)(2,1)S(1)} %get-tuple-element.39), channel_id=1, source_target_pairs={{0,12},{1,14},{4,8},{5,10},{8,4},{9,6},{12,0},{13,2},{2,13},{3,15}... | collective-permute-start | bytes 196616 | tf_op jit(solution)/shard_map/ppermute | solution.py:166
  30.6 0.6 %collective-permute-start.10 = (bf16[32,1024]{1,0:T(8,128)(2,1)S(1)}, bf16[32,1024]{1,0:T(8,128)(2,1)S(1)}, u32[]{:S(2)}, u32[]{:S(2)}) collective-permute-start(bf16[32,1024]{1,0:T(8,128)(2,1)S(1)} %get-tuple-element.40), channel_id=1, source_target_pairs={{0,4},{1,6},{4,0},{5,2},{8,12},{9,14},{12,8},{13,10},{2,5},{3,7},{... | collective-permute-start | bytes 196616 | tf_op jit(solution)/shard_map/ppermute | solution.py:166
  31.2 0.0 collective-permute-done.13.refs_3_
  31.2 0.7 %collective-permute-start.11 = (bf16[32,1024]{1,0:T(8,128)(2,1)S(1)}, bf16[32,1024]{1,0:T(8,128)(2,1)S(1)}, u32[]{:S(2)}, u32[]{:S(2)}) collective-permute-start(bf16[32,1024]{1,0:T(8,128)(2,1)S(1)} %get-tuple-element.41), channel_id=1, source_target_pairs={{0,0},{1,2},{4,4},{5,6},{8,8},{9,10},{12,12},{13,14},{2,1},{3,3},{... | collective-permute-start | bytes 196616 | tf_op jit(solution)/shard_map/ppermute | solution.py:166
  31.8 0.0 collective-permute-done.12.refs_1_
  31.8 1.8 %shard_map.108 = (bf16[224,1024]{1,0:T(8,128)(2,1)}, bf16[224,1024]{1,0:T(8,128)(2,1)}, bf16[224,1024]{1,0:T(8,128)(2,1)}, f32[8,128]{1,0:T(8,128)S(1)}) custom-call(bf16[256,1024]{1,0:T(8,128)(2,1)S(1)} %get-tuple-element.42.refs_0_, bf16[256,1024]{1,0:T(8,128)(2,1)S(1)} %collective-permute-done.12.refs_1_, bf16[672,256]{1,0:T(8,128)(2,1)S(1)} %get-tuple-element.43.refs_2_, ...), custom_call_target="tpu_custom_call" | custom-call | flops 352321536 | bytes 3117056 | tf_op jit(solution)/shard_map/pallas_call | solution.py:29
  33.6 0.6 %collective-permute-done.8.refs_1_ = bf16[32,1024]{1,0:T(8,128)(2,1)S(1)} collective-permute-done((bf16[32,1024]{1,0:T(8,128)(2,1)S(1)}, bf16[32,1024]{1,0:T(8,128)(2,1)S(1)}, u32[]{:S(2)}, u32[]{:S(2)}) %collective-permute-start.8) | collective-permute-done | bytes 65568 | tf_op jit(solution)/shard_map/ppermute | solution.py:166
  34.3 2.6 %collective-permute-done.9.refs_2_ = bf16[32,1024]{1,0:T(8,128)(2,1)S(1)} collective-permute-done((bf16[32,1024]{1,0:T(8,128)(2,1)S(1)}, bf16[32,1024]{1,0:T(8,128)(2,1)S(1)}, u32[]{:S(2)}, u32[]{:S(2)}) %collective-permute-start.9) | collective-permute-done | bytes 65568 | tf_op jit(solution)/shard_map/ppermute | solution.py:166
  36.8 0.2 collective-permute-done.10.refs_3_
  37.0 1.0 %shard_map.109 = bf16[128,1024]{1,0:T(8,128)(2,1)} custom-call(bf16[32,128]{1,0:T(8,128)(2,1)S(1)} %get-tuple-element.26.refs_0_, bf16[32,1024]{1,0:T(8,128)(2,1)S(1)} %collective-permute-done.8.refs_1_, bf16[32,1024]{1,0:T(8,128)(2,1)S(1)} %collective-permute-done.9.refs_2_, bf16[32,1024]{1,0:T(8,128)(2,1)S(1)} %collective-permute-done.10.refs_3_, ...), custom_call_target="tpu_custom_call" | custom-call | bytes 532480 | tf_op jit(solution)/shard_map/pallas_call | solution.py:29
  (4 shorter events, 0.0 us)
Async XLA Ops:
  2.2 12.3 %collective-permute-start.3 = (bf16[672,1024]{1,0:T(8,128)(2,1)S(1)}, bf16[672,1024]{1,0:T(8,128)(2,1)S(1)}, u32[]{:S(2)}, u32[]{:S(2)}) collective-permute-start(bf16[672,1024]{1,0:T(8,128)(2,1)S(1)} %get-tuple-element.28.refs_2_.refs_4_), channel_id=1, source_target_pairs={{0,1},{1,0},{2,3},{3,2},{4,5},{5,4},{6,7},{7,6},{8,9},{9,8},{10,11... | collective-permute-start | bytes 4128776 | tf_op jit(solution)/shard_map/ppermute | solution.py:169
  2.7 10.3 %collective-permute-start.1 = (bf16[64,1024]{1,0:T(8,128)(2,1)S(1)}, bf16[64,1024]{1,0:T(8,128)(2,1)S(1)}, u32[]{:S(2)}, u32[]{:S(2)}) collective-permute-start(bf16[64,1024]{1,0:T(8,128)(2,1)S(1)} %get-tuple-element.27), channel_id=1, source_target_pairs={{0,8},{1,10},{4,12},{5,14},{8,0},{9,2},{12,4},{13,6},{2,9},{3,11},... | collective-permute-start | bytes 393224 | tf_op jit(solution)/shard_map/ppermute | solution.py:166
  6.4 8.1 %collective-permute-start.6 = (bf16[64,1024]{1,0:T(8,128)(2,1)S(1)}, bf16[64,1024]{1,0:T(8,128)(2,1)S(1)}, u32[]{:S(2)}, u32[]{:S(2)}) collective-permute-start(bf16[64,1024]{1,0:T(8,128)(2,1)S(1)} %get-tuple-element.27), channel_id=1, source_target_pairs={{0,4},{1,6},{4,0},{5,2},{8,12},{9,14},{12,8},{13,10},{2,5},{3,7},{... | collective-permute-start | bytes 393224 | tf_op jit(solution)/shard_map/ppermute | solution.py:166
  7.9 8.7 %collective-permute-start = (bf16[64,1024]{1,0:T(8,128)(2,1)S(1)}, bf16[64,1024]{1,0:T(8,128)(2,1)S(1)}, u32[]{:S(2)}, u32[]{:S(2)}) collective-permute-start(bf16[64,1024]{1,0:T(8,128)(2,1)S(1)} %get-tuple-element.27), channel_id=1, source_target_pairs={{0,0},{1,2},{4,4},{5,6},{8,8},{9,10},{12,12},{13,14},{2,1},{3,3},{... | collective-permute-start | bytes 393224 | tf_op jit(solution)/shard_map/ppermute | solution.py:166
  13.0 6.1 %collective-permute-start.2 = (bf16[64,1024]{1,0:T(8,128)(2,1)S(1)}, bf16[64,1024]{1,0:T(8,128)(2,1)S(1)}, u32[]{:S(2)}, u32[]{:S(2)}) collective-permute-start(bf16[64,1024]{1,0:T(8,128)(2,1)S(1)} %collective-permute-done.1.refs_1_.refs_10_), channel_id=1, source_target_pairs={{0,4},{4,0},{8,12},{12,8},{1,5},{5,1},{9,13},{13,9},{2,6},{6,2},{1... | collective-permute-start | bytes 393224 | tf_op jit(solution)/shard_map/ppermute | solution.py:180
  15.4 6.9 %collective-permute-start.7 = (bf16[672,128]{1,0:T(8,128)(2,1)S(1)}, bf16[672,128]{1,0:T(8,128)(2,1)S(1)}, u32[]{:S(2)}, u32[]{:S(2)}) collective-permute-start(bf16[672,128]{1,0:T(8,128)(2,1)S(1)} %get-tuple-element.34), channel_id=1, source_target_pairs={{0,2},{2,0},{1,3},{3,1},{4,6},{6,4},{5,7},{7,5},{8,10},{10,8},{9,1... | collective-permute-start | bytes 516104 | tf_op jit(solution)/shard_map/ppermute | solution.py:169
  19.8 6.8 %collective-permute-start.4 = (bf16[448,128]{1,0:T(8,128)(2,1)S(1)}, bf16[448,128]{1,0:T(8,128)(2,1)S(1)}, u32[]{:S(2)}, u32[]{:S(2)}) collective-permute-start(bf16[448,128]{1,0:T(8,128)(2,1)S(1)} %get-tuple-element.31), channel_id=1, source_target_pairs={{0,2},{2,0},{1,3},{3,1},{4,6},{6,4},{5,7},{7,5},{8,10},{10,8},{9,1... | collective-permute-start | bytes 344072 | tf_op jit(solution)/shard_map/ppermute | solution.py:169
  21.4 5.2 %collective-permute-start.5 = (bf16[224,128]{1,0:T(8,128)(2,1)S(1)}, bf16[224,128]{1,0:T(8,128)(2,1)S(1)}, u32[]{:S(2)}, u32[]{:S(2)}) collective-permute-start(bf16[224,128]{1,0:T(8,128)(2,1)S(1)} %get-tuple-element.32), channel_id=1, source_target_pairs={{0,2},{2,0},{1,3},{3,1},{4,6},{6,4},{5,7},{7,5},{8,10},{10,8},{9,1... | collective-permute-start | bytes 172040 | tf_op jit(solution)/shard_map/ppermute | solution.py:169
  27.1 4.7 %collective-permute-start.12 = (bf16[256,1024]{1,0:T(8,128)(2,1)S(1)}, bf16[256,1024]{1,0:T(8,128)(2,1)S(1)}, u32[]{:S(2)}, u32[]{:S(2)}) collective-permute-start(bf16[256,1024]{1,0:T(8,128)(2,1)S(1)} %get-tuple-element.42.refs_0_), channel_id=1, source_target_pairs={{0,1},{1,0},{2,3},{3,2},{4,5},{5,4},{6,7},{7,6},{8,9},{9,8},{10,11... | collective-permute-start | bytes 1572872 | tf_op jit(solution)/shard_map/ppermute | solution.py:169
  27.2 4.0 %collective-permute-start.13 = (bf16[672,256]{1,0:T(8,128)(2,1)S(1)}, bf16[672,256]{1,0:T(8,128)(2,1)S(1)}, u32[]{:S(2)}, u32[]{:S(2)}) collective-permute-start(bf16[672,256]{1,0:T(8,128)(2,1)S(1)} %get-tuple-element.43.refs_2_), channel_id=1, source_target_pairs={{0,1},{1,0},{2,3},{3,2},{4,5},{5,4},{6,7},{7,6},{8,9},{9,8},{10,11... | collective-permute-start | bytes 1032200 | tf_op jit(solution)/shard_map/ppermute | solution.py:169
  27.7 6.6 %collective-permute-start.8 = (bf16[32,1024]{1,0:T(8,128)(2,1)S(1)}, bf16[32,1024]{1,0:T(8,128)(2,1)S(1)}, u32[]{:S(2)}, u32[]{:S(2)}) collective-permute-start(bf16[32,1024]{1,0:T(8,128)(2,1)S(1)} %get-tuple-element.38), channel_id=1, source_target_pairs={{0,8},{1,10},{4,12},{5,14},{8,0},{9,2},{12,4},{13,6},{2,9},{3,11},... | collective-permute-start | bytes 196616 | tf_op jit(solution)/shard_map/ppermute | solution.py:166
  29.9 6.9 %collective-permute-start.9 = (bf16[32,1024]{1,0:T(8,128)(2,1)S(1)}, bf16[32,1024]{1,0:T(8,128)(2,1)S(1)}, u32[]{:S(2)}, u32[]{:S(2)}) collective-permute-start(bf16[32,1024]{1,0:T(8,128)(2,1)S(1)} %get-tuple-element.39), channel_id=1, source_target_pairs={{0,12},{1,14},{4,8},{5,10},{8,4},{9,6},{12,0},{13,2},{2,13},{3,15}... | collective-permute-start | bytes 196616 | tf_op jit(solution)/shard_map/ppermute | solution.py:166
  30.6 6.5 %collective-permute-start.10 = (bf16[32,1024]{1,0:T(8,128)(2,1)S(1)}, bf16[32,1024]{1,0:T(8,128)(2,1)S(1)}, u32[]{:S(2)}, u32[]{:S(2)}) collective-permute-start(bf16[32,1024]{1,0:T(8,128)(2,1)S(1)} %get-tuple-element.40), channel_id=1, source_target_pairs={{0,4},{1,6},{4,0},{5,2},{8,12},{9,14},{12,8},{13,10},{2,5},{3,7},{... | collective-permute-start | bytes 196616 | tf_op jit(solution)/shard_map/ppermute | solution.py:166
  31.2 5.9 %collective-permute-start.11 = (bf16[32,1024]{1,0:T(8,128)(2,1)S(1)}, bf16[32,1024]{1,0:T(8,128)(2,1)S(1)}, u32[]{:S(2)}, u32[]{:S(2)}) collective-permute-start(bf16[32,1024]{1,0:T(8,128)(2,1)S(1)} %get-tuple-element.41), channel_id=1, source_target_pairs={{0,0},{1,2},{4,4},{5,6},{8,8},{9,10},{12,12},{13,14},{2,1},{3,3},{... | collective-permute-start | bytes 196616 | tf_op jit(solution)/shard_map/ppermute | solution.py:166
